TPU v7x, 512 devices: a whole 4x4x16 slice. The times are simulated.
512 devices in a mesh: dp: 16 (over x, z_lo), tensor: 16 (over y, z_hi), draft: 2 (over core).
Axes of the slice: x: 4, y: 4, z: 16 (z_hi: 4, z_lo: 4; z = z_hi * 4 + z_lo), core: 2. Of those that a mesh axis runs over, the one named last changes fastest.
Arguments:
- rotated_queries: bfloat16 [16, 512, 8192], P('dp', None, ('tensor', 'draft')), may hold values from -6 to 6
- rotated_keys: bfloat16 [16, 512, 1024], P('dp'), may hold values from -6 to 6
- stored_values: bfloat16 [16, 512, 1024], P('dp'), may hold values from -6 to 6
- segment_labels: int32 [16, 512], P('dp'), may hold values from 0 to 7, never falling along the last dimension, each value on 1 to 128 neighbouring positions
- output_gradient: bfloat16 [16, 512, 8192], P('dp', 'draft', 'tensor'), may hold values from -6 to 6
- draft_loss_gradients: bfloat16 [16, 128, 8192], P('dp', 'draft', 'tensor'), may hold values from -6 to 6
- tapped_row_index: int32 [16, 128], P('dp'), may hold values from 0 to 511, as said below
- output_projector: bfloat16 [8192, 8192], P(('tensor', 'draft'), 'dp'), may hold values from -0.0625 to 0.0625
- lower_factor_weight: bfloat16 [8192, 64], P(('tensor', 'draft')), may hold values from -0.0625 to 0.0625
- upper_factor_weight: bfloat16 [64, 8192], P(None, ('tensor', 'draft')), may hold values from -0.0625 to 0.0625
Outputs:
- query_grad: bfloat16 [16, 512, 8192], P('dp', None, ('tensor', 'draft'))
- key_grad: bfloat16 [16, 512, 1024], P('dp', None, ('tensor', 'draft'))
- value_grad: bfloat16 [16, 512, 1024], P('dp', None, ('tensor', 'draft'))
- lower_factor_gradient: float32 [8192, 64], P(('tensor', 'draft'))
- upper_factor_gradient: float32 [64, 8192], P(None, ('tensor', 'draft'))
Inputs may be any that keep to these rules, and one draw needn't show every extreme that they name: `tapped_row_index`: within a sequence the 128 rows are distinct and increasing; rows 0 and 511 are always among them.
All inputs are finite; a program needn't handle non-finite values.
Results may differ from a plain program's by a relative error of at most 0.024.
Values may be sent and summed in bfloat16 or wider, within the bound.
No kernel may reach another device: no remote copies, remote signals or barrier semaphores. Data moves between devices by JAX's collectives and lax.ppermute only.
A program may use at most 64 MiB of HBM per device.

v0:
```python
import jax
import jax.numpy as jnp
from jax import lax
from jax.sharding import PartitionSpec as P

QUERY_HEAD_COUNT = 64
KVH = 8
HEAD_WIDTH = 128


adapter_scale = 2.0


def swapped(array, axis, bit):
    return lax.ppermute(array, axis, [(i, i ^ 1 << bit) for i in range(lax.axis_size(axis))])


def insert_taps(row_block, tap_block, tapped):
    summed = row_block[tapped].astype(jnp.float32) + tap_block.astype(jnp.float32)
    return row_block.at[tapped].set(summed.astype(jnp.bfloat16))


def project_columns(row_block, slab_piece):
    return lax.dot_general(
        row_block, slab_piece, (((1,), (1,)), ((), ())), preferred_element_type=jnp.float32
    )


def on_device(
    rotated_queries,
    rotated_keys,
    stored_values,
    segment_labels,
    output_gradient,
    draft_loss_gradients,
    tapped_row_index,
    output_projector,
    lower_factor_weight,
    upper_factor_weight,
):
    seq_len = rotated_queries.shape[1]
    head_size = HEAD_WIDTH
    heads_dev = rotated_queries.shape[2] // head_size
    group_size = QUERY_HEAD_COUNT // KVH
    kv_devices = group_size // heads_dev
    score_scale = head_size ** (-0.5)
    draft_count = lax.axis_size("draft")
    rank_index = lax.axis_index("tensor") * draft_count + lax.axis_index("draft")
    kv_head = rank_index * heads_dev // group_size
    tapped = tapped_row_index[0]
    column_span = upper_factor_weight.shape[1]
    own_rows, own_taps = (
        lax.all_gather(output_gradient[0], "draft", axis=0, tiled=True),
        lax.all_gather(draft_loss_gradients[0], "draft", axis=0, tiled=True),
    )
    row_block, tap_block = (
        lax.all_gather(own_rows, "tensor", axis=1, tiled=True),
        lax.all_gather(own_taps, "tensor", axis=1, tiled=True),
    )
    row_block = insert_taps(row_block, tap_block, tapped)
    frozen_gradient = project_columns(
        row_block, lax.all_gather(output_projector, "dp", axis=1, tiled=True)
    )
    local_columns = lax.dynamic_slice_in_dim(row_block, rank_index * column_span, column_span, 1)
    adapter_piece = lax.dot_general(
        local_columns,
        upper_factor_weight,
        (((1,), (1,)), ((), ())),
        preferred_element_type=jnp.float32,
    )
    query_heads = rotated_queries[0].reshape(seq_len, heads_dev, head_size)
    key_head = lax.dynamic_slice_in_dim(rotated_keys[0], kv_head * head_size, head_size, 1)
    value_head = lax.dynamic_slice_in_dim(stored_values[0], kv_head * head_size, head_size, 1)
    positions = jnp.arange(seq_len)
    segments_row = segment_labels[0]
    allowed = (positions[None, :] <= positions[:, None]) & (
        segments_row[:, None] == segments_row[None, :]
    )
    scores = (
        jnp.einsum("ihd,jd->hij", query_heads, key_head, preferred_element_type=jnp.float32)
        * score_scale
    )
    scores = jnp.where(allowed[None], scores, -jnp.inf)
    probs_full = jax.nn.softmax(scores, axis=-1)
    probs_half = probs_full.astype(jnp.bfloat16)
    attn_out = jnp.einsum(
        "hij,jd->ihd", probs_half, value_head, preferred_element_type=jnp.float32
    ).astype(jnp.bfloat16)
    output_flattened = attn_out.reshape(seq_len, heads_dev * head_size)
    inner_piece = jnp.dot(output_flattened, lower_factor_weight, preferred_element_type=jnp.float32)
    inner_total, adapter_total = lax.psum((inner_piece, adapter_piece), ("tensor", "draft"))
    adapter_gradient = adapter_total.astype(jnp.bfloat16)
    adapter_backward = lax.dot_general(
        adapter_gradient,
        lower_factor_weight,
        (((1,), (1,)), ((), ())),
        preferred_element_type=jnp.float32,
    )
    head_gradient = (frozen_gradient + adapter_scale * adapter_backward).astype(jnp.bfloat16)
    grad_heads = head_gradient.reshape(seq_len, heads_dev, head_size)
    value_part = jnp.einsum(
        "hij,ihd->jd", probs_half, grad_heads, preferred_element_type=jnp.float32
    )
    prob_grad = jnp.einsum(
        "ihd,jd->hij", grad_heads, value_head, preferred_element_type=jnp.float32
    )
    row_terms = jnp.einsum("ihd,ihd->hi", grad_heads, attn_out, preferred_element_type=jnp.float32)
    score_grad = (probs_full * (prob_grad - row_terms[:, :, None])).astype(jnp.bfloat16)
    query_grad = score_scale * jnp.einsum(
        "hij,jd->ihd", score_grad, key_head, preferred_element_type=jnp.float32
    )
    query_grad = query_grad.astype(jnp.bfloat16).reshape(1, seq_len, heads_dev * head_size)
    key_part = score_scale * jnp.einsum(
        "hij,ihd->jd", score_grad, query_heads, preferred_element_type=jnp.float32
    )
    combined = jnp.stack([key_part, value_part], axis=1).reshape(
        seq_len, 2, kv_devices, head_size // kv_devices
    )
    for bit_step in reversed(range(kv_devices.bit_length() - 1)):
        half_count = combined.shape[2] // 2
        low_half = combined[:, :, :half_count]
        high_half = combined[:, :, half_count:]
        upper_mine = rank_index >> bit_step & 1 == 1
        retained = jnp.where(upper_mine, high_half, low_half)
        outgoing = jnp.where(upper_mine, low_half, high_half)
        combined = retained + swapped(outgoing, ("tensor", "draft"), bit_step)
    key_grad = combined[:, 0, 0, :].astype(jnp.bfloat16)[None]
    value_grad = combined[:, 1, 0, :].astype(jnp.bfloat16)[None]
    adapter_inner = inner_total.astype(jnp.bfloat16)
    lower_factor_piece = adapter_scale * lax.dot_general(
        output_flattened,
        adapter_gradient,
        (((0,), (0,)), ((), ())),
        preferred_element_type=jnp.float32,
    )
    upper_factor_piece = adapter_scale * lax.dot_general(
        adapter_inner, local_columns, (((0,), (0,)), ((), ())), preferred_element_type=jnp.float32
    )
    down_sum, up_sum = lax.psum((lower_factor_piece, upper_factor_piece), "dp")
    group_count = lax.axis_size("dp")
    return (query_grad, key_grad, value_grad, down_sum / group_count, up_sum / group_count)


def solution(mesh):
    in_specs = (
        P("dp", None, ("tensor", "draft")),
        P("dp", None, None),
        P("dp", None, None),
        P("dp", None),
        P("dp", "draft", "tensor"),
        P("dp", "draft", "tensor"),
        P("dp", None),
        P(("tensor", "draft"), "dp"),
        P(("tensor", "draft"), None),
        P(None, ("tensor", "draft")),
    )
    out_specs = (
        P("dp", None, ("tensor", "draft")),
        P("dp", None, ("tensor", "draft")),
        P("dp", None, ("tensor", "draft")),
        P(("tensor", "draft"), None),
        P(None, ("tensor", "draft")),
    )
    return jax.shard_map(
        on_device, mesh=mesh, in_specs=in_specs, out_specs=out_specs, check_vma=False
    )
```

profile of v0, /device:TPU:1, one launch (start us, length us, event | category | flops | bytes accessed | tf_op | source)
XLA Modules:
  0.0 734.3 jit_solution(7567148464305826308)
XLA Ops:
  7.2 0.0 copy-start
  7.2 0.0 copy-start.2
  7.2 0.0 copy-start.5
  7.2 0.0 all-gather.12.cloned.1.call-start
  7.2 10.2 %all-gather.2 = bf16[1,128,512]{2,1,0:T(8,128)(2,1)} all-gather(bf16[1,64,512]{2,1,0:T(8,128)(2,1)} %param.15), channel_id=4, replica_groups=mesh['dp'=16,'tensor'=16,'draft'=2] {'draft'}, dimensions={1}, use_global_device_ids=true | all-gather | bytes 196608 | tf_op jit(solution)/shard_map/all_gather | solution.py:54
  17.5 0.0 all-gather.12.cloned.1.call-update
  17.5 0.0 all-gather.10.cloned.1.call-start
  17.5 3.9 all-gather
  21.4 0.0 all-gather.10.cloned.1.call-update
  21.4 0.0 all-gather.8.cloned.1.call-start
  21.5 0.7 all-gather.8.cloned.1.call-update
  22.1 0.0 all-reduce.5.cloned.1.call-start
  22.2 0.0 copy-done.2
  22.2 0.1 copy.54
  22.4 0.0 copy-done.5
  22.4 0.2 fusion.15
  22.6 0.0 copy-done
  22.6 2.2 fusion.55
  24.8 0.0 copy-start.3
  24.8 0.0 copy-start.6
  24.8 1.9 fusion.17
  26.7 1.2 convolution_convert_fusion
  28.0 0.0 copy-done.3
  28.0 0.3 fusion.59
  28.2 0.0 copy-done.6
  28.3 87.4 %all-gather.12.cloned.1.call-done = bf16[1,128,8192]{2,1,0:T(8,128)(2,1)} async-done(((bf16[1,128,512]{2,1,0:T(8,128)(2,1)}), bf16[1,128,8192]{2,1,0:T(8,128)(2,1)}) %all-gather.12.cloned.1.call-update) | async-done | bytes 2097168 | tf_op jit(solution)/shard_map/all_gather | solution.py:58
  115.7 229.3 %all-gather.10.cloned.1.call-done = bf16[1,512,8192]{2,1,0:T(8,128)(2,1)} async-done(((bf16[1,512,512]{2,1,0:T(8,128)(2,1)}), bf16[1,512,8192]{2,1,0:T(8,128)(2,1)}) %all-gather.10.cloned.1.call-update) | async-done | bytes 8388624 | tf_op jit(solution)/shard_map/all_gather | solution.py:57
  344.9 0.0 copy-start.4
  344.9 17.7 %scatter_custom_fusion = bf16[512,8192]{1,0:T(8,128)(2,1)} fusion(bf16[512,8192]{1,0:T(8,128)(2,1)} %bitcast.104, s32[128]{0:T(128)S(1)} %fusion.51, bf16[1,128,8192]{2,1,0:T(8,128)(2,1)} %all-gather.12.cloned.1.call-done, s32[1024]{0:T(1024)S(1)} %pad_clamp_fusion), kind=kCustom, calls=%fused_computation.5 | custom fusion | flops 4194304 | bytes 18878464 | tf_op jit(solution)/shard_map/scatter | solution.py:20
  362.7 0.0 copy-done.4
  362.7 1.1 fusion.21
  363.8 166.5 %all-reduce.6 = (bf16[512,64]{0,1:T(8,128)(2,1)S(1)}, bf16[512,64]{1,0:T(8,128)(2,1)S(1)}) all-reduce(f32[512,64]{0,1:T(8,128)S(1)} %fusion.21, f32[512,64]{1,0:T(8,128)S(1)} %fusion.59), channel_id=1, replica_groups=mesh['dp'=16,'tensor'=16,'draft'=2] {'tensor','draft'}, use_global_device_ids=true, to_apply=%region_3.4 | all-reduce | flops 65536 | bytes 393216 | tf_op jit(solution)/shard_map/psum | solution.py:91
  530.3 0.8 convolution_multiply_fusion.3
  531.1 0.0 all-gather.8.cloned.1.call-done
  531.1 6.9 fusion.58
  538.1 0.3 fusion.18
  538.4 0.0 copy-start.1
  538.4 0.5 convolution_bitcast_fusion
  538.9 1.1 copy-done.1
  540.0 1.3 fusion.6
  541.3 0.5 fusion.11
  541.8 1.9 collective-permute-start
  543.8 1.8 convolution_multiply_fusion.2
  545.6 0.0 all-reduce.5.cloned.1.call-update
  545.6 0.3 fusion.10
  545.9 0.8 copy.35
  546.8 163.9 %all-reduce.5.cloned.1.call-done = (f32[256,64]{0,1:T(8,128)}, f32[64,256]{1,0:T(8,128)}) async-done(((f32[256,64]{0,1:T(8,128)}, f32[64,256]{1,0:T(8,128)}), (f32[256,64]{0,1:T(8,128)}, f32[64,256]{1,0:T(8,128)})) %all-reduce.5.cloned.1.call-update) | async-done | bytes 131088 | tf_op jit(solution)/shard_map/psum | solution.py:139
  710.7 1.5 broadcast_multiply_fusion.1
  712.2 0.0 collective-permute-done
  712.2 0.1 select_add_fusion
  712.3 13.3 %collective-permute-start.1 = (f32[512,2,1,32]{0,3,2,1:T(8,128)S(1)}, f32[512,2,1,32]{0,3,2,1:T(8,128)S(1)}, u32[]{:S(2)}, u32[]{:S(2)}) collective-permute-start(f32[512,2,1,32]{0,3,2,1:T(8,128)S(1)} %slice_select_fusion), channel_id=1, source_target_pairs={{0,1},{1,0},{2,3},{3,2},{4,5},{5,4},{6,7},{7,6},{8,9},{9,8},{10,11... | collective-permute-start | bytes 393224 | tf_op jit(solution)/shard_map/ppermute | solution.py:15
  725.7 1.5 broadcast_multiply_fusion
  727.1 0.0 collective-permute-done.1
  727.2 0.6 slice_bitcast_fusion
  (5 shorter events, 0.1 us)
Async XLA Ops:
  7.2 15.4 %copy-start = (bf16[1,512,1024]{2,1,0:T(8,128)(2,1)S(1)}, bf16[1,512,1024]{2,1,0:T(8,128)(2,1)}, u32[]{:S(2)}) copy-start(bf16[1,512,1024]{2,1,0:T(8,128)(2,1)} %param.11) | copy-start | bytes 3145732
  7.2 15.0 %copy-start.2 = (bf16[1,512,256]{2,1,0:T(8,128)(2,1)S(1)}, bf16[1,512,256]{2,1,0:T(8,128)(2,1)}, u32[]{:S(2)}) copy-start(bf16[1,512,256]{2,1,0:T(8,128)(2,1)} %param.10) | copy-start | bytes 786436
  7.2 15.2 %copy-start.5 = (s32[1,512]{1,0:T(1,128)S(1)}, s32[1,512]{1,0:T(1,128)}, u32[]{:S(2)}) copy-start(s32[1,512]{1,0:T(1,128)} %param.13) | copy-start | bytes 6148
  7.2 108.5 %all-gather.12.cloned.1.call-start = ((), (), s32[]{:S(2)}) async-start(), calls=%async_computation.2 | async-start | bytes 2228224 | tf_op jit(solution)/shard_map/all_gather | solution.py:58
  17.5 327.4 %all-gather.10.cloned.1.call-start = ((), (), s32[]{:S(2)}) async-start(), calls=%async_computation.1 | async-start | bytes 8912896 | tf_op jit(solution)/shard_map/all_gather | solution.py:57
  21.4 509.7 %all-gather.8.cloned.1.call-start = ((), (), s32[]{:S(2)}) async-start(), calls=%async_computation | async-start | bytes 4456448 | tf_op jit(solution)/shard_map/all_gather | solution.py:62
  22.1 688.6 %all-reduce.5.cloned.1.call-start = ((), (), s32[]{:S(2)}) async-start(), calls=%async_computation.3 | async-start | bytes 262144 | tf_op jit(solution)/shard_map/psum | solution.py:139
  24.8 3.1 copy-start.3
  24.8 3.4 copy-start.6
  344.9 17.7 %copy-start.4 = (bf16[64,256]{1,0:T(8,128)(2,1)S(1)}, bf16[64,256]{1,0:T(8,128)(2,1)}, u32[]{:S(2)}) copy-start(bf16[64,256]{1,0:T(8,128)(2,1)} %param.19) | copy-start | bytes 98308
  538.4 1.6 copy-start.1
  541.8 170.4 %collective-permute-start = (f32[512,2,2,32]{0,3,2,1:T(8,128)S(1)}, f32[512,2,2,32]{0,3,2,1:T(8,128)S(1)}, u32[]{:S(2)}, u32[]{:S(2)}) collective-permute-start(f32[512,2,2,32]{0,3,2,1:T(8,128)S(1)} %broadcast_select_fusion), channel_id=1, source_target_pairs={{0,2},{1,3},{2,0},{3,1},{4,6},{5,7},{6,4},{7,5},{8,10},{9,11},{10,... | collective-permute-start | bytes 786440 | tf_op jit(solution)/shard_map/ppermute | solution.py:15
  712.3 14.8 %collective-permute-start.1 = (f32[512,2,1,32]{0,3,2,1:T(8,128)S(1)}, f32[512,2,1,32]{0,3,2,1:T(8,128)S(1)}, u32[]{:S(2)}, u32[]{:S(2)}) collective-permute-start(f32[512,2,1,32]{0,3,2,1:T(8,128)S(1)} %slice_select_fusion), channel_id=1, source_target_pairs={{0,1},{1,0},{2,3},{3,2},{4,5},{5,4},{6,7},{7,6},{8,9},{9,8},{10,11... | collective-permute-start | bytes 393224 | tf_op jit(solution)/shard_map/ppermute | solution.py:15
Sparse Core Ops, SparseCore 0:
  17.6 98.0 all-gather.11
  118.6 226.2 all-gather.9
  347.0 105.2 all-gather.7
  545.7 164.9 all-reduce.4
where the time goes:
time: 735 us; the launch traced here: 734 us
  waiting for transfers between devices  481 us (65%)
  blocking collectives  181 us (25%)
  other arithmetic  22.9 us (3%)
  matrix products  17.3 us (2%)
  starting transfers between devices  15.4 us (2%)
  between operations  14 us (2%)
    all_gather x1, waiting for transfers between devices, on_device(): lax.all_gather(own_rows, 'tensor', axis=1, tiled=True)  229 us
    psum x1, blocking collectives, on_device(): lax.psum((inner_piece, adapter_piece), ('tensor', 'draft'))  166 us
    psum x1, waiting for transfers between devices, on_device(): down_sum, up_sum = lax.psum((lower_factor_piece, upper_factor_piece), 'dp')  164 us
    all_gather x1, waiting for transfers between devices, on_device(): lax.all_gather(own_taps, 'tensor', axis=1, tiled=True)  87.4 us
    scatter x1, other arithmetic, insert_taps(): return row_block.at[tapped].set(summed.astype(jnp.bfloat16))  17.7 us
    ppermute x2, starting transfers between devices, swapped(): lax.ppermute(array, axis, [(i, i ^ 1 << bit) for i in range(lax.axis_size...  15.3 us
  transfers between devices with their start and end apart: 6, of which 3 were waited for; matrix products, arithmetic and copies ran while one was open for 4% of the time, Pallas kernels for 0%

commit v1 on v0

v1 whole, which is shorter than its diff:
```python
import jax
import jax.numpy as jnp
from jax import lax
from jax.experimental import pallas as pl
from jax.experimental.pallas import tpu as pltpu
from jax.sharding import PartitionSpec as P

QUERY_HEAD_COUNT = 64
KVH = 8
HEAD_WIDTH = 128
SIDE = 4

adapter_scale = 2.0

F32, BF16 = jnp.float32, jnp.bfloat16
NT = (((1,), (1,)), ((), ()))
TN = (((0,), (0,)), ((), ()))


def high_shift(array, axis, k):
    pairs = [(i * SIDE + j, (i + k) % SIDE * SIDE + j) for i in range(SIDE) for j in range(SIDE)]
    return lax.ppermute(array, axis, pairs)


def low_shift(array, axis, k):
    pairs = [(i * SIDE + j, i * SIDE + (j + k) % SIDE) for i in range(SIDE) for j in range(SIDE)]
    return lax.ppermute(array, axis, pairs)


def swapped(array, axis, mask):
    return lax.ppermute(array, axis, [(i, i ^ mask) for i in range(lax.axis_size(axis))])


def halves(array, upper):
    n = array.shape[0] // 2
    low, high = array[:n], array[n:]
    return jnp.where(upper, high, low), jnp.where(upper, low, high)


def scatter_step(array, axis, mask, upper):
    keep, give = halves(array, upper)
    return keep + swapped(give, axis, mask)


def gather_step(array, axis, mask, upper):
    other = swapped(array, axis, mask)
    return jnp.concatenate([jnp.where(upper, other, array), jnp.where(upper, array, other)], axis=0)


def frozen_kernel(order_ref, *refs):
    pieces, slab, mine, other = refs[:16], refs[16], refs[17], refs[18]
    n = mine.shape[1]
    total = None
    for i, piece in enumerate(pieces):
        term = lax.dot_general(piece[...], slab[order_ref[i]], NT, preferred_element_type=F32)
        total = term if total is None else total + term
    mine[...] = total[:, :n]
    other[...] = total[:, n:]


def frozen_product(order, pieces, slab):
    rows, cols = pieces[0].shape[0], slab.shape[1] // 2
    return pl.pallas_call(
        frozen_kernel,
        out_shape=(jax.ShapeDtypeStruct((rows, cols), F32),) * 2,
        in_specs=[pl.BlockSpec(memory_space=pltpu.SMEM)]
        + [pl.BlockSpec(memory_space=pltpu.VMEM)] * 17,
        out_specs=(pl.BlockSpec(memory_space=pltpu.VMEM),) * 2,
        compiler_params=pltpu.CompilerParams(vmem_limit_bytes=40 * 1024 * 1024),
        name="frozen",
    )(order, *pieces, slab)


def on_device(
    rotated_queries,
    rotated_keys,
    stored_values,
    segment_labels,
    output_gradient,
    draft_loss_gradients,
    tapped_row_index,
    output_projector,
    lower_factor_weight,
    upper_factor_weight,
):
    seq_len = rotated_queries.shape[1]
    head_size = HEAD_WIDTH
    heads_dev = rotated_queries.shape[2] // head_size
    group_size = QUERY_HEAD_COUNT // KVH
    score_scale = head_size ** (-0.5)
    core = lax.axis_index("draft")
    tensor = lax.axis_index("tensor")
    dp = lax.axis_index("dp")
    upper_core = core == 1
    rank_index = tensor * 2 + core
    kv_head = rank_index * heads_dev // group_size
    tapped = tapped_row_index[0]
    width = output_projector.shape[1] // 2
    rank = lower_factor_weight.shape[1]

    local = jnp.concatenate([output_gradient[0], draft_loss_gradients[0], output_projector], axis=0)
    low, high = local[:, :width], local[:, width:]
    own = jnp.where(upper_core, high, low)
    came = swapped(jnp.where(upper_core, low, high), "draft", 1)
    nr, nt = output_gradient.shape[1], draft_loss_gradients.shape[1]
    first, second = jnp.where(upper_core, came, own), jnp.where(upper_core, own, came)
    slab_own = jnp.concatenate([own[nr + nt :], came[nr + nt :]], axis=0)
    slab = lax.all_gather(slab_own, "dp", axis=0)
    rows = jnp.concatenate([first[:nr], second[:nr]], axis=0)
    taps = jnp.concatenate([first[nr : nr + nt], second[nr : nr + nt]], axis=0)
    hit = (jnp.arange(seq_len)[:, None] == tapped[None, :]).astype(BF16)
    spread = jnp.dot(hit, taps, preferred_element_type=F32)
    residual = (rows.astype(F32) + spread).astype(BF16)

    z1, z3, z2 = (low_shift(residual, "tensor", k) for k in (1, 3, 2))
    pieces = {(0, 0): residual, (0, 1): z1, (0, 3): z3, (0, 2): z2}
    near = jnp.concatenate([z1, z3], axis=0)
    for k in (1, 3, 2):
        pieces[k, 0] = high_shift(residual, "tensor", k)
    for k in (1, 3, 2):
        both = high_shift(near, "tensor", k)
        pieces[k, 1], pieces[k, 3] = both[:seq_len], both[seq_len:]
    for k in (1, 3, 2):
        pieces[k, 2] = high_shift(z2, "tensor", k)
    keys = sorted(pieces)
    order = jnp.stack(
        [(tensor // SIDE - a) % SIDE * SIDE + (tensor % SIDE - b) % SIDE for a, b in keys]
    ).astype(jnp.int32)

    query_heads = rotated_queries[0].reshape(seq_len, heads_dev, head_size)
    key_head = lax.dynamic_slice_in_dim(rotated_keys[0], kv_head * head_size, head_size, 1)
    value_head = lax.dynamic_slice_in_dim(stored_values[0], kv_head * head_size, head_size, 1)
    positions = jnp.arange(seq_len)
    segments_row = segment_labels[0]
    allowed = (positions[None, :] <= positions[:, None]) & (
        segments_row[:, None] == segments_row[None, :]
    )
    scores = (
        jnp.einsum("ihd,jd->hij", query_heads, key_head, preferred_element_type=F32) * score_scale
    )
    scores = jnp.where(allowed[None], scores, -jnp.inf)
    probs_full = jax.nn.softmax(scores, axis=-1)
    probs_half = probs_full.astype(BF16)
    attn_out = jnp.einsum("hij,jd->ihd", probs_half, value_head, preferred_element_type=F32).astype(
        BF16
    )
    output_flattened = attn_out.reshape(seq_len, heads_dev * head_size)

    inner_piece = jnp.dot(output_flattened, lower_factor_weight, preferred_element_type=F32)
    adapter_piece = lax.dot_general(residual, upper_factor_weight, NT, preferred_element_type=F32)
    sums = jnp.concatenate([inner_piece, adapter_piece], axis=1)
    sums = scatter_step(sums, "draft", 1, upper_core)
    sums = scatter_step(sums, "tensor", 4, tensor & 4 != 0)
    sums = scatter_step(sums, "tensor", 8, tensor & 8 != 0)
    sums = sums + swapped(sums, "tensor", 1)
    sums = sums + swapped(sums, "tensor", 2)
    sums = sums.astype(BF16)
    sums = gather_step(sums, "tensor", 8, tensor & 8 != 0)
    sums = gather_step(sums, "tensor", 4, tensor & 4 != 0)
    sums = gather_step(sums, "draft", 1, upper_core)
    adapter_inner, adapter_gradient = sums[:, :rank], sums[:, rank:]

    lower_piece = lax.dot_general(adapter_gradient, output_flattened, TN, preferred_element_type=F32)
    upper_piece = lax.dot_general(adapter_inner, residual, TN, preferred_element_type=F32)
    factor = jnp.concatenate([lower_piece, upper_piece], axis=0)
    factor = scatter_step(factor, "dp", 4, dp & 4 != 0)
    factor = scatter_step(factor, "dp", 8, dp & 8 != 0)
    factor = factor + swapped(factor, "dp", 1)
    factor = factor + swapped(factor, "dp", 2)
    factor = factor * (adapter_scale / lax.axis_size("dp"))
    factor = gather_step(factor, "dp", 8, dp & 8 != 0)
    factor = gather_step(factor, "dp", 4, dp & 4 != 0)
    lower_gradient, upper_gradient = factor[:rank].T, factor[rank:]

    part_mine, part_other = frozen_product(order, [pieces[k] for k in keys], slab)
    frozen_gradient = part_mine + swapped(part_other, "draft", 1)
    adapter_backward = lax.dot_general(
        adapter_gradient, lower_factor_weight, NT, preferred_element_type=F32
    )
    head_gradient = (frozen_gradient + adapter_scale * adapter_backward).astype(BF16)

    grad_heads = head_gradient.reshape(seq_len, heads_dev, head_size)
    value_part = jnp.einsum("hij,ihd->jd", probs_half, grad_heads, preferred_element_type=F32)
    prob_grad = jnp.einsum("ihd,jd->hij", grad_heads, value_head, preferred_element_type=F32)
    row_terms = jnp.einsum("ihd,ihd->hi", grad_heads, attn_out, preferred_element_type=F32)
    score_grad = (probs_full * (prob_grad - row_terms[:, :, None])).astype(BF16)
    query_grad = score_scale * jnp.einsum(
        "hij,jd->ihd", score_grad, key_head, preferred_element_type=F32
    )
    query_grad = query_grad.astype(BF16).reshape(1, seq_len, heads_dev * head_size)
    key_part = score_scale * jnp.einsum(
        "hij,ihd->jd", score_grad, query_heads, preferred_element_type=F32
    )
    combined = jnp.stack([key_part, value_part], axis=1).reshape(
        seq_len, 2, 2, 2, head_size // 4
    )
    keep = jnp.where(upper_core, combined[:, :, :, 1], combined[:, :, :, 0])
    give = jnp.where(upper_core, combined[:, :, :, 0], combined[:, :, :, 1])
    combined = keep + swapped(give, "draft", 1)
    upper_chip = tensor & 1 == 1
    keep = jnp.where(upper_chip, combined[:, :, 1], combined[:, :, 0])
    give = jnp.where(upper_chip, combined[:, :, 0], combined[:, :, 1])
    combined = keep + swapped(give, "tensor", 1)
    key_grad = combined[:, 0].astype(BF16)[None]
    value_grad = combined[:, 1].astype(BF16)[None]
    return (query_grad, key_grad, value_grad, lower_gradient, upper_gradient)


def solution(mesh):
    in_specs = (
        P("dp", None, ("tensor", "draft")),
        P("dp", None, None),
        P("dp", None, None),
        P("dp", None),
        P("dp", "draft", "tensor"),
        P("dp", "draft", "tensor"),
        P("dp", None),
        P(("tensor", "draft"), "dp"),
        P(("tensor", "draft"), None),
        P(None, ("tensor", "draft")),
    )
    out_specs = (
        P("dp", None, ("tensor", "draft")),
        P("dp", None, ("tensor", "draft")),
        P("dp", None, ("tensor", "draft")),
        P(("tensor", "draft"), None),
        P(None, ("tensor", "draft")),
    )
    return jax.shard_map(
        on_device, mesh=mesh, in_specs=in_specs, out_specs=out_specs, check_vma=False
    )
```

time: 735 us -> 274 us (0.37)
  waiting for transfers between devices: 481 us -> 86.4 us
  blocking collectives: 181 us -> 0 us
  starting transfers between devices: 15.4 us -> 130 us
  local copies, waits for them, and re-layouts: 2.75 us -> 20.2 us
  other arithmetic: 22.9 us -> 9.51 us
  matrix products: 17.3 us -> 8.36 us
    all_gather x3 -> x1, waiting for transfers between devices: 317 us -> 0.01 us  [on_device(): slab = lax.all_gather(slab_own, 'dp', axis=0)]
    psum x1 -> x0, blocking collectives: 166 us -> none  [on_device(): lax.psum((inner_piece, adapter_piece), ('tensor', 'draft'))]
    psum x1 -> x0, waiting for transfers between devices: 164 us -> none  [on_device(): down_sum, up_sum = lax.psum((lower_factor_piece, upper_factor_piece), 'dp')]
    ppermute x2 -> x30, starting transfers between devices: 15.3 us -> 130 us  [the longest x18 82.1 us: swapped(): lax.ppermute(array, axis, [(i, i ^ mask) for i in range(lax.axis_size(axi...]
    ppermute x2 -> x30, waiting for transfers between devices: 0.01 us -> 86.4 us  [the longest x18 46.7 us: swapped(): lax.ppermute(array, axis, [(i, i ^ mask) for i in range(lax.axis_size(axi...]
    scatter x1 -> x0, other arithmetic: 17.7 us -> none  [insert_taps(): return row_block.at[tapped].set(summed.astype(jnp.bfloat16))]
    unnamed x15 -> x63, local copies, waits for them, and re-layouts: 1.98 us -> 16.2 us
    all_gather x2 -> x0, blocking collectives: 14.1 us -> none  [the longest x1 10.2 us: on_device(): lax.all_gather(draft_loss_gradients[0], 'draft', axis=0, tiled=True)]
  transfers between devices with their start and end apart: 6 -> 31, of which waited for: 3 -> 12; matrix products, arithmetic and copies ran while one was open for 4% -> 8% of each run, Pallas kernels for 0% -> 1%
where the time goes in v1:
time: 274 us; the launch traced here: 272 us
  starting transfers between devices  130 us (47%)
  waiting for transfers between devices  86.4 us (32%)
  local copies, waits for them, and re-layouts  20.2 us (7%)
  between operations  15.1 us (6%)
  other arithmetic  9.51 us (3%)
  matrix products  8.36 us (3%)
  Pallas kernels  2.89 us (1%)
    ppermute x18, starting transfers between devices, swapped(): lax.ppermute(array, axis, [(i, i ^ mask) for i in range(lax.axis_size(axi...  82.1 us
    ppermute x18, waiting for transfers between devices, swapped(): lax.ppermute(array, axis, [(i, i ^ mask) for i in range(lax.axis_size(axi...  46.7 us
    ppermute x3, waiting for transfers between devices, low_shift(): return lax.ppermute(array, axis, pairs)  37.5 us
    ppermute x9, starting transfers between devices, high_shift(): return lax.ppermute(array, axis, pairs)  33.7 us
    unnamed x63, local copies, waits for them, and re-layouts  16.2 us
    ppermute x3, starting transfers between devices, low_shift(): return lax.ppermute(array, axis, pairs)  14.1 us
  transfers between devices with their start and end apart: 31, of which 12 were waited for; matrix products, arithmetic and copies ran while one was open for 8% of the time, Pallas kernels for 1%

profile of v1, /device:TPU:1, one launch (start us, length us, event | category | flops | bytes accessed | tf_op | source)
XLA Modules:
  0.0 272.4 jit_solution(5546139072597008160)
XLA Ops:
  7.2 1.2 pad_maximum_fusion
  8.5 8.9 %collective-permute-start = (bf16[576,256]{1,0:T(8,128)(2,1)S(1)}, bf16[576,256]{1,0:T(8,128)(2,1)S(1)}, u32[]{:S(2)}, u32[]{:S(2)}) collective-permute-start(bf16[576,256]{1,0:T(8,128)(2,1)S(1)} %broadcast_select_fusion.3), channel_id=1, source_target_pairs={{0,1},{1,0},{2,3},{3,2},{4,5},{5,4},{6,7},{7,6},{8,9},{9,8},{10,11... | collective-permute-start | bytes 884744 | tf_op jit(solution)/shard_map/ppermute | solution.py:31
  17.4 1.2 collective-permute-done
  19.9 2.3 fusion.60
  22.2 1.9 fusion.11
  24.1 1.5 convolution_convert_fusion
  26.3 2.3 collective-permute-start.14
  28.6 1.0 collective-permute-done.14
  29.6 1.9 collective-permute-start.15
  31.5 3.1 %collective-permute-done.15 = f32[128,128]{0,1:T(8,128)S(1)} collective-permute-done((f32[128,128]{0,1:T(8,128)S(1)}, f32[128,128]{0,1:T(8,128)S(1)}, u32[]{:S(2)}, u32[]{:S(2)}) %collective-permute-start.15) | collective-permute-done | bytes 65568 | tf_op jit(solution)/shard_map/ppermute | solution.py:31
  34.7 1.9 collective-permute-start.16
  36.7 5.0 %collective-permute-done.16 = f32[64,128]{0,1:T(8,128)S(1)} collective-permute-done((f32[64,128]{0,1:T(8,128)S(1)}, f32[64,128]{0,1:T(8,128)S(1)}, u32[]{:S(2)}, u32[]{:S(2)}) %collective-permute-start.16) | collective-permute-done | bytes 32800 | tf_op jit(solution)/shard_map/ppermute | solution.py:31
  41.7 3.0 %collective-permute-start.17 = (f32[64,128]{0,1:T(8,128)S(1)}, f32[64,128]{0,1:T(8,128)S(1)}, u32[]{:S(2)}, u32[]{:S(2)}) collective-permute-start(f32[64,128]{0,1:T(8,128)S(1)} %select_add_fusion.2), channel_id=1, source_target_pairs={{0,2},{2,0},{4,6},{6,4},{8,10},{10,8},{12,14},{14,12},{16,18},{18,... | collective-permute-start | bytes 98312 | tf_op jit(solution)/shard_map/ppermute | solution.py:31
  44.8 7.3 %collective-permute-done.17 = f32[64,128]{0,1:T(8,128)S(1)} collective-permute-done((f32[64,128]{0,1:T(8,128)S(1)}, f32[64,128]{0,1:T(8,128)S(1)}, u32[]{:S(2)}, u32[]{:S(2)}) %collective-permute-start.17) | collective-permute-done | bytes 32800 | tf_op jit(solution)/shard_map/ppermute | solution.py:31
  52.1 9.2 %collective-permute-start.18 = (f32[64,128]{0,1:T(8,128)S(1)}, f32[64,128]{0,1:T(8,128)S(1)}, u32[]{:S(2)}, u32[]{:S(2)}) collective-permute-start(f32[64,128]{0,1:T(8,128)S(1)} %add.204), channel_id=1, source_target_pairs={{0,4},{2,6},{4,0},{6,2},{8,12},{10,14},{12,8},{14,10},{16,20},{18,... | collective-permute-start | bytes 98312 | tf_op jit(solution)/shard_map/ppermute | solution.py:31
  61.4 5.7 %collective-permute-done.18 = f32[64,128]{0,1:T(8,128)S(1)} collective-permute-done((f32[64,128]{0,1:T(8,128)S(1)}, f32[64,128]{0,1:T(8,128)S(1)}, u32[]{:S(2)}, u32[]{:S(2)}) %collective-permute-start.18) | collective-permute-done | bytes 32800 | tf_op jit(solution)/shard_map/ppermute | solution.py:31
  67.1 2.2 collective-permute-start.19
  69.3 4.3 %collective-permute-done.19 = bf16[64,128]{0,1:T(8,128)(2,1)S(1)} collective-permute-done((bf16[64,128]{0,1:T(8,128)(2,1)S(1)}, bf16[64,128]{0,1:T(8,128)(2,1)S(1)}, u32[]{:S(2)}, u32[]{:S(2)}) %collective-permute-start.19) | collective-permute-done | bytes 16416 | tf_op jit(solution)/shard_map/ppermute | solution.py:31
  73.7 1.9 collective-permute-start.20
  75.7 3.1 %collective-permute-done.20 = bf16[128,128]{0,1:T(8,128)(2,1)S(1)} collective-permute-done((bf16[128,128]{0,1:T(8,128)(2,1)S(1)}, bf16[128,128]{0,1:T(8,128)(2,1)S(1)}, u32[]{:S(2)}, u32[]{:S(2)}) %collective-permute-start.20) | collective-permute-done | bytes 32800 | tf_op jit(solution)/shard_map/ppermute | solution.py:31
  78.9 7.0 %collective-permute-start.21 = (bf16[256,128]{0,1:T(8,128)(2,1)S(1)}, bf16[256,128]{0,1:T(8,128)(2,1)S(1)}, u32[]{:S(2)}, u32[]{:S(2)}) collective-permute-start(bf16[256,128]{0,1:T(8,128)(2,1)S(1)} %pad_maximum_fusion.6), channel_id=1, source_target_pairs={{0,1},{1,0},{2,3},{3,2},{4,5},{5,4},{6,7},{7,6},{8,9},{9,8},{10,11... | collective-permute-start | bytes 196616 | tf_op jit(solution)/shard_map/ppermute | solution.py:31
  85.9 8.6 %collective-permute-start.3 = (bf16[512,256]{1,0:T(8,128)(2,1)S(1)}, bf16[512,256]{1,0:T(8,128)(2,1)S(1)}, u32[]{:S(2)}, u32[]{:S(2)}) collective-permute-start(bf16[512,256]{1,0:T(8,128)(2,1)S(1)} %add_convert_fusion.1.refs_0_), channel_id=1, source_target_pairs={{0,6},{2,0},{4,2},{6,4},{8,14},{10,8},{12,10},{14,12},{16,22},{18,... | collective-permute-start | bytes 786440 | tf_op jit(solution)/shard_map/ppermute | solution.py:27
  94.5 1.9 collective-permute-start.1
  96.8 2.8 %collective-permute-start.24 = (f32[64,256]{1,0:T(8,128)S(1)}, f32[64,256]{1,0:T(8,128)S(1)}, u32[]{:S(2)}, u32[]{:S(2)}) collective-permute-start(f32[64,256]{1,0:T(8,128)S(1)} %get-tuple-element.41), channel_id=1, source_target_pairs={{0,128},{32,160},{64,192},{96,224},{128,0},{160,32},{192,64},{224,... | collective-permute-start | bytes 196616 | tf_op jit(solution)/shard_map/ppermute | solution.py:31
  99.7 22.1 %collective-permute-done.1.refs_1_ = bf16[512,256]{1,0:T(8,128)(2,1)S(1)} collective-permute-done((bf16[512,256]{1,0:T(8,128)(2,1)S(1)}, bf16[512,256]{1,0:T(8,128)(2,1)S(1)}, u32[]{:S(2)}, u32[]{:S(2)}) %collective-permute-start.1) | collective-permute-done | bytes 262176 | tf_op jit(solution)/shard_map/ppermute | solution.py:27
  122.5 4.6 %collective-permute-start.25 = (f32[32,256]{1,0:T(8,128)S(1)}, f32[32,256]{1,0:T(8,128)S(1)}, u32[]{:S(2)}, u32[]{:S(2)}) collective-permute-start(f32[32,256]{1,0:T(8,128)S(1)} %slice_select_fusion.2), channel_id=1, source_target_pairs={{0,256},{32,288},{64,320},{96,352},{128,384},{160,416},{192,448},{... | collective-permute-start | bytes 98312 | tf_op jit(solution)/shard_map/ppermute | solution.py:31
  127.9 4.5 %collective-permute-start.11 = (bf16[1024,256]{1,0:T(8,128)(2,1)}, bf16[1024,256]{1,0:T(8,128)(2,1)S(1)}, u32[]{:S(2)}, u32[]{:S(2)}) collective-permute-start(bf16[1024,256]{1,0:T(8,128)(2,1)} %constant_dynamic-update-slice_fusion), channel_id=1, source_target_pairs={{0,24},{2,26},{4,28},{6,30},{8,0},{10,2},{12,4},{14,6},{16,8},{18,... | collective-permute-start | bytes 1572872 | tf_op jit(solution)/shard_map/ppermute | solution.py:22
  132.4 19.4 %collective-permute-start.26 = (f32[32,256]{1,0:T(8,128)S(1)}, f32[32,256]{1,0:T(8,128)S(1)}, u32[]{:S(2)}, u32[]{:S(2)}) collective-permute-start(f32[32,256]{1,0:T(8,128)S(1)} %select_add_fusion.4), channel_id=1, source_target_pairs={{0,32},{32,0},{64,96},{96,64},{128,160},{160,128},{192,224},{224,1... | collective-permute-start | bytes 98312 | tf_op jit(solution)/shard_map/ppermute | solution.py:31
  151.8 2.3 collective-permute-start.8
  154.1 2.7 %collective-permute-start.5 = (bf16[1024,256]{1,0:T(8,128)(2,1)}, bf16[1024,256]{1,0:T(8,128)(2,1)S(1)}, u32[]{:S(2)}, u32[]{:S(2)}) collective-permute-start(bf16[1024,256]{1,0:T(8,128)(2,1)} %constant_dynamic-update-slice_fusion), channel_id=1, source_target_pairs={{0,8},{2,10},{4,12},{6,14},{8,16},{10,18},{12,20},{14,22},{16,24},... | collective-permute-start | bytes 1572872 | tf_op jit(solution)/shard_map/ppermute | solution.py:22
  157.5 3.3 %collective-permute-start.27 = (f32[32,256]{1,0:T(8,128)}, f32[32,256]{1,0:T(8,128)}, u32[]{:S(2)}, u32[]{:S(2)}) collective-permute-start(f32[32,256]{1,0:T(8,128)} %add.211), channel_id=1, source_target_pairs={{0,64},{32,96},{64,0},{96,32},{128,192},{160,224},{192,128},{224,1... | collective-permute-start | bytes 98312 | tf_op jit(solution)/shard_map/ppermute | solution.py:31
  161.1 3.9 %collective-permute-start.10 = (bf16[512,256]{1,0:T(8,128)(2,1)S(1)}, bf16[512,256]{1,0:T(8,128)(2,1)S(1)}, u32[]{:S(2)}, u32[]{:S(2)}) collective-permute-start(bf16[512,256]{1,0:T(8,128)(2,1)S(1)} %add_convert_fusion.1.refs_0_), channel_id=1, source_target_pairs={{0,24},{2,26},{4,28},{6,30},{8,0},{10,2},{12,4},{14,6},{16,8},{18,... | collective-permute-start | bytes 786440 | tf_op jit(solution)/shard_map/ppermute | solution.py:22
  165.0 3.6 %collective-permute-start.2 = (bf16[512,256]{1,0:T(8,128)(2,1)S(1)}, bf16[512,256]{1,0:T(8,128)(2,1)S(1)}, u32[]{:S(2)}, u32[]{:S(2)}) collective-permute-start(bf16[512,256]{1,0:T(8,128)(2,1)S(1)} %add_convert_fusion.1.refs_0_), channel_id=1, source_target_pairs={{0,4},{2,6},{4,0},{6,2},{8,12},{10,14},{12,8},{14,10},{16,20},{18,... | collective-permute-start | bytes 786440 | tf_op jit(solution)/shard_map/ppermute | solution.py:27
  168.6 1.4 add_multiply_fusion
  170.0 0.8 copy-done.23
  170.8 3.3 %collective-permute-start.7 = (bf16[512,256]{1,0:T(8,128)(2,1)S(1)}, bf16[512,256]{1,0:T(8,128)(2,1)S(1)}, u32[]{:S(2)}, u32[]{:S(2)}) collective-permute-start(bf16[512,256]{1,0:T(8,128)(2,1)S(1)} %add_convert_fusion.1.refs_0_), channel_id=1, source_target_pairs={{0,16},{2,18},{4,20},{6,22},{8,24},{10,26},{12,28},{14,30},{16,0},... | collective-permute-start | bytes 786440 | tf_op jit(solution)/shard_map/ppermute | solution.py:22
  174.1 1.1 fusion.57
  175.2 1.9 collective-permute-start.4
  177.1 15.4 %collective-permute-done.2.refs_2_ = bf16[512,256]{1,0:T(8,128)(2,1)S(1)} collective-permute-done((bf16[512,256]{1,0:T(8,128)(2,1)S(1)}, bf16[512,256]{1,0:T(8,128)(2,1)S(1)}, u32[]{:S(2)}, u32[]{:S(2)}) %collective-permute-start.2) | collective-permute-done | bytes 262176 | tf_op jit(solution)/shard_map/ppermute | solution.py:27
  192.5 1.9 collective-permute-start.12
  194.4 10.5 %collective-permute-start.9 = (bf16[512,256]{1,0:T(8,128)(2,1)S(1)}, bf16[512,256]{1,0:T(8,128)(2,1)S(1)}, u32[]{:S(2)}, u32[]{:S(2)}) collective-permute-start(bf16[512,256]{1,0:T(8,128)(2,1)S(1)} %collective-permute-done.2.refs_2_), channel_id=1, source_target_pairs={{0,16},{2,18},{4,20},{6,22},{8,24},{10,26},{12,28},{14,30},{16,0},... | collective-permute-start | bytes 786440 | tf_op jit(solution)/shard_map/ppermute | solution.py:22
  205.0 0.8 copy-done.22
  205.8 2.7 %collective-permute-start.6 = (bf16[512,256]{1,0:T(8,128)(2,1)S(1)}, bf16[512,256]{1,0:T(8,128)(2,1)S(1)}, u32[]{:S(2)}, u32[]{:S(2)}) collective-permute-start(bf16[512,256]{1,0:T(8,128)(2,1)S(1)} %collective-permute-done.2.refs_2_), channel_id=1, source_target_pairs={{0,8},{2,10},{4,12},{6,14},{8,16},{10,18},{12,20},{14,22},{16,24},... | collective-permute-start | bytes 786440 | tf_op jit(solution)/shard_map/ppermute | solution.py:22
  208.6 1.1 fusion.59
  210.4 1.9 collective-permute-start.28
  214.5 2.2 collective-permute-done.6.refs_6_
  217.4 2.2 copy-done.1
  219.6 0.9 copy-done.3
  220.5 0.9 copy-done.5
  221.5 0.9 copy-done.7
  222.4 0.9 copy-done.9
  223.4 0.9 copy-done.11
  224.3 0.9 copy-done.13
  225.3 0.9 copy-done.15
  226.2 2.9 %frozen.1 = (f32[512,256]{1,0:T(8,128)S(1)}, f32[512,256]{1,0:T(8,128)S(1)}) custom-call(s32[16]{0:T(128)S(1)} %stack.74.order_ref, bf16[512,256]{1,0:T(8,128)(2,1)S(1)} %add_convert_fusion.1.refs_0_, bf16[512,256]{1,0:T(8,128)(2,1)S(1)} %collective-permute-done.1.refs_1_, bf16[512,256]{1,0:T(8,128)(2,1)S(1)} %copy-done.5, ...), custom_call_target="tpu_custom_call" | custom-call | tf_op jit(solution)/shard_map/frozen/pallas_call | solution.py:63
  229.1 3.7 %collective-permute-start.13 = (f32[512,256]{1,0:T(8,128)S(1)}, f32[512,256]{1,0:T(8,128)S(1)}, u32[]{:S(2)}, u32[]{:S(2)}) collective-permute-start(f32[512,256]{1,0:T(8,128)S(1)} %get-tuple-element.8), channel_id=1, source_target_pairs={{0,1},{1,0},{2,3},{3,2},{4,5},{5,4},{6,7},{7,6},{8,9},{9,8},{10,11... | collective-permute-start | bytes 1572872 | tf_op jit(solution)/shard_map/ppermute | solution.py:31
  233.1 0.9 broadcast_select_fusion.14
  233.9 3.7 %collective-permute-start.29 = (f32[64,256]{1,0:T(8,128)S(1)}, f32[64,256]{1,0:T(8,128)}, u32[]{:S(2)}, u32[]{:S(2)}) collective-permute-start(f32[64,256]{1,0:T(8,128)S(1)} %pad_maximum_fusion.7), channel_id=1, source_target_pairs={{0,128},{32,160},{64,192},{96,224},{128,0},{160,32},{192,64},{224,... | collective-permute-start | bytes 196616 | tf_op jit(solution)/shard_map/ppermute | solution.py:31
  239.3 2.1 fusion.2
  242.0 2.2 collective-permute-start.22
  244.2 1.5 broadcast_select_fusion.7
  245.8 1.9 collective-permute-start.23
  248.1 0.8 copy.56
  248.9 16.0 %collective-permute-done.23 = f32[512,2,32]{0,2,1:T(8,128)S(1)} collective-permute-done((f32[512,2,32]{0,2,1:T(8,128)S(1)}, f32[512,2,32]{0,2,1:T(8,128)S(1)}, u32[]{:S(2)}, u32[]{:S(2)}) %collective-permute-start.23) | collective-permute-done | bytes 131104 | tf_op jit(solution)/shard_map/ppermute | solution.py:31
  (125 shorter events, 12.0 us)
Async XLA Ops:
  7.2 12.7 %copy-start = (bf16[1,512,1024]{2,1,0:T(8,128)(2,1)S(1)}, bf16[1,512,1024]{2,1,0:T(8,128)(2,1)}, u32[]{:S(2)}) copy-start(bf16[1,512,1024]{2,1,0:T(8,128)(2,1)} %param.11) | copy-start | bytes 3145732
  7.2 210.2 %all-gather.3.cloned.1.call-start = ((), (), s32[]{:S(2)}) async-start(), calls=%async_computation | async-start | bytes 4456448 | tf_op jit(solution)/shard_map/all_gather | solution.py:108
  8.4 11.0 %copy-start.24 = (bf16[1,512,256]{2,1,0:T(8,128)(2,1)S(1)}, bf16[1,512,256]{2,1,0:T(8,128)(2,1)}, u32[]{:S(2)}) copy-start(bf16[1,512,256]{2,1,0:T(8,128)(2,1)} %param.10) | copy-start | bytes 786436
  8.4 11.2 %copy-start.28 = (s32[1,512]{1,0:T(1,128)S(1)}, s32[1,512]{1,0:T(1,128)}, u32[]{:S(2)}) copy-start(s32[1,512]{1,0:T(1,128)} %param.13) | copy-start | bytes 6148
  8.5 10.1 %collective-permute-start = (bf16[576,256]{1,0:T(8,128)(2,1)S(1)}, bf16[576,256]{1,0:T(8,128)(2,1)S(1)}, u32[]{:S(2)}, u32[]{:S(2)}) collective-permute-start(bf16[576,256]{1,0:T(8,128)(2,1)S(1)} %broadcast_select_fusion.3), channel_id=1, source_target_pairs={{0,1},{1,0},{2,3},{3,2},{4,5},{5,4},{6,7},{7,6},{8,9},{9,8},{10,11... | collective-permute-start | bytes 884744 | tf_op jit(solution)/shard_map/ppermute | solution.py:31
  19.6 2.5 copy-start.20
  22.1 3.4 %copy-start.25 = (bf16[256,64]{0,1:T(8,128)(2,1)S(1)}, bf16[256,64]{0,1:T(8,128)(2,1)}, u32[]{:S(2)}) copy-start(bf16[256,64]{0,1:T(8,128)(2,1)} %param.18) | copy-start | bytes 98308
  24.0 2.2 copy-start.16
  24.0 1.8 copy-start.29
  24.1 2.0 copy-start.27
  25.5 71.1 %copy-start.18 = (bf16[128,2,512]{2,0,1:T(8,128)(2,1)}, bf16[128,2,512]{2,0,1:T(8,128)(2,1)S(1)}, u32[]{:S(2)}) copy-start(bf16[128,2,512]{2,0,1:T(8,128)(2,1)S(1)} %convolution_convert_fusion) | copy-start | bytes 786436
  26.3 3.3 %collective-permute-start.14 = (f32[256,128]{0,1:T(8,128)S(1)}, f32[256,128]{0,1:T(8,128)S(1)}, u32[]{:S(2)}, u32[]{:S(2)}) collective-permute-start(f32[256,128]{0,1:T(8,128)S(1)} %broadcast_select_fusion.6), channel_id=1, source_target_pairs={{0,1},{1,0},{2,3},{3,2},{4,5},{5,4},{6,7},{7,6},{8,9},{9,8},{10,11... | collective-permute-start | bytes 393224 | tf_op jit(solution)/shard_map/ppermute | solution.py:31
  29.6 5.0 %collective-permute-start.15 = (f32[128,128]{0,1:T(8,128)S(1)}, f32[128,128]{0,1:T(8,128)S(1)}, u32[]{:S(2)}, u32[]{:S(2)}) collective-permute-start(f32[128,128]{0,1:T(8,128)S(1)} %slice_select_fusion.1), channel_id=1, source_target_pairs={{0,8},{2,10},{4,12},{6,14},{8,0},{10,2},{12,4},{14,6},{16,24},{18,... | collective-permute-start | bytes 196616 | tf_op jit(solution)/shard_map/ppermute | solution.py:31
  34.7 6.9 %collective-permute-start.16 = (f32[64,128]{0,1:T(8,128)S(1)}, f32[64,128]{0,1:T(8,128)S(1)}, u32[]{:S(2)}, u32[]{:S(2)}) collective-permute-start(f32[64,128]{0,1:T(8,128)S(1)} %slice_select_fusion), channel_id=1, source_target_pairs={{0,16},{2,18},{4,20},{6,22},{8,24},{10,26},{12,28},{14,30},{16,0},... | collective-permute-start | bytes 98312 | tf_op jit(solution)/shard_map/ppermute | solution.py:31
  41.7 10.4 %collective-permute-start.17 = (f32[64,128]{0,1:T(8,128)S(1)}, f32[64,128]{0,1:T(8,128)S(1)}, u32[]{:S(2)}, u32[]{:S(2)}) collective-permute-start(f32[64,128]{0,1:T(8,128)S(1)} %select_add_fusion.2), channel_id=1, source_target_pairs={{0,2},{2,0},{4,6},{6,4},{8,10},{10,8},{12,14},{14,12},{16,18},{18,... | collective-permute-start | bytes 98312 | tf_op jit(solution)/shard_map/ppermute | solution.py:31
  52.1 14.9 %collective-permute-start.18 = (f32[64,128]{0,1:T(8,128)S(1)}, f32[64,128]{0,1:T(8,128)S(1)}, u32[]{:S(2)}, u32[]{:S(2)}) collective-permute-start(f32[64,128]{0,1:T(8,128)S(1)} %add.204), channel_id=1, source_target_pairs={{0,4},{2,6},{4,0},{6,2},{8,12},{10,14},{12,8},{14,10},{16,20},{18,... | collective-permute-start | bytes 98312 | tf_op jit(solution)/shard_map/ppermute | solution.py:31
  67.1 6.6 %collective-permute-start.19 = (bf16[64,128]{0,1:T(8,128)(2,1)S(1)}, bf16[64,128]{0,1:T(8,128)(2,1)S(1)}, u32[]{:S(2)}, u32[]{:S(2)}) collective-permute-start(bf16[64,128]{0,1:T(8,128)(2,1)S(1)} %add_convert_fusion.2), channel_id=1, source_target_pairs={{0,16},{2,18},{4,20},{6,22},{8,24},{10,26},{12,28},{14,30},{16,0},... | collective-permute-start | bytes 49160 | tf_op jit(solution)/shard_map/ppermute | solution.py:31
  73.7 5.1 %collective-permute-start.20 = (bf16[128,128]{0,1:T(8,128)(2,1)S(1)}, bf16[128,128]{0,1:T(8,128)(2,1)S(1)}, u32[]{:S(2)}, u32[]{:S(2)}) collective-permute-start(bf16[128,128]{0,1:T(8,128)(2,1)S(1)} %pad_maximum_fusion.8), channel_id=1, source_target_pairs={{0,8},{2,10},{4,12},{6,14},{8,0},{10,2},{12,4},{14,6},{16,24},{18,... | collective-permute-start | bytes 98312 | tf_op jit(solution)/shard_map/ppermute | solution.py:31
  78.9 17.5 %collective-permute-start.21 = (bf16[256,128]{0,1:T(8,128)(2,1)S(1)}, bf16[256,128]{0,1:T(8,128)(2,1)S(1)}, u32[]{:S(2)}, u32[]{:S(2)}) collective-permute-start(bf16[256,128]{0,1:T(8,128)(2,1)S(1)} %pad_maximum_fusion.6), channel_id=1, source_target_pairs={{0,1},{1,0},{2,3},{3,2},{4,5},{5,4},{6,7},{7,6},{8,9},{9,8},{10,11... | collective-permute-start | bytes 196616 | tf_op jit(solution)/shard_map/ppermute | solution.py:31
  85.9 41.3 %collective-permute-start.3 = (bf16[512,256]{1,0:T(8,128)(2,1)S(1)}, bf16[512,256]{1,0:T(8,128)(2,1)S(1)}, u32[]{:S(2)}, u32[]{:S(2)}) collective-permute-start(bf16[512,256]{1,0:T(8,128)(2,1)S(1)} %add_convert_fusion.1.refs_0_), channel_id=1, source_target_pairs={{0,6},{2,0},{4,2},{6,4},{8,14},{10,8},{12,10},{14,12},{16,22},{18,... | collective-permute-start | bytes 786440 | tf_op jit(solution)/shard_map/ppermute | solution.py:27
  94.5 27.3 %collective-permute-start.1 = (bf16[512,256]{1,0:T(8,128)(2,1)S(1)}, bf16[512,256]{1,0:T(8,128)(2,1)S(1)}, u32[]{:S(2)}, u32[]{:S(2)}) collective-permute-start(bf16[512,256]{1,0:T(8,128)(2,1)S(1)} %add_convert_fusion.1.refs_0_), channel_id=1, source_target_pairs={{0,2},{2,4},{4,6},{6,0},{8,10},{10,12},{12,14},{14,8},{16,18},{18,... | collective-permute-start | bytes 786440 | tf_op jit(solution)/shard_map/ppermute | solution.py:27
  96.8 25.7 %collective-permute-start.24 = (f32[64,256]{1,0:T(8,128)S(1)}, f32[64,256]{1,0:T(8,128)S(1)}, u32[]{:S(2)}, u32[]{:S(2)}) collective-permute-start(f32[64,256]{1,0:T(8,128)S(1)} %get-tuple-element.41), channel_id=1, source_target_pairs={{0,128},{32,160},{64,192},{96,224},{128,0},{160,32},{192,64},{224,... | collective-permute-start | bytes 196616 | tf_op jit(solution)/shard_map/ppermute | solution.py:31
  122.5 9.8 %collective-permute-start.25 = (f32[32,256]{1,0:T(8,128)S(1)}, f32[32,256]{1,0:T(8,128)S(1)}, u32[]{:S(2)}, u32[]{:S(2)}) collective-permute-start(f32[32,256]{1,0:T(8,128)S(1)} %slice_select_fusion.2), channel_id=1, source_target_pairs={{0,256},{32,288},{64,320},{96,352},{128,384},{160,416},{192,448},{... | collective-permute-start | bytes 98312 | tf_op jit(solution)/shard_map/ppermute | solution.py:31
  127.9 42.1 %collective-permute-start.11 = (bf16[1024,256]{1,0:T(8,128)(2,1)}, bf16[1024,256]{1,0:T(8,128)(2,1)S(1)}, u32[]{:S(2)}, u32[]{:S(2)}) collective-permute-start(bf16[1024,256]{1,0:T(8,128)(2,1)} %constant_dynamic-update-slice_fusion), channel_id=1, source_target_pairs={{0,24},{2,26},{4,28},{6,30},{8,0},{10,2},{12,4},{14,6},{16,8},{18,... | collective-permute-start | bytes 1572872 | tf_op jit(solution)/shard_map/ppermute | solution.py:22
  132.4 24.5 %collective-permute-start.26 = (f32[32,256]{1,0:T(8,128)S(1)}, f32[32,256]{1,0:T(8,128)S(1)}, u32[]{:S(2)}, u32[]{:S(2)}) collective-permute-start(f32[32,256]{1,0:T(8,128)S(1)} %select_add_fusion.4), channel_id=1, source_target_pairs={{0,32},{32,0},{64,96},{96,64},{128,160},{160,128},{192,224},{224,1... | collective-permute-start | bytes 98312 | tf_op jit(solution)/shard_map/ppermute | solution.py:31
  151.8 42.6 %collective-permute-start.8 = (bf16[1024,256]{1,0:T(8,128)(2,1)}, bf16[1024,256]{1,0:T(8,128)(2,1)S(1)}, u32[]{:S(2)}, u32[]{:S(2)}) collective-permute-start(bf16[1024,256]{1,0:T(8,128)(2,1)} %constant_dynamic-update-slice_fusion), channel_id=1, source_target_pairs={{0,16},{2,18},{4,20},{6,22},{8,24},{10,26},{12,28},{14,30},{16,0},... | collective-permute-start | bytes 1572872 | tf_op jit(solution)/shard_map/ppermute | solution.py:22
  154.1 50.9 %collective-permute-start.5 = (bf16[1024,256]{1,0:T(8,128)(2,1)}, bf16[1024,256]{1,0:T(8,128)(2,1)S(1)}, u32[]{:S(2)}, u32[]{:S(2)}) collective-permute-start(bf16[1024,256]{1,0:T(8,128)(2,1)} %constant_dynamic-update-slice_fusion), channel_id=1, source_target_pairs={{0,8},{2,10},{4,12},{6,14},{8,16},{10,18},{12,20},{14,22},{16,24},... | collective-permute-start | bytes 1572872 | tf_op jit(solution)/shard_map/ppermute | solution.py:22
  157.5 7.5 %collective-permute-start.27 = (f32[32,256]{1,0:T(8,128)}, f32[32,256]{1,0:T(8,128)}, u32[]{:S(2)}, u32[]{:S(2)}) collective-permute-start(f32[32,256]{1,0:T(8,128)} %add.211), channel_id=1, source_target_pairs={{0,64},{32,96},{64,0},{96,32},{128,192},{160,224},{192,128},{224,1... | collective-permute-start | bytes 98312 | tf_op jit(solution)/shard_map/ppermute | solution.py:31
  161.1 14.1 %collective-permute-start.10 = (bf16[512,256]{1,0:T(8,128)(2,1)S(1)}, bf16[512,256]{1,0:T(8,128)(2,1)S(1)}, u32[]{:S(2)}, u32[]{:S(2)}) collective-permute-start(bf16[512,256]{1,0:T(8,128)(2,1)S(1)} %add_convert_fusion.1.refs_0_), channel_id=1, source_target_pairs={{0,24},{2,26},{4,28},{6,30},{8,0},{10,2},{12,4},{14,6},{16,8},{18,... | collective-permute-start | bytes 786440 | tf_op jit(solution)/shard_map/ppermute | solution.py:22
  165.0 27.5 %collective-permute-start.2 = (bf16[512,256]{1,0:T(8,128)(2,1)S(1)}, bf16[512,256]{1,0:T(8,128)(2,1)S(1)}, u32[]{:S(2)}, u32[]{:S(2)}) collective-permute-start(bf16[512,256]{1,0:T(8,128)(2,1)S(1)} %add_convert_fusion.1.refs_0_), channel_id=1, source_target_pairs={{0,4},{2,6},{4,0},{6,2},{8,12},{10,14},{12,8},{14,10},{16,20},{18,... | collective-permute-start | bytes 786440 | tf_op jit(solution)/shard_map/ppermute | solution.py:27
  170.0 0.8 copy-start.23
  170.8 38.9 %collective-permute-start.7 = (bf16[512,256]{1,0:T(8,128)(2,1)S(1)}, bf16[512,256]{1,0:T(8,128)(2,1)S(1)}, u32[]{:S(2)}, u32[]{:S(2)}) collective-permute-start(bf16[512,256]{1,0:T(8,128)(2,1)S(1)} %add_convert_fusion.1.refs_0_), channel_id=1, source_target_pairs={{0,16},{2,18},{4,20},{6,22},{8,24},{10,26},{12,28},{14,30},{16,0},... | collective-permute-start | bytes 786440 | tf_op jit(solution)/shard_map/ppermute | solution.py:22
  175.2 37.2 %copy-start.2 = (bf16[512,256]{1,0:T(8,128)(2,1)}, bf16[512,256]{1,0:T(8,128)(2,1)S(1)}, u32[]{:S(2)}) copy-start(bf16[512,256]{1,0:T(8,128)(2,1)S(1)} %collective-permute-done.10.refs_12_) | copy-start | bytes 786436
  175.2 37.2 %collective-permute-start.4 = (bf16[512,256]{1,0:T(8,128)(2,1)S(1)}, bf16[512,256]{1,0:T(8,128)(2,1)S(1)}, u32[]{:S(2)}, u32[]{:S(2)}) collective-permute-start(bf16[512,256]{1,0:T(8,128)(2,1)S(1)} %add_convert_fusion.1.refs_0_), channel_id=1, source_target_pairs={{0,8},{2,10},{4,12},{6,14},{8,16},{10,18},{12,20},{14,22},{16,24},... | collective-permute-start | bytes 786440 | tf_op jit(solution)/shard_map/ppermute | solution.py:22
  192.5 20.6 %copy-start.4 = (bf16[512,256]{1,0:T(8,128)(2,1)}, bf16[512,256]{1,0:T(8,128)(2,1)S(1)}, u32[]{:S(2)}) copy-start(bf16[512,256]{1,0:T(8,128)(2,1)S(1)} %collective-permute-done.2.refs_2_) | copy-start | bytes 786436
  192.5 20.6 %collective-permute-start.12 = (bf16[512,256]{1,0:T(8,128)(2,1)S(1)}, bf16[512,256]{1,0:T(8,128)(2,1)S(1)}, u32[]{:S(2)}, u32[]{:S(2)}) collective-permute-start(bf16[512,256]{1,0:T(8,128)(2,1)S(1)} %collective-permute-done.2.refs_2_), channel_id=1, source_target_pairs={{0,24},{2,26},{4,28},{6,30},{8,0},{10,2},{12,4},{14,6},{16,8},{18,... | collective-permute-start | bytes 786440 | tf_op jit(solution)/shard_map/ppermute | solution.py:22
  194.4 19.4 %collective-permute-start.9 = (bf16[512,256]{1,0:T(8,128)(2,1)S(1)}, bf16[512,256]{1,0:T(8,128)(2,1)S(1)}, u32[]{:S(2)}, u32[]{:S(2)}) collective-permute-start(bf16[512,256]{1,0:T(8,128)(2,1)S(1)} %collective-permute-done.2.refs_2_), channel_id=1, source_target_pairs={{0,16},{2,18},{4,20},{6,22},{8,24},{10,26},{12,28},{14,30},{16,0},... | collective-permute-start | bytes 786440 | tf_op jit(solution)/shard_map/ppermute | solution.py:22
  205.0 0.8 copy-start.22
  205.8 10.8 %collective-permute-start.6 = (bf16[512,256]{1,0:T(8,128)(2,1)S(1)}, bf16[512,256]{1,0:T(8,128)(2,1)S(1)}, u32[]{:S(2)}, u32[]{:S(2)}) collective-permute-start(bf16[512,256]{1,0:T(8,128)(2,1)S(1)} %collective-permute-done.2.refs_2_), channel_id=1, source_target_pairs={{0,8},{2,10},{4,12},{6,14},{8,16},{10,18},{12,20},{14,22},{16,24},... | collective-permute-start | bytes 786440 | tf_op jit(solution)/shard_map/ppermute | solution.py:22
  209.7 0.7 copy-start.6
  210.4 22.6 %collective-permute-start.28 = (f32[32,256]{1,0:T(8,128)}, f32[32,256]{1,0:T(8,128)}, u32[]{:S(2)}, u32[]{:S(2)}) collective-permute-start(f32[32,256]{1,0:T(8,128)} %add_multiply_fusion), channel_id=1, source_target_pairs={{0,256},{32,288},{64,320},{96,352},{128,384},{160,416},{192,448},{... | collective-permute-start | bytes 98312 | tf_op jit(solution)/shard_map/ppermute | solution.py:31
  212.4 0.7 copy-start.8
  213.1 0.7 copy-start.10
  213.8 0.7 copy-start.12
  216.7 0.7 copy-start.14
  217.4 2.2 copy-start.1
  219.6 0.9 copy-start.3
  220.5 0.9 copy-start.5
  221.5 0.9 copy-start.7
  222.4 0.9 copy-start.9
  223.4 0.9 copy-start.11
  224.3 0.9 copy-start.13
  225.3 0.9 copy-start.15
  226.2 6.6 %copy-start.26 = (bf16[256,64]{0,1:T(8,128)(2,1)S(1)}, bf16[256,64]{0,1:T(8,128)(2,1)}, u32[]{:S(2)}) copy-start(bf16[256,64]{0,1:T(8,128)(2,1)} %param.18) | copy-start | bytes 98308
  229.1 8.6 %collective-permute-start.13 = (f32[512,256]{1,0:T(8,128)S(1)}, f32[512,256]{1,0:T(8,128)S(1)}, u32[]{:S(2)}, u32[]{:S(2)}) collective-permute-start(f32[512,256]{1,0:T(8,128)S(1)} %get-tuple-element.8), channel_id=1, source_target_pairs={{0,1},{1,0},{2,3},{3,2},{4,5},{5,4},{6,7},{7,6},{8,9},{9,8},{10,11... | collective-permute-start | bytes 1572872 | tf_op jit(solution)/shard_map/ppermute | solution.py:31
  233.1 5.2 %copy-start.17 = (bf16[2,512,512]{1,2,0:T(8,128)(2,1)S(1)}, bf16[2,512,512]{1,2,0:T(8,128)(2,1)}, u32[]{:S(2)}) copy-start(bf16[2,512,512]{1,2,0:T(8,128)(2,1)} %copy-done.16) | copy-start | bytes 3145732
  233.9 10.2 %collective-permute-start.29 = (f32[64,256]{1,0:T(8,128)S(1)}, f32[64,256]{1,0:T(8,128)}, u32[]{:S(2)}, u32[]{:S(2)}) collective-permute-start(f32[64,256]{1,0:T(8,128)S(1)} %pad_maximum_fusion.7), channel_id=1, source_target_pairs={{0,128},{32,160},{64,192},{96,224},{128,0},{160,32},{192,64},{224,... | collective-permute-start | bytes 196616 | tf_op jit(solution)/shard_map/ppermute | solution.py:31
  238.3 1.0 copy-start.19
  239.3 2.1 copy-start.21
  242.0 3.7 %collective-permute-start.22 = (f32[512,2,2,32]{0,3,2,1:T(8,128)S(1)}, f32[512,2,2,32]{0,3,2,1:T(8,128)S(1)}, u32[]{:S(2)}, u32[]{:S(2)}) collective-permute-start(f32[512,2,2,32]{0,3,2,1:T(8,128)S(1)} %select_bitcast_fusion), channel_id=1, source_target_pairs={{0,1},{1,0},{2,3},{3,2},{4,5},{5,4},{6,7},{7,6},{8,9},{9,8},{10,11... | collective-permute-start | bytes 786440 | tf_op jit(solution)/shard_map/ppermute | solution.py:31
  245.8 19.1 %collective-permute-start.23 = (f32[512,2,32]{0,2,1:T(8,128)S(1)}, f32[512,2,32]{0,2,1:T(8,128)S(1)}, u32[]{:S(2)}, u32[]{:S(2)}) collective-permute-start(f32[512,2,32]{0,2,1:T(8,128)S(1)} %select_bitcast_fusion.1), channel_id=1, source_target_pairs={{0,2},{2,0},{4,6},{6,4},{8,10},{10,8},{12,14},{14,12},{16,18},{18,... | collective-permute-start | bytes 393224 | tf_op jit(solution)/shard_map/ppermute | solution.py:31
Sparse Core Ops, SparseCore 0:
  19.6 137.6 all-gather.2

commit v2 on v1

--- a/solution.py
+++ b/solution.py
@@ -1,3 +1,5 @@
+import functools
+
 import jax
 import jax.numpy as jnp
 from jax import lax
@@ -17,14 +19,29 @@
 TN = (((0,), (0,)), ((), ()))
 
 
-def high_shift(array, axis, k):
-    pairs = [(i * SIDE + j, (i + k) % SIDE * SIDE + j) for i in range(SIDE) for j in range(SIDE)]
-    return lax.ppermute(array, axis, pairs)
-
-
-def low_shift(array, axis, k):
-    pairs = [(i * SIDE + j, i * SIDE + (j + k) % SIDE) for i in range(SIDE) for j in range(SIDE)]
-    return lax.ppermute(array, axis, pairs)
+AXES = ("dp", "tensor", "draft")
+Z_SHIFT, Z_MASK = (0, 1, 3, 2), (0, 1, 2, 3)
+
+
+def moved(array, residual_to, slab_to):
+    n_dp, n_tensor = lax.axis_size("dp"), lax.axis_size("tensor")
+    pairs = []
+    for d in range(n_dp):
+        for t in range(n_tensor):
+            at = (d * n_tensor + t) * 2
+            pairs.append((at, (d * n_tensor + residual_to(t)) * 2))
+            pairs.append((at + 1, (slab_to(d) * n_tensor + t) * 2 + 1))
+    return lax.ppermute(array, AXES, pairs)
+
+
+def far_move(array, k):
+    step = lambda i: (i + k * SIDE) % (SIDE * SIDE)
+    return moved(array, step, step)
+
+
+def near_move(array, stage):
+    ahead = lambda t: t // SIDE * SIDE + (t + Z_SHIFT[stage]) % SIDE
+    return moved(array, ahead, lambda d: d ^ Z_MASK[stage])
 
 
 def swapped(array, axis, mask):
@@ -47,28 +64,157 @@
     return jnp.concatenate([jnp.where(upper, other, array), jnp.where(upper, array, other)], axis=0)
 
 
-def frozen_kernel(order_ref, *refs):
-    pieces, slab, mine, other = refs[:16], refs[16], refs[17], refs[18]
-    n = mine.shape[1]
-    total = None
-    for i, piece in enumerate(pieces):
-        term = lax.dot_general(piece[...], slab[order_ref[i]], NT, preferred_element_type=F32)
-        total = term if total is None else total + term
-    mine[...] = total[:, :n]
-    other[...] = total[:, n:]
-
-
-def frozen_product(order, pieces, slab):
-    rows, cols = pieces[0].shape[0], slab.shape[1] // 2
+def after(array, *earlier):
+    return lax.optimization_barrier((array, *earlier))[0]
+
+
+def pack_kernel(core_ref, rows_ref, taps_ref, slab_ref, give_ref):
+    n = rows_ref.shape[0]
+
+    @pl.when(core_ref[0] == 0)
+    def _():
+        give_ref[:n] = slab_ref[...]
+
+    @pl.when(core_ref[0] == 1)
+    def _():
+        give_ref[:n] = rows_ref[...]
+
+    give_ref[n:] = taps_ref[...]
+
+
+def pack(core, rows, taps, slab):
     return pl.pallas_call(
-        frozen_kernel,
-        out_shape=(jax.ShapeDtypeStruct((rows, cols), F32),) * 2,
+        pack_kernel,
+        out_shape=jax.ShapeDtypeStruct((rows.shape[0] + taps.shape[0], rows.shape[1]), BF16),
         in_specs=[pl.BlockSpec(memory_space=pltpu.SMEM)]
-        + [pl.BlockSpec(memory_space=pltpu.VMEM)] * 17,
+        + [pl.BlockSpec(memory_space=pltpu.VMEM)] * 3,
+        out_specs=pl.BlockSpec(memory_space=pltpu.VMEM),
+        name="pack",
+    )(core, rows, taps, slab)
+
+
+def blend_kernel(core_ref, tapped_ref, rows_ref, taps_ref, slab_ref, came_ref, block_ref, give_ref):
+    n, n_taps = rows_ref.shape[0], taps_ref.shape[0]
+    half = give_ref.shape[1]
+
+    @pl.when(core_ref[0] == 0)
+    def _():
+        taps = jnp.concatenate([taps_ref[...], came_ref[n:]], axis=0)
+        place = lax.broadcasted_iota(jnp.int32, (2 * n, 2 * n_taps), 0)
+        hit = jnp.where(place == tapped_ref[...], 1.0, 0.0).astype(BF16)
+        spread = jnp.dot(hit, taps, preferred_element_type=F32)
+        block_ref[:n] = (rows_ref[...].astype(F32) + spread[:n]).astype(BF16)
+        block_ref[n:] = (came_ref[:n].astype(F32) + spread[n:]).astype(BF16)
+        give_ref[...] = block_ref[:, half:]
+
+    @pl.when(core_ref[0] == 1)
+    def _():
+        block_ref[:n] = came_ref[:n]
+        block_ref[n:] = slab_ref[...]
+        give_ref[...] = block_ref[:, :half]
+
+
+def blend(core, tapped, rows, taps, slab, came):
+    n, width = rows.shape
+    return pl.pallas_call(
+        blend_kernel,
+        out_shape=(
+            jax.ShapeDtypeStruct((2 * n, width), BF16),
+            jax.ShapeDtypeStruct((2 * n, width // 2), BF16),
+        ),
+        in_specs=[pl.BlockSpec(memory_space=pltpu.SMEM)]
+        + [pl.BlockSpec(memory_space=pltpu.VMEM)] * 5,
         out_specs=(pl.BlockSpec(memory_space=pltpu.VMEM),) * 2,
-        compiler_params=pltpu.CompilerParams(vmem_limit_bytes=40 * 1024 * 1024),
+        name="blend",
+    )(core, tapped, rows, taps, slab, came)
+
+
+def give_half(core, arrays):
+    half = arrays[0].shape[1] // 2
+    return jnp.concatenate(
+        [jnp.where(core == 1, a[:, :half], a[:, half:]) for a in arrays], axis=0
+    )
+
+
+def frozen_kernel(n_held, sizes, core_ref, order_ref, *refs):
+    n = len(sizes)
+    sources, (mine, other, own, came, sems) = refs[:n], refs[n:]
+    rows, cols = mine.shape
+    width = own.shape[1]
+    blocks = own.shape[0] // rows
+    columns = pl.ds(pl.multiple_of(core_ref[0] * width, width), width)
+    copies, at = [], 0
+    for i, size in enumerate(sizes):
+        if i == n_held:
+            at = 0
+        if i < n_held:
+            source, target = sources[i].at[:, columns], own.at[pl.ds(at, size)]
+        else:
+            source, target = sources[i], came.at[pl.ds(at, size)]
+        copies.append(pltpu.make_async_copy(source, target, sems.at[i]))
+        copies[-1].start()
+        at += size
+    for copy in copies:
+        copy.wait()
+
+    def matched(i):
+        return came[pl.ds(pl.multiple_of(order_ref[i] * rows, rows), rows)]
+
+    def held(i):
+        return own[i * rows : (i + 1) * rows]
+
+    def product(left, right):
+        return lax.dot_general(left, right, NT, preferred_element_type=F32)
+
+    @pl.when(core_ref[0] == 0)
+    def _():
+        total = product(held(0), matched(0))
+        for i in range(1, blocks):
+            total = total + product(held(i), matched(i))
+        mine[...] = total[:, :cols]
+        other[...] = total[:, cols:]
+
+    @pl.when(core_ref[0] == 1)
+    def _():
+        total = product(matched(0), held(0))
+        for i in range(1, blocks):
+            total = total + product(matched(i), held(i))
+        mine[...] = total[:, cols:]
+        other[...] = total[:, :cols]
+
+
+def frozen_product(core, order, own, came, rows):
+    arrays = (*own, *came)
+    sizes = tuple(a.shape[0] for a in arrays)
+    width = came[0].shape[1]
+    held = pltpu.VMEM((sum(a.shape[0] for a in own), width), BF16)
+    return pl.pallas_call(
+        functools.partial(frozen_kernel, len(own), sizes),
+        out_shape=(jax.ShapeDtypeStruct((rows, rows // 2), F32),) * 2,
+        in_specs=[pl.BlockSpec(memory_space=pltpu.SMEM)] * 2
+        + [pl.BlockSpec(memory_space=pl.ANY)] * len(arrays),
+        out_specs=(pl.BlockSpec(memory_space=pltpu.VMEM),) * 2,
+        scratch_shapes=[held, held, pltpu.SemaphoreType.DMA((len(arrays),))],
+        compiler_params=pltpu.CompilerParams(vmem_limit_bytes=56 * 1024 * 1024),
         name="frozen",
-    )(order, *pieces, slab)
+    )(core, order, *arrays)
+
+
+def block_order(core, dp, tensor):
+    stage = jnp.array([0] * 4 + [1, 2] * 4 + [3] * 4, jnp.int32)
+    step = jnp.array([0, 1, 2, 3, 0, 0, 1, 1, 2, 2, 3, 3, 0, 1, 2, 3], jnp.int32)
+    shift = jnp.where(stage == 2, 3, jnp.where(stage == 3, 2, stage))
+    first = core == 0
+    high = jnp.where(first, tensor // SIDE - step, dp // SIDE - step) % SIDE
+    low = jnp.where(first, (tensor - shift) % SIDE, (dp % SIDE) ^ stage)
+    their_step = jnp.where(first, dp // SIDE - high, tensor // SIDE - high) % SIDE
+    back = (tensor - low) % SIDE
+    back = jnp.where(back == 2, 3, jnp.where(back == 3, 2, back))
+    their_stage = jnp.where(first, (dp % SIDE) ^ low, back)
+    middle = 3 + their_stage + 2 * their_step
+    return jnp.where(
+        their_stage == 0, their_step, jnp.where(their_stage == 3, 12 + their_step, middle)
+    )
 
 
 def on_device(
@@ -94,38 +240,26 @@
     upper_core = core == 1
     rank_index = tensor * 2 + core
     kv_head = rank_index * heads_dev // group_size
-    tapped = tapped_row_index[0]
     width = output_projector.shape[1] // 2
     rank = lower_factor_weight.shape[1]
 
-    local = jnp.concatenate([output_gradient[0], draft_loss_gradients[0], output_projector], axis=0)
-    low, high = local[:, :width], local[:, width:]
-    own = jnp.where(upper_core, high, low)
-    came = swapped(jnp.where(upper_core, low, high), "draft", 1)
-    nr, nt = output_gradient.shape[1], draft_loss_gradients.shape[1]
-    first, second = jnp.where(upper_core, came, own), jnp.where(upper_core, own, came)
-    slab_own = jnp.concatenate([own[nr + nt :], came[nr + nt :]], axis=0)
-    slab = lax.all_gather(slab_own, "dp", axis=0)
-    rows = jnp.concatenate([first[:nr], second[:nr]], axis=0)
-    taps = jnp.concatenate([first[nr : nr + nt], second[nr : nr + nt]], axis=0)
-    hit = (jnp.arange(seq_len)[:, None] == tapped[None, :]).astype(BF16)
-    spread = jnp.dot(hit, taps, preferred_element_type=F32)
-    residual = (rows.astype(F32) + spread).astype(BF16)
-
-    z1, z3, z2 = (low_shift(residual, "tensor", k) for k in (1, 3, 2))
-    pieces = {(0, 0): residual, (0, 1): z1, (0, 3): z3, (0, 2): z2}
-    near = jnp.concatenate([z1, z3], axis=0)
-    for k in (1, 3, 2):
-        pieces[k, 0] = high_shift(residual, "tensor", k)
-    for k in (1, 3, 2):
-        both = high_shift(near, "tensor", k)
-        pieces[k, 1], pieces[k, 3] = both[:seq_len], both[seq_len:]
-    for k in (1, 3, 2):
-        pieces[k, 2] = high_shift(z2, "tensor", k)
-    keys = sorted(pieces)
-    order = jnp.stack(
-        [(tensor // SIDE - a) % SIDE * SIDE + (tensor % SIDE - b) % SIDE for a, b in keys]
-    ).astype(jnp.int32)
+    core_ref = core.reshape(1)
+    rows, taps = output_gradient[0], draft_loss_gradients[0]
+    came = swapped(pack(core_ref, rows, taps, output_projector), "draft", 1)
+    block, give = blend(core_ref, tapped_row_index, rows, taps, output_projector, came)
+    came_own = swapped(give, "draft", 1)
+    residual = jnp.where(upper_core, came_own, block[:, :width])
+
+    z1, z2 = near_move(block, 1), near_move(block, 2)
+    own_far = [far_move(block, k) for k in (1, 2, 3)]
+    z3 = near_move(after(block, z1, z2, *own_far), 3)
+    near = jnp.concatenate([z1, z2], axis=0)
+    near_far = [far_move(near, k) for k in (1, 2, 3)]
+    came_far = swapped(after(give_half(core, own_far), z1, z2), "draft", 1)
+    last_far = [far_move(z3, k) for k in (1, 2, 3)]
+    came_near = swapped(after(give_half(core, [z1, z2, *near_far]), z3), "draft", 1)
+    came_last = swapped(give_half(core, [z3, *last_far]), "draft", 1)
+    order = block_order(core, dp, tensor)
 
     query_heads = rotated_queries[0].reshape(seq_len, heads_dev, head_size)
     key_head = lax.dynamic_slice_in_dim(rotated_keys[0], kv_head * head_size, head_size, 1)
@@ -149,9 +283,10 @@
     inner_piece = jnp.dot(output_flattened, lower_factor_weight, preferred_element_type=F32)
     adapter_piece = lax.dot_general(residual, upper_factor_weight, NT, preferred_element_type=F32)
     sums = jnp.concatenate([inner_piece, adapter_piece], axis=1)
-    sums = scatter_step(sums, "draft", 1, upper_core)
-    sums = scatter_step(sums, "tensor", 4, tensor & 4 != 0)
+    sums = scatter_step(after(sums, *own_far), "draft", 1, upper_core)
+    sums = scatter_step(after(sums, z1, z2), "tensor", 4, tensor & 4 != 0)
     sums = scatter_step(sums, "tensor", 8, tensor & 8 != 0)
+    sums = after(sums, z3)
     sums = sums + swapped(sums, "tensor", 1)
     sums = sums + swapped(sums, "tensor", 2)
     sums = sums.astype(BF16)
@@ -163,16 +298,19 @@
     lower_piece = lax.dot_general(adapter_gradient, output_flattened, TN, preferred_element_type=F32)
     upper_piece = lax.dot_general(adapter_inner, residual, TN, preferred_element_type=F32)
     factor = jnp.concatenate([lower_piece, upper_piece], axis=0)
-    factor = scatter_step(factor, "dp", 4, dp & 4 != 0)
-    factor = scatter_step(factor, "dp", 8, dp & 8 != 0)
-    factor = factor + swapped(factor, "dp", 1)
-    factor = factor + swapped(factor, "dp", 2)
+    factor = after(factor, *near_far)
+    for mask in (4, 8, 1, 2):
+        factor = factor + swapped(factor, "dp", mask)
     factor = factor * (adapter_scale / lax.axis_size("dp"))
-    factor = gather_step(factor, "dp", 8, dp & 8 != 0)
-    factor = gather_step(factor, "dp", 4, dp & 4 != 0)
     lower_gradient, upper_gradient = factor[:rank].T, factor[rank:]
 
-    part_mine, part_other = frozen_product(order, [pieces[k] for k in keys], slab)
+    part_mine, part_other = frozen_product(
+        core_ref,
+        order,
+        [block, *own_far, z1, z2, *near_far, z3, *last_far],
+        [came_own, came_far, came_near, came_last],
+        seq_len,
+    )
     frozen_gradient = part_mine + swapped(part_other, "draft", 1)
     adapter_backward = lax.dot_general(
         adapter_gradient, lower_factor_weight, NT, preferred_element_type=F32
@@ -200,7 +338,7 @@
     upper_chip = tensor & 1 == 1
     keep = jnp.where(upper_chip, combined[:, :, 1], combined[:, :, 0])
     give = jnp.where(upper_chip, combined[:, :, 0], combined[:, :, 1])
-    combined = keep + swapped(give, "tensor", 1)
+    combined = keep + swapped(give.astype(BF16), "tensor", 1).astype(F32)
     key_grad = combined[:, 0].astype(BF16)[None]
     value_grad = combined[:, 1].astype(BF16)[None]
     return (query_grad, key_grad, value_grad, lower_gradient, upper_gradient)

time: 274 us -> 239 us (0.87)
  waiting for transfers between devices: 86.4 us -> 59.1 us
  local copies, waits for them, and re-layouts: 20.2 us -> 5.82 us
  between operations: 15.1 us -> 1.78 us
  starting transfers between devices: 130 us -> 139 us
  Pallas kernels: 2.89 us -> 11.6 us
    ppermute x18 -> x20, waiting for transfers between devices: 46.7 us -> 27.1 us  [swapped(): lax.ppermute(array, axis, [(i, i ^ mask) for i in range(lax.axis_size(axi...]
    ppermute x18 -> x20, starting transfers between devices: 82.1 us -> 100 us  [swapped(): lax.ppermute(array, axis, [(i, i ^ mask) for i in range(lax.axis_size(axi...]
    unnamed x63 -> x51, local copies, waits for them, and re-layouts: 16.2 us -> 3.17 us
    ppermute x12, starting transfers between devices: 47.8 us -> 38.6 us  [moved(): return lax.ppermute(array, AXES, pairs)]
    pallas_call x1 -> x3, Pallas kernels: 2.89 us -> 11.6 us  [the longest x1 7.58 us: frozen_product(): pl.pallas_call(functools.partial(frozen_kernel, len(own), sizes), out_sha...]
    ppermute x12, waiting for transfers between devices: 39.6 us -> 32 us  [moved(): return lax.ppermute(array, AXES, pairs)]
  transfers between devices with their start and end apart: 31 -> 32, of which waited for: 12 -> 14; matrix products, arithmetic and copies ran while one was open for 8% -> 9% of each run, Pallas kernels for 1% -> 0%
where the time goes in v2:
time: 239 us; the launch traced here: 235 us
  starting transfers between devices  139 us (58%)
  waiting for transfers between devices  59.1 us (25%)
  Pallas kernels  11.6 us (5%)
  matrix products  10.7 us (4%)
  other arithmetic  7.24 us (3%)
  local copies, waits for them, and re-layouts  5.82 us (2%)
    ppermute x20, starting transfers between devices, swapped(): lax.ppermute(array, axis, [(i, i ^ mask) for i in range(lax.axis_size(axi...  100 us
    ppermute x12, starting transfers between devices, moved(): return lax.ppermute(array, AXES, pairs)  38.6 us
    ppermute x12, waiting for transfers between devices, moved(): return lax.ppermute(array, AXES, pairs)  32 us
    ppermute x20, waiting for transfers between devices, swapped(): lax.ppermute(array, axis, [(i, i ^ mask) for i in range(lax.axis_size(axi...  27.1 us
    pallas_call x1, Pallas kernels, frozen_product(): pl.pallas_call(functools.partial(frozen_kernel, len(own), sizes), out_sha...  7.58 us
  transfers between devices with their start and end apart: 32, of which 14 were waited for; matrix products, arithmetic and copies ran while one was open for 9% of the time, Pallas kernels for 0%

profile of v2, /device:TPU:1, one launch (start us, length us, event | category | flops | bytes accessed | tf_op | source)
XLA Modules:
  0.0 235.2 jit_solution(15639590741145268209)
XLA Ops:
  0.7 1.9 pack.1
  2.6 8.8 %collective-permute-start = (bf16[320,512]{1,0:T(8,128)(2,1)}, bf16[320,512]{1,0:T(8,128)(2,1)S(1)}, u32[]{:S(2)}, u32[]{:S(2)}) collective-permute-start(bf16[320,512]{1,0:T(8,128)(2,1)} %pack.1), channel_id=1, source_target_pairs={{0,1},{1,0},{2,3},{3,2},{4,5},{5,4},{6,7},{7,6},{8,9},{9,8},{10,11... | collective-permute-start | bytes 983048 | tf_op jit(solution)/shard_map/ppermute | solution.py:48
  11.4 1.1 copy.78
  12.5 1.0 fusion.9
  13.5 2.3 fusion.62
  15.7 1.9 fusion.11
  17.6 0.7 copy-done.19
  18.4 2.1 blend.1
  20.5 2.1 collective-permute-start.13
  22.6 1.2 convolution_convert_fusion
  23.9 1.9 collective-permute-start.4
  25.8 1.9 collective-permute-start.5
  27.7 0.9 fusion.65
  28.7 2.5 %collective-permute-start.1 = (bf16[512,512]{1,0:T(8,128)(2,1)}, bf16[512,512]{1,0:T(8,128)(2,1)S(1)}, u32[]{:S(2)}, u32[]{:S(2)}) collective-permute-start(bf16[512,512]{1,0:T(8,128)(2,1)} %get-tuple-element.17.refs_0_), channel_id=1, source_target_pairs={{0,8},{1,129},{2,10},{3,131},{4,12},{5,133},{6,14},{7,135},{8,16},... | collective-permute-start | bytes 1572872 | tf_op jit(solution)/shard_map/ppermute | solution.py:34
  31.2 4.4 %collective-permute-start.2 = (bf16[512,512]{1,0:T(8,128)(2,1)}, bf16[512,512]{1,0:T(8,128)(2,1)S(1)}, u32[]{:S(2)}, u32[]{:S(2)}) collective-permute-start(bf16[512,512]{1,0:T(8,128)(2,1)} %get-tuple-element.17.refs_0_), channel_id=1, source_target_pairs={{0,16},{1,257},{2,18},{3,259},{4,20},{5,261},{6,22},{7,263},{8,24}... | collective-permute-start | bytes 1572872 | tf_op jit(solution)/shard_map/ppermute | solution.py:34
  35.6 3.1 %collective-permute-start.3 = (bf16[512,512]{1,0:T(8,128)(2,1)}, bf16[512,512]{1,0:T(8,128)(2,1)S(1)}, u32[]{:S(2)}, u32[]{:S(2)}) collective-permute-start(bf16[512,512]{1,0:T(8,128)(2,1)} %get-tuple-element.17.refs_0_), channel_id=1, source_target_pairs={{0,24},{1,385},{2,26},{3,387},{4,28},{5,389},{6,30},{7,391},{8,0},... | collective-permute-start | bytes 1572872 | tf_op jit(solution)/shard_map/ppermute | solution.py:34
  38.6 1.2 fusion.41
  39.9 5.2 %collective-permute-done.4.refs_4_ = bf16[512,512]{1,0:T(8,128)(2,1)S(1)} collective-permute-done((bf16[512,512]{1,0:T(8,128)(2,1)}, bf16[512,512]{1,0:T(8,128)(2,1)S(1)}, u32[]{:S(2)}, u32[]{:S(2)}) %collective-permute-start.4) | collective-permute-done | bytes 524320 | tf_op jit(solution)/shard_map/ppermute | solution.py:34
  45.1 18.9 %collective-permute-done.5.refs_5_ = bf16[512,512]{1,0:T(8,128)(2,1)S(1)} collective-permute-done((bf16[512,512]{1,0:T(8,128)(2,1)}, bf16[512,512]{1,0:T(8,128)(2,1)S(1)}, u32[]{:S(2)}, u32[]{:S(2)}) %collective-permute-start.5) | collective-permute-done | bytes 524320 | tf_op jit(solution)/shard_map/ppermute | solution.py:34
  64.0 1.9 collective-permute-start.6
  65.9 1.9 collective-permute-start.7
  67.9 4.6 %collective-permute-start.8 = (bf16[1024,512]{1,0:T(8,128)(2,1)S(1)}, bf16[1024,512]{1,0:T(8,128)(2,1)S(1)}, u32[]{:S(2)}, u32[]{:S(2)}) collective-permute-start(bf16[1024,512]{1,0:T(8,128)(2,1)S(1)} %constant_dynamic-update-slice_fusion), channel_id=1, source_target_pairs={{0,24},{1,385},{2,26},{3,387},{4,28},{5,389},{6,30},{7,391},{8,0},... | collective-permute-start | bytes 3145736 | tf_op jit(solution)/shard_map/ppermute | solution.py:34
  72.5 1.9 collective-permute-start.18
  74.5 3.1 %collective-permute-start.9 = (bf16[512,512]{1,0:T(8,128)(2,1)S(1)}, bf16[512,512]{1,0:T(8,128)(2,1)S(1)}, u32[]{:S(2)}, u32[]{:S(2)}) collective-permute-start(bf16[512,512]{1,0:T(8,128)(2,1)S(1)} %copy-done.17), channel_id=1, source_target_pairs={{0,4},{1,97},{2,6},{3,99},{4,0},{5,101},{6,2},{7,103},{8,12},{9,10... | collective-permute-start | bytes 1572872 | tf_op jit(solution)/shard_map/ppermute | solution.py:34
  77.7 1.9 collective-permute-start.19
  79.7 4.1 %collective-permute-done.19 = f32[128,128]{0,1:T(8,128)S(1)} collective-permute-done((f32[128,128]{0,1:T(8,128)S(1)}, f32[128,128]{0,1:T(8,128)S(1)}, u32[]{:S(2)}, u32[]{:S(2)}) %collective-permute-start.19) | collective-permute-done | bytes 65568 | tf_op jit(solution)/shard_map/ppermute | solution.py:48
  83.9 1.9 collective-permute-start.20
  85.9 4.8 %collective-permute-done.20 = f32[64,128]{0,1:T(8,128)S(1)} collective-permute-done((f32[64,128]{0,1:T(8,128)S(1)}, f32[64,128]{0,1:T(8,128)S(1)}, u32[]{:S(2)}, u32[]{:S(2)}) %collective-permute-start.20) | collective-permute-done | bytes 32800 | tf_op jit(solution)/shard_map/ppermute | solution.py:48
  90.7 11.3 %collective-permute-start.14 = (bf16[1536,256]{1,0:T(8,128)(2,1)S(1)}, bf16[1536,256]{1,0:T(8,128)(2,1)S(1)}, u32[]{:S(2)}, u32[]{:S(2)}) collective-permute-start(bf16[1536,256]{1,0:T(8,128)(2,1)S(1)} %pad_maximum_fusion.1), channel_id=1, source_target_pairs={{0,1},{1,0},{2,3},{3,2},{4,5},{5,4},{6,7},{7,6},{8,9},{9,8},{10,11... | collective-permute-start | bytes 2359304 | tf_op jit(solution)/shard_map/ppermute | solution.py:48
  102.1 7.0 %collective-permute-start.21 = (f32[64,128]{0,1:T(8,128)S(1)}, f32[64,128]{0,1:T(8,128)S(1)}, u32[]{:S(2)}, u32[]{:S(2)}) collective-permute-start(f32[64,128]{0,1:T(8,128)S(1)} %select_add_fusion.1), channel_id=1, source_target_pairs={{0,2},{2,0},{4,6},{6,4},{8,10},{10,8},{12,14},{14,12},{16,18},{18,... | collective-permute-start | bytes 98312 | tf_op jit(solution)/shard_map/ppermute | solution.py:48
  109.3 3.8 %collective-permute-done.21 = f32[64,128]{0,1:T(8,128)S(1)} collective-permute-done((f32[64,128]{0,1:T(8,128)S(1)}, f32[64,128]{0,1:T(8,128)S(1)}, u32[]{:S(2)}, u32[]{:S(2)}) %collective-permute-start.21) | collective-permute-done | bytes 32800 | tf_op jit(solution)/shard_map/ppermute | solution.py:48
  113.1 13.9 %collective-permute-start.22 = (f32[64,128]{0,1:T(8,128)S(1)}, f32[64,128]{0,1:T(8,128)S(1)}, u32[]{:S(2)}, u32[]{:S(2)}) collective-permute-start(f32[64,128]{0,1:T(8,128)S(1)} %add.95), channel_id=1, source_target_pairs={{0,4},{2,6},{4,0},{6,2},{8,12},{10,14},{12,8},{14,10},{16,20},{18,... | collective-permute-start | bytes 98312 | tf_op jit(solution)/shard_map/ppermute | solution.py:48
  127.1 1.9 collective-permute-done.22
  128.9 5.4 %collective-permute-start.23 = (bf16[64,128]{0,1:T(8,128)(2,1)S(1)}, bf16[64,128]{0,1:T(8,128)(2,1)S(1)}, u32[]{:S(2)}, u32[]{:S(2)}) collective-permute-start(bf16[64,128]{0,1:T(8,128)(2,1)S(1)} %add_convert_fusion.1), channel_id=1, source_target_pairs={{0,16},{2,18},{4,20},{6,22},{8,24},{10,26},{12,28},{14,30},{16,0},... | collective-permute-start | bytes 49160 | tf_op jit(solution)/shard_map/ppermute | solution.py:48
  134.3 1.4 collective-permute-done.23
  135.8 8.4 %collective-permute-start.12 = (bf16[512,512]{1,0:T(8,128)(2,1)S(1)}, bf16[512,512]{1,0:T(8,128)(2,1)S(1)}, u32[]{:S(2)}, u32[]{:S(2)}) collective-permute-start(bf16[512,512]{1,0:T(8,128)(2,1)S(1)} %collective-permute-done.9.refs_9_), channel_id=1, source_target_pairs={{0,24},{1,385},{2,26},{3,387},{4,28},{5,389},{6,30},{7,391},{8,0},... | collective-permute-start | bytes 1572872 | tf_op jit(solution)/shard_map/ppermute | solution.py:34
  144.3 2.1 collective-permute-start.11
  146.6 2.8 %collective-permute-start.10 = (bf16[512,512]{1,0:T(8,128)(2,1)S(1)}, bf16[512,512]{1,0:T(8,128)(2,1)S(1)}, u32[]{:S(2)}, u32[]{:S(2)}) collective-permute-start(bf16[512,512]{1,0:T(8,128)(2,1)S(1)} %collective-permute-done.9.refs_9_), channel_id=1, source_target_pairs={{0,8},{1,129},{2,10},{3,131},{4,12},{5,133},{6,14},{7,135},{8,16},... | collective-permute-start | bytes 1572872 | tf_op jit(solution)/shard_map/ppermute | solution.py:34
  149.5 1.9 collective-permute-start.24
  151.6 4.3 %collective-permute-done.12.refs_12_ = bf16[512,512]{1,0:T(8,128)(2,1)S(1)} collective-permute-done((bf16[512,512]{1,0:T(8,128)(2,1)S(1)}, bf16[512,512]{1,0:T(8,128)(2,1)S(1)}, u32[]{:S(2)}, u32[]{:S(2)}) %collective-permute-start.12) | collective-permute-done | bytes 524320 | tf_op jit(solution)/shard_map/ppermute | solution.py:34
  155.9 1.9 collective-permute-start.15
  158.0 3.7 %collective-permute-done.10.refs_10_ = bf16[512,512]{1,0:T(8,128)(2,1)S(1)} collective-permute-done((bf16[512,512]{1,0:T(8,128)(2,1)S(1)}, bf16[512,512]{1,0:T(8,128)(2,1)S(1)}, u32[]{:S(2)}, u32[]{:S(2)}) %collective-permute-start.10) | collective-permute-done | bytes 524320 | tf_op jit(solution)/shard_map/ppermute | solution.py:34
  161.8 5.0 %collective-permute-start.16 = (bf16[2048,256]{1,0:T(8,128)(2,1)S(1)}, bf16[2048,256]{1,0:T(8,128)(2,1)S(1)}, u32[]{:S(2)}, u32[]{:S(2)}) collective-permute-start(bf16[2048,256]{1,0:T(8,128)(2,1)S(1)} %pad_maximum_fusion), channel_id=1, source_target_pairs={{0,1},{1,0},{2,3},{3,2},{4,5},{5,4},{6,7},{7,6},{8,9},{9,8},{10,11... | collective-permute-start | bytes 3145736 | tf_op jit(solution)/shard_map/ppermute | solution.py:48
  166.9 1.9 collective-permute-start.25
  169.4 0.7 collective-permute-done.25
  170.3 1.1 fusion.40
  171.5 0.8 copy-done.16
  172.8 7.6 %frozen.1 = (f32[512,256]{1,0:T(8,128)}, f32[512,256]{1,0:T(8,128)}) custom-call(s32[1]{0:T(128)} %bitcast.10.core_ref, s32[16]{0:T(128)} %compare_select_fusion.10.order_ref, bf16[512,512]{1,0:T(8,128)(2,1)} %get-tuple-element.17.refs_0_, bf16[512,512]{1,0:T(8,128)(2,1)} %copy-done.6, bf16[512,512]{1,0:T(8,128)(2,1)} %copy-done.7, ...), custom_call_target="tpu_custom_call" | custom-call | tf_op jit(solution)/shard_map/frozen/pallas_call | solution.py:191
  180.4 2.1 collective-permute-start.17
  182.4 2.8 %collective-permute-start.28 = (f32[128,256]{1,0:T(8,128)S(1)}, f32[128,256]{1,0:T(8,128)S(1)}, u32[]{:S(2)}, u32[]{:S(2)}) collective-permute-start(f32[128,256]{1,0:T(8,128)S(1)} %pad_maximum_fusion.4), channel_id=1, source_target_pairs={{0,128},{32,160},{64,192},{96,224},{128,0},{160,32},{192,64},{224,... | collective-permute-start | bytes 393224 | tf_op jit(solution)/shard_map/ppermute | solution.py:48
  185.3 3.6 %collective-permute-done.28 = f32[128,256]{1,0:T(8,128)S(1)} collective-permute-done((f32[128,256]{1,0:T(8,128)S(1)}, f32[128,256]{1,0:T(8,128)S(1)}, u32[]{:S(2)}, u32[]{:S(2)}) %collective-permute-start.28) | collective-permute-done | bytes 131104 | tf_op jit(solution)/shard_map/ppermute | solution.py:48
  188.9 4.6 %collective-permute-start.29 = (f32[128,256]{1,0:T(8,128)S(1)}, f32[128,256]{1,0:T(8,128)S(1)}, u32[]{:S(2)}, u32[]{:S(2)}) collective-permute-start(f32[128,256]{1,0:T(8,128)S(1)} %add.100), channel_id=1, source_target_pairs={{0,256},{32,288},{64,320},{96,352},{128,384},{160,416},{192,448},{... | collective-permute-start | bytes 393224 | tf_op jit(solution)/shard_map/ppermute | solution.py:48
  193.6 2.6 %collective-permute-done.29 = f32[128,256]{1,0:T(8,128)S(1)} collective-permute-done((f32[128,256]{1,0:T(8,128)S(1)}, f32[128,256]{1,0:T(8,128)S(1)}, u32[]{:S(2)}, u32[]{:S(2)}) %collective-permute-start.29) | collective-permute-done | bytes 131104 | tf_op jit(solution)/shard_map/ppermute | solution.py:48
  196.2 12.5 %collective-permute-start.30 = (f32[128,256]{1,0:T(8,128)S(1)}, f32[128,256]{1,0:T(8,128)S(1)}, u32[]{:S(2)}, u32[]{:S(2)}) collective-permute-start(f32[128,256]{1,0:T(8,128)S(1)} %add.101), channel_id=1, source_target_pairs={{0,32},{32,0},{64,96},{96,64},{128,160},{160,128},{192,224},{224,1... | collective-permute-start | bytes 393224 | tf_op jit(solution)/shard_map/ppermute | solution.py:48
  208.9 2.1 collective-permute-done.30
  211.0 1.9 collective-permute-start.31
  213.0 1.1 add_convert_fusion
  215.3 2.1 fusion.2
  218.0 5.3 %collective-permute-start.26 = (f32[512,2,2,32]{0,3,2,1:T(8,128)S(1)}, f32[512,2,2,32]{0,3,2,1:T(8,128)S(1)}, u32[]{:S(2)}, u32[]{:S(2)}) collective-permute-start(f32[512,2,2,32]{0,3,2,1:T(8,128)S(1)} %select_bitcast_fusion), channel_id=1, source_target_pairs={{0,1},{1,0},{2,3},{3,2},{4,5},{5,4},{6,7},{7,6},{8,9},{9,8},{10,11... | collective-permute-start | bytes 786440 | tf_op jit(solution)/shard_map/ppermute | solution.py:48
  223.3 0.9 add_multiply_fusion
  224.2 0.7 fusion.61
  225.0 6.2 %collective-permute-start.27 = (bf16[512,2,32]{0,2,1:T(8,128)(2,1)S(1)}, bf16[512,2,32]{0,2,1:T(8,128)(2,1)S(1)}, u32[]{:S(2)}, u32[]{:S(2)}) collective-permute-start(bf16[512,2,32]{0,2,1:T(8,128)(2,1)S(1)} %fusion.42), channel_id=1, source_target_pairs={{0,2},{2,0},{4,6},{6,4},{8,10},{10,8},{12,14},{14,12},{16,18},{18,... | collective-permute-start | bytes 196616 | tf_op jit(solution)/shard_map/ppermute | solution.py:48
  231.5 0.8 copy.58
  232.3 2.2 collective-permute-done.27
  (114 shorter events, 5.8 us)
Async XLA Ops:
  0.6 12.8 %copy-start = (bf16[1,512,1024]{2,1,0:T(8,128)(2,1)S(1)}, bf16[1,512,1024]{2,1,0:T(8,128)(2,1)}, u32[]{:S(2)}) copy-start(bf16[1,512,1024]{2,1,0:T(8,128)(2,1)} %param.13) | copy-start | bytes 3145732
  2.6 15.1 %collective-permute-start = (bf16[320,512]{1,0:T(8,128)(2,1)}, bf16[320,512]{1,0:T(8,128)(2,1)S(1)}, u32[]{:S(2)}, u32[]{:S(2)}) collective-permute-start(bf16[320,512]{1,0:T(8,128)(2,1)} %pack.1), channel_id=1, source_target_pairs={{0,1},{1,0},{2,3},{3,2},{4,5},{5,4},{6,7},{7,6},{8,9},{9,8},{10,11... | collective-permute-start | bytes 983048 | tf_op jit(solution)/shard_map/ppermute | solution.py:48
  12.5 3.3 %copy-start.14 = (bf16[1,512,256]{1,2,0:T(8,128)(2,1)}, bf16[1,512,256]{1,2,0:T(8,128)(2,1)S(1)}, u32[]{:S(2)}) copy-start(bf16[1,512,256]{1,2,0:T(8,128)(2,1)S(1)} %copy.78) | copy-start | bytes 786436
  17.6 0.7 copy-start.19
  20.5 15.1 %collective-permute-start.13 = (bf16[512,256]{1,0:T(8,128)(2,1)}, bf16[512,256]{1,0:T(8,128)(2,1)}, u32[]{:S(2)}, u32[]{:S(2)}) collective-permute-start(bf16[512,256]{1,0:T(8,128)(2,1)} %get-tuple-element.18), channel_id=1, source_target_pairs={{0,1},{1,0},{2,3},{3,2},{4,5},{5,4},{6,7},{7,6},{8,9},{9,8},{10,11... | collective-permute-start | bytes 786440 | tf_op jit(solution)/shard_map/ppermute | solution.py:48
  23.9 21.2 %collective-permute-start.4 = (bf16[512,512]{1,0:T(8,128)(2,1)}, bf16[512,512]{1,0:T(8,128)(2,1)S(1)}, u32[]{:S(2)}, u32[]{:S(2)}) collective-permute-start(bf16[512,512]{1,0:T(8,128)(2,1)} %get-tuple-element.17.refs_0_), channel_id=1, source_target_pairs={{0,2},{1,33},{2,4},{3,35},{4,6},{5,37},{6,0},{7,39},{8,10},{9,41},... | collective-permute-start | bytes 1572872 | tf_op jit(solution)/shard_map/ppermute | solution.py:34
  25.8 38.2 %collective-permute-start.5 = (bf16[512,512]{1,0:T(8,128)(2,1)}, bf16[512,512]{1,0:T(8,128)(2,1)S(1)}, u32[]{:S(2)}, u32[]{:S(2)}) collective-permute-start(bf16[512,512]{1,0:T(8,128)(2,1)} %get-tuple-element.17.refs_0_), channel_id=1, source_target_pairs={{0,6},{1,65},{2,0},{3,67},{4,2},{5,69},{6,4},{7,71},{8,14},{9,73},... | collective-permute-start | bytes 1572872 | tf_op jit(solution)/shard_map/ppermute | solution.py:34
  28.7 45.8 %copy-start.17 = (bf16[512,512]{1,0:T(8,128)(2,1)S(1)}, bf16[512,512]{1,0:T(8,128)(2,1)}, u32[]{:S(2)}) copy-start(bf16[512,512]{1,0:T(8,128)(2,1)} %get-tuple-element.17.refs_0_) | copy-start | bytes 1572868
  28.7 39.2 %collective-permute-start.1 = (bf16[512,512]{1,0:T(8,128)(2,1)}, bf16[512,512]{1,0:T(8,128)(2,1)S(1)}, u32[]{:S(2)}, u32[]{:S(2)}) collective-permute-start(bf16[512,512]{1,0:T(8,128)(2,1)} %get-tuple-element.17.refs_0_), channel_id=1, source_target_pairs={{0,8},{1,129},{2,10},{3,131},{4,12},{5,133},{6,14},{7,135},{8,16},... | collective-permute-start | bytes 1572872 | tf_op jit(solution)/shard_map/ppermute | solution.py:34
  31.2 41.3 %collective-permute-start.2 = (bf16[512,512]{1,0:T(8,128)(2,1)}, bf16[512,512]{1,0:T(8,128)(2,1)S(1)}, u32[]{:S(2)}, u32[]{:S(2)}) collective-permute-start(bf16[512,512]{1,0:T(8,128)(2,1)} %get-tuple-element.17.refs_0_), channel_id=1, source_target_pairs={{0,16},{1,257},{2,18},{3,259},{4,20},{5,261},{6,22},{7,263},{8,24}... | collective-permute-start | bytes 1572872 | tf_op jit(solution)/shard_map/ppermute | solution.py:34
  35.6 36.9 %collective-permute-start.3 = (bf16[512,512]{1,0:T(8,128)(2,1)}, bf16[512,512]{1,0:T(8,128)(2,1)S(1)}, u32[]{:S(2)}, u32[]{:S(2)}) collective-permute-start(bf16[512,512]{1,0:T(8,128)(2,1)} %get-tuple-element.17.refs_0_), channel_id=1, source_target_pairs={{0,24},{1,385},{2,26},{3,387},{4,28},{5,389},{6,30},{7,391},{8,0},... | collective-permute-start | bytes 1572872 | tf_op jit(solution)/shard_map/ppermute | solution.py:34
  45.0 64.1 %copy-start.1 = (bf16[512,512]{1,0:T(8,128)(2,1)}, bf16[512,512]{1,0:T(8,128)(2,1)S(1)}, u32[]{:S(2)}) copy-start(bf16[512,512]{1,0:T(8,128)(2,1)S(1)} %collective-permute-done.4.refs_4_) | copy-start | bytes 1572868
  64.0 63.0 %copy-start.2 = (bf16[512,512]{1,0:T(8,128)(2,1)}, bf16[512,512]{1,0:T(8,128)(2,1)S(1)}, u32[]{:S(2)}) copy-start(bf16[512,512]{1,0:T(8,128)(2,1)S(1)} %collective-permute-done.5.refs_5_) | copy-start | bytes 1572868
  64.0 80.3 %collective-permute-start.6 = (bf16[1024,512]{1,0:T(8,128)(2,1)S(1)}, bf16[1024,512]{1,0:T(8,128)(2,1)S(1)}, u32[]{:S(2)}, u32[]{:S(2)}) collective-permute-start(bf16[1024,512]{1,0:T(8,128)(2,1)S(1)} %constant_dynamic-update-slice_fusion), channel_id=1, source_target_pairs={{0,8},{1,129},{2,10},{3,131},{4,12},{5,133},{6,14},{7,135},{8,16},... | collective-permute-start | bytes 3145736 | tf_op jit(solution)/shard_map/ppermute | solution.py:34
  65.9 80.7 %collective-permute-start.7 = (bf16[1024,512]{1,0:T(8,128)(2,1)S(1)}, bf16[1024,512]{1,0:T(8,128)(2,1)S(1)}, u32[]{:S(2)}, u32[]{:S(2)}) collective-permute-start(bf16[1024,512]{1,0:T(8,128)(2,1)S(1)} %constant_dynamic-update-slice_fusion), channel_id=1, source_target_pairs={{0,16},{1,257},{2,18},{3,259},{4,20},{5,261},{6,22},{7,263},{8,24}... | collective-permute-start | bytes 3145736 | tf_op jit(solution)/shard_map/ppermute | solution.py:34
  67.9 18.0 %copy-start.6 = (bf16[512,512]{1,0:T(8,128)(2,1)}, bf16[512,512]{1,0:T(8,128)(2,1)S(1)}, u32[]{:S(2)}) copy-start(bf16[512,512]{1,0:T(8,128)(2,1)S(1)} %collective-permute-done.1.refs_1_) | copy-start | bytes 1572868
  67.9 81.6 %collective-permute-start.8 = (bf16[1024,512]{1,0:T(8,128)(2,1)S(1)}, bf16[1024,512]{1,0:T(8,128)(2,1)S(1)}, u32[]{:S(2)}, u32[]{:S(2)}) collective-permute-start(bf16[1024,512]{1,0:T(8,128)(2,1)S(1)} %constant_dynamic-update-slice_fusion), channel_id=1, source_target_pairs={{0,24},{1,385},{2,26},{3,387},{4,28},{5,389},{6,30},{7,391},{8,0},... | collective-permute-start | bytes 3145736 | tf_op jit(solution)/shard_map/ppermute | solution.py:34
  72.5 13.4 %copy-start.7 = (bf16[512,512]{1,0:T(8,128)(2,1)}, bf16[512,512]{1,0:T(8,128)(2,1)S(1)}, u32[]{:S(2)}) copy-start(bf16[512,512]{1,0:T(8,128)(2,1)S(1)} %collective-permute-done.2.refs_2_) | copy-start | bytes 1572868
  72.5 7.2 %copy-start.8 = (bf16[512,512]{1,0:T(8,128)(2,1)}, bf16[512,512]{1,0:T(8,128)(2,1)S(1)}, u32[]{:S(2)}) copy-start(bf16[512,512]{1,0:T(8,128)(2,1)S(1)} %collective-permute-done.3.refs_3_) | copy-start | bytes 1572868
  72.5 5.2 %collective-permute-start.18 = (f32[256,128]{0,1:T(8,128)S(1)}, f32[256,128]{0,1:T(8,128)S(1)}, u32[]{:S(2)}, u32[]{:S(2)}) collective-permute-start(f32[256,128]{0,1:T(8,128)S(1)} %slice_select_fusion.13), channel_id=1, source_target_pairs={{0,1},{1,0},{2,3},{3,2},{4,5},{5,4},{6,7},{7,6},{8,9},{9,8},{10,11... | collective-permute-start | bytes 393224 | tf_op jit(solution)/shard_map/ppermute | solution.py:48
  74.5 27.7 %collective-permute-start.9 = (bf16[512,512]{1,0:T(8,128)(2,1)S(1)}, bf16[512,512]{1,0:T(8,128)(2,1)S(1)}, u32[]{:S(2)}, u32[]{:S(2)}) collective-permute-start(bf16[512,512]{1,0:T(8,128)(2,1)S(1)} %copy-done.17), channel_id=1, source_target_pairs={{0,4},{1,97},{2,6},{3,99},{4,0},{5,101},{6,2},{7,103},{8,12},{9,10... | collective-permute-start | bytes 1572872 | tf_op jit(solution)/shard_map/ppermute | solution.py:34
  77.7 6.1 %collective-permute-start.19 = (f32[128,128]{0,1:T(8,128)S(1)}, f32[128,128]{0,1:T(8,128)S(1)}, u32[]{:S(2)}, u32[]{:S(2)}) collective-permute-start(f32[128,128]{0,1:T(8,128)S(1)} %slice_select_fusion.17), channel_id=1, source_target_pairs={{0,8},{2,10},{4,12},{6,14},{8,0},{10,2},{12,4},{14,6},{16,24},{18,... | collective-permute-start | bytes 196616 | tf_op jit(solution)/shard_map/ppermute | solution.py:48
  83.9 6.8 %collective-permute-start.20 = (f32[64,128]{0,1:T(8,128)S(1)}, f32[64,128]{0,1:T(8,128)S(1)}, u32[]{:S(2)}, u32[]{:S(2)}) collective-permute-start(f32[64,128]{0,1:T(8,128)S(1)} %slice_select_fusion.16), channel_id=1, source_target_pairs={{0,16},{2,18},{4,20},{6,22},{8,24},{10,26},{12,28},{14,30},{16,0},... | collective-permute-start | bytes 98312 | tf_op jit(solution)/shard_map/ppermute | solution.py:48
  90.7 80.7 %collective-permute-start.14 = (bf16[1536,256]{1,0:T(8,128)(2,1)S(1)}, bf16[1536,256]{1,0:T(8,128)(2,1)S(1)}, u32[]{:S(2)}, u32[]{:S(2)}) collective-permute-start(bf16[1536,256]{1,0:T(8,128)(2,1)S(1)} %pad_maximum_fusion.1), channel_id=1, source_target_pairs={{0,1},{1,0},{2,3},{3,2},{4,5},{5,4},{6,7},{7,6},{8,9},{9,8},{10,11... | collective-permute-start | bytes 2359304 | tf_op jit(solution)/shard_map/ppermute | solution.py:48
  102.1 44.5 %copy-start.9 = (bf16[512,512]{1,0:T(8,128)(2,1)}, bf16[512,512]{1,0:T(8,128)(2,1)S(1)}, u32[]{:S(2)}) copy-start(bf16[512,512]{1,0:T(8,128)(2,1)S(1)} %collective-permute-done.9.refs_9_) | copy-start | bytes 1572868
  102.1 10.9 %collective-permute-start.21 = (f32[64,128]{0,1:T(8,128)S(1)}, f32[64,128]{0,1:T(8,128)S(1)}, u32[]{:S(2)}, u32[]{:S(2)}) collective-permute-start(f32[64,128]{0,1:T(8,128)S(1)} %select_add_fusion.1), channel_id=1, source_target_pairs={{0,2},{2,0},{4,6},{6,4},{8,10},{10,8},{12,14},{14,12},{16,18},{18,... | collective-permute-start | bytes 98312 | tf_op jit(solution)/shard_map/ppermute | solution.py:48
  113.1 15.8 %collective-permute-start.22 = (f32[64,128]{0,1:T(8,128)S(1)}, f32[64,128]{0,1:T(8,128)S(1)}, u32[]{:S(2)}, u32[]{:S(2)}) collective-permute-start(f32[64,128]{0,1:T(8,128)S(1)} %add.95), channel_id=1, source_target_pairs={{0,4},{2,6},{4,0},{6,2},{8,12},{10,14},{12,8},{14,10},{16,20},{18,... | collective-permute-start | bytes 98312 | tf_op jit(solution)/shard_map/ppermute | solution.py:48
  128.9 6.8 %collective-permute-start.23 = (bf16[64,128]{0,1:T(8,128)(2,1)S(1)}, bf16[64,128]{0,1:T(8,128)(2,1)S(1)}, u32[]{:S(2)}, u32[]{:S(2)}) collective-permute-start(bf16[64,128]{0,1:T(8,128)(2,1)S(1)} %add_convert_fusion.1), channel_id=1, source_target_pairs={{0,16},{2,18},{4,20},{6,22},{8,24},{10,26},{12,28},{14,30},{16,0},... | collective-permute-start | bytes 49160 | tf_op jit(solution)/shard_map/ppermute | solution.py:48
  135.8 20.1 %collective-permute-start.12 = (bf16[512,512]{1,0:T(8,128)(2,1)S(1)}, bf16[512,512]{1,0:T(8,128)(2,1)S(1)}, u32[]{:S(2)}, u32[]{:S(2)}) collective-permute-start(bf16[512,512]{1,0:T(8,128)(2,1)S(1)} %collective-permute-done.9.refs_9_), channel_id=1, source_target_pairs={{0,24},{1,385},{2,26},{3,387},{4,28},{5,389},{6,30},{7,391},{8,0},... | collective-permute-start | bytes 1572872 | tf_op jit(solution)/shard_map/ppermute | solution.py:34
  144.3 7.3 %copy-start.3 = (bf16[1024,512]{1,0:T(8,128)(2,1)}, bf16[1024,512]{1,0:T(8,128)(2,1)S(1)}, u32[]{:S(2)}) copy-start(bf16[1024,512]{1,0:T(8,128)(2,1)S(1)} %collective-permute-done.6.refs_6_) | copy-start | bytes 3145732
  144.3 13.6 %collective-permute-start.11 = (bf16[512,512]{1,0:T(8,128)(2,1)S(1)}, bf16[512,512]{1,0:T(8,128)(2,1)S(1)}, u32[]{:S(2)}, u32[]{:S(2)}) collective-permute-start(bf16[512,512]{1,0:T(8,128)(2,1)S(1)} %collective-permute-done.9.refs_9_), channel_id=1, source_target_pairs={{0,16},{1,257},{2,18},{3,259},{4,20},{5,261},{6,22},{7,263},{8,24}... | collective-permute-start | bytes 1572872 | tf_op jit(solution)/shard_map/ppermute | solution.py:34
  146.6 11.4 %copy-start.4 = (bf16[1024,512]{1,0:T(8,128)(2,1)}, bf16[1024,512]{1,0:T(8,128)(2,1)S(1)}, u32[]{:S(2)}) copy-start(bf16[1024,512]{1,0:T(8,128)(2,1)S(1)} %collective-permute-done.7.refs_7_) | copy-start | bytes 3145732
  146.6 15.0 %collective-permute-start.10 = (bf16[512,512]{1,0:T(8,128)(2,1)S(1)}, bf16[512,512]{1,0:T(8,128)(2,1)S(1)}, u32[]{:S(2)}, u32[]{:S(2)}) collective-permute-start(bf16[512,512]{1,0:T(8,128)(2,1)S(1)} %collective-permute-done.9.refs_9_), channel_id=1, source_target_pairs={{0,8},{1,129},{2,10},{3,131},{4,12},{5,133},{6,14},{7,135},{8,16},... | collective-permute-start | bytes 1572872 | tf_op jit(solution)/shard_map/ppermute | solution.py:34
  149.5 12.2 %copy-start.5 = (bf16[1024,512]{1,0:T(8,128)(2,1)}, bf16[1024,512]{1,0:T(8,128)(2,1)S(1)}, u32[]{:S(2)}) copy-start(bf16[1024,512]{1,0:T(8,128)(2,1)S(1)} %collective-permute-done.8.refs_8_) | copy-start | bytes 3145732
  149.5 17.2 %collective-permute-start.24 = (bf16[128,128]{0,1:T(8,128)(2,1)S(1)}, bf16[128,128]{0,1:T(8,128)(2,1)S(1)}, u32[]{:S(2)}, u32[]{:S(2)}) collective-permute-start(bf16[128,128]{0,1:T(8,128)(2,1)S(1)} %pad_maximum_fusion.8), channel_id=1, source_target_pairs={{0,8},{2,10},{4,12},{6,14},{8,0},{10,2},{12,4},{14,6},{16,24},{18,... | collective-permute-start | bytes 98312 | tf_op jit(solution)/shard_map/ppermute | solution.py:48
  155.9 5.9 %copy-start.10 = (bf16[512,512]{1,0:T(8,128)(2,1)}, bf16[512,512]{1,0:T(8,128)(2,1)S(1)}, u32[]{:S(2)}) copy-start(bf16[512,512]{1,0:T(8,128)(2,1)S(1)} %collective-permute-done.12.refs_12_) | copy-start | bytes 1572868
  155.9 15.6 %collective-permute-start.15 = (bf16[4096,256]{1,0:T(8,128)(2,1)S(1)}, bf16[4096,256]{1,0:T(8,128)(2,1)}, u32[]{:S(2)}, u32[]{:S(2)}) collective-permute-start(bf16[4096,256]{1,0:T(8,128)(2,1)S(1)} %fusion.12), channel_id=1, source_target_pairs={{0,1},{1,0},{2,3},{3,2},{4,5},{5,4},{6,7},{7,6},{8,9},{9,8},{10,11... | collective-permute-start | bytes 6291464 | tf_op jit(solution)/shard_map/ppermute | solution.py:48
  157.9 11.0 %copy-start.21 = (s32[16]{0:T(128)S(1)}, s32[16]{0:T(128)}, u32[]{:S(2)}) copy-start(s32[16]{0:T(128)} %constant.117.clone) | copy-start | bytes 196
  157.9 11.0 %copy-start.22 = (s32[16]{0:T(128)S(1)}, s32[16]{0:T(128)}, u32[]{:S(2)}) copy-start(s32[16]{0:T(128)} %constant.130) | copy-start | bytes 196
  157.9 11.0 %copy-start.23 = (s32[16]{0:T(128)S(1)}, s32[16]{0:T(128)}, u32[]{:S(2)}) copy-start(s32[16]{0:T(128)} %constant.131) | copy-start | bytes 196
  157.9 12.2 %copy-start.11 = (bf16[512,512]{1,0:T(8,128)(2,1)}, bf16[512,512]{1,0:T(8,128)(2,1)S(1)}, u32[]{:S(2)}) copy-start(bf16[512,512]{1,0:T(8,128)(2,1)S(1)} %collective-permute-done.11.refs_11_) | copy-start | bytes 1572868
  161.7 9.8 %copy-start.12 = (bf16[512,512]{1,0:T(8,128)(2,1)}, bf16[512,512]{1,0:T(8,128)(2,1)S(1)}, u32[]{:S(2)}) copy-start(bf16[512,512]{1,0:T(8,128)(2,1)S(1)} %collective-permute-done.10.refs_10_) | copy-start | bytes 1572868
  161.8 9.7 %collective-permute-start.16 = (bf16[2048,256]{1,0:T(8,128)(2,1)S(1)}, bf16[2048,256]{1,0:T(8,128)(2,1)S(1)}, u32[]{:S(2)}, u32[]{:S(2)}) collective-permute-start(bf16[2048,256]{1,0:T(8,128)(2,1)S(1)} %pad_maximum_fusion), channel_id=1, source_target_pairs={{0,1},{1,0},{2,3},{3,2},{4,5},{5,4},{6,7},{7,6},{8,9},{9,8},{10,11... | collective-permute-start | bytes 3145736 | tf_op jit(solution)/shard_map/ppermute | solution.py:48
  166.9 3.1 %collective-permute-start.25 = (bf16[256,128]{0,1:T(8,128)(2,1)S(1)}, bf16[256,128]{0,1:T(8,128)(2,1)S(1)}, u32[]{:S(2)}, u32[]{:S(2)}) collective-permute-start(bf16[256,128]{0,1:T(8,128)(2,1)S(1)} %pad_maximum_fusion.7), channel_id=1, source_target_pairs={{0,1},{1,0},{2,3},{3,2},{4,5},{5,4},{6,7},{7,6},{8,9},{9,8},{10,11... | collective-permute-start | bytes 196616 | tf_op jit(solution)/shard_map/ppermute | solution.py:48
  171.4 37.2 %copy-start.20 = (bf16[256,64]{0,1:T(8,128)(2,1)S(1)}, bf16[256,64]{0,1:T(8,128)(2,1)}, u32[]{:S(2)}) copy-start(bf16[256,64]{0,1:T(8,128)(2,1)} %param.20) | copy-start | bytes 98308
  171.5 0.9 copy-start.16
  171.5 1.3 copy-start.13
  180.3 32.6 %copy-start.18 = (f32[512,256]{1,0:T(8,128)S(1)}, f32[512,256]{1,0:T(8,128)}, u32[]{:S(2)}) copy-start(f32[512,256]{1,0:T(8,128)} %get-tuple-element.21) | copy-start | bytes 1572868
  180.4 32.6 %collective-permute-start.17 = (f32[512,256]{1,0:T(8,128)}, f32[512,256]{1,0:T(8,128)}, u32[]{:S(2)}, u32[]{:S(2)}) collective-permute-start(f32[512,256]{1,0:T(8,128)} %get-tuple-element.22), channel_id=1, source_target_pairs={{0,1},{1,0},{2,3},{3,2},{4,5},{5,4},{6,7},{7,6},{8,9},{9,8},{10,11... | collective-permute-start | bytes 1572872 | tf_op jit(solution)/shard_map/ppermute | solution.py:48
  182.4 6.5 %collective-permute-start.28 = (f32[128,256]{1,0:T(8,128)S(1)}, f32[128,256]{1,0:T(8,128)S(1)}, u32[]{:S(2)}, u32[]{:S(2)}) collective-permute-start(f32[128,256]{1,0:T(8,128)S(1)} %pad_maximum_fusion.4), channel_id=1, source_target_pairs={{0,128},{32,160},{64,192},{96,224},{128,0},{160,32},{192,64},{224,... | collective-permute-start | bytes 393224 | tf_op jit(solution)/shard_map/ppermute | solution.py:48
  188.9 7.2 %collective-permute-start.29 = (f32[128,256]{1,0:T(8,128)S(1)}, f32[128,256]{1,0:T(8,128)S(1)}, u32[]{:S(2)}, u32[]{:S(2)}) collective-permute-start(f32[128,256]{1,0:T(8,128)S(1)} %add.100), channel_id=1, source_target_pairs={{0,256},{32,288},{64,320},{96,352},{128,384},{160,416},{192,448},{... | collective-permute-start | bytes 393224 | tf_op jit(solution)/shard_map/ppermute | solution.py:48
  196.2 14.9 %collective-permute-start.30 = (f32[128,256]{1,0:T(8,128)S(1)}, f32[128,256]{1,0:T(8,128)S(1)}, u32[]{:S(2)}, u32[]{:S(2)}) collective-permute-start(f32[128,256]{1,0:T(8,128)S(1)} %add.101), channel_id=1, source_target_pairs={{0,32},{32,0},{64,96},{96,64},{128,160},{160,128},{192,224},{224,1... | collective-permute-start | bytes 393224 | tf_op jit(solution)/shard_map/ppermute | solution.py:48
  211.0 12.3 %collective-permute-start.31 = (f32[128,256]{1,0:T(8,128)S(1)}, f32[128,256]{1,0:T(8,128)}, u32[]{:S(2)}, u32[]{:S(2)}) collective-permute-start(f32[128,256]{1,0:T(8,128)S(1)} %add.102), channel_id=1, source_target_pairs={{0,64},{32,96},{64,0},{96,32},{128,192},{160,224},{192,128},{224,1... | collective-permute-start | bytes 393224 | tf_op jit(solution)/shard_map/ppermute | solution.py:48
  215.3 2.2 copy-start.15
  218.0 6.9 %collective-permute-start.26 = (f32[512,2,2,32]{0,3,2,1:T(8,128)S(1)}, f32[512,2,2,32]{0,3,2,1:T(8,128)S(1)}, u32[]{:S(2)}, u32[]{:S(2)}) collective-permute-start(f32[512,2,2,32]{0,3,2,1:T(8,128)S(1)} %select_bitcast_fusion), channel_id=1, source_target_pairs={{0,1},{1,0},{2,3},{3,2},{4,5},{5,4},{6,7},{7,6},{8,9},{9,8},{10,11... | collective-permute-start | bytes 786440 | tf_op jit(solution)/shard_map/ppermute | solution.py:48
  225.0 9.5 %collective-permute-start.27 = (bf16[512,2,32]{0,2,1:T(8,128)(2,1)S(1)}, bf16[512,2,32]{0,2,1:T(8,128)(2,1)S(1)}, u32[]{:S(2)}, u32[]{:S(2)}) collective-permute-start(bf16[512,2,32]{0,2,1:T(8,128)(2,1)S(1)} %fusion.42), channel_id=1, source_target_pairs={{0,2},{2,0},{4,6},{6,4},{8,10},{10,8},{12,14},{14,12},{16,18},{18,... | collective-permute-start | bytes 196616 | tf_op jit(solution)/shard_map/ppermute | solution.py:48

commit v3 on v2

v3 whole, which is shorter than its diff:
```python
import functools

import jax
import jax.numpy as jnp
from jax import lax
from jax.experimental import pallas as pl
from jax.experimental.pallas import tpu as pltpu
from jax.sharding import PartitionSpec as P

QUERY_HEAD_COUNT = 64
KVH = 8
HEAD_WIDTH = 128
SIDE = 4
SEGMENT_MOST = 128
JOIN_WEIGHT = 96 << 20

adapter_scale = 2.0

F32, BF16 = jnp.float32, jnp.bfloat16
NT = (((1,), (1,)), ((), ()))
TN = (((0,), (0,)), ((), ()))


AXES = ("dp", "tensor", "draft")


def moved(array, residual_to, slab_to):
    n_dp, n_tensor = lax.axis_size("dp"), lax.axis_size("tensor")
    pairs = []
    for d in range(n_dp):
        for t in range(n_tensor):
            at = (d * n_tensor + t) * 2
            pairs.append((at, (d * n_tensor + residual_to(t)) * 2))
            pairs.append((at + 1, (slab_to(d) * n_tensor + t) * 2 + 1))
    return lax.ppermute(array, AXES, pairs)


def spread(stacked, axes, groups):
    return lax.all_to_all(stacked, axes, 0, 0, axis_index_groups=groups, tiled=True)


def high_groups():
    return [[i * SIDE + j for i in range(SIDE)] for j in range(SIDE)]


def far_groups():
    n_dp, n_tensor = lax.axis_size("dp"), lax.axis_size("tensor")
    groups = []
    for one in high_groups():
        groups += [[(d * n_tensor + t) * 2 for t in one] for d in range(n_dp)]
        groups += [[(d * n_tensor + t) * 2 + 1 for d in one] for t in range(n_tensor)]
    return groups


def far_move(array, k):
    step = lambda i: (i + k * SIDE) % (SIDE * SIDE)
    return moved(array, step, step)


def near_move(array, shift, mask):
    ahead = lambda t: t // SIDE * SIDE + (t + shift) % SIDE
    return moved(array, ahead, lambda d: d ^ mask)


def first_swapped(array, mask):
    n = lax.axis_size("dp") * lax.axis_size("tensor")
    return lax.ppermute(array, AXES, [(2 * i, 2 * (i ^ mask)) for i in range(n)])


def swapped(array, axis, mask):
    return lax.ppermute(array, axis, [(i, i ^ mask) for i in range(lax.axis_size(axis))])


def after(array, *earlier):
    return lax.optimization_barrier((array, *earlier))[0]


def blend_kernel(
    place_ref, tapped_ref, rows_ref, taps_ref, upper_ref, slab_ref, came_ref, inner_ref,
    block_ref, sums_ref, stack_ref,
):
    n, n_taps, rank = rows_ref.shape[0], taps_ref.shape[0], upper_ref.shape[0]
    width = upper_ref.shape[1]
    at_upper = n + n_taps
    at_inner = at_upper + rank // 2

    @pl.when(place_ref[0] == 0)
    def _():
        taps = jnp.concatenate([taps_ref[...], came_ref[n:at_upper]], axis=0)
        place = lax.broadcasted_iota(jnp.int32, (2 * n, 2 * n_taps), 0)
        hit = jnp.where(place == tapped_ref[...], 1.0, 0.0).astype(BF16)
        spread = jnp.dot(hit, taps, preferred_element_type=F32)
        block_ref[:n] = (rows_ref[...].astype(F32) + spread[:n]).astype(BF16)
        block_ref[n:] = (came_ref[:n].astype(F32) + spread[n:]).astype(BF16)
        upper = came_ref[at_upper:at_inner]
        upper = jnp.concatenate([upper[:, :width], upper[:, width:]], axis=0)
        lora = lax.dot_general(
            block_ref[:, :width], upper_ref[...], NT, preferred_element_type=F32
        ) + lax.dot_general(block_ref[:, width:], upper, NT, preferred_element_type=F32)
        inner = came_ref[at_inner:].astype(F32)
        inner = [inner[:, i * rank : (i + 1) * rank] for i in range(inner.shape[1] // rank)]
        inner = inner_ref[...] + jnp.concatenate(inner, axis=0)
        sums_ref[...] = jnp.concatenate([inner, lora], axis=1)

    @pl.when(place_ref[0] == 1)
    def _():
        block_ref[:n] = came_ref[:n]
        block_ref[n:] = slab_ref[...]
        sums_ref[...] = jnp.zeros_like(sums_ref)

    quarter = 2 * n // SIDE
    step = stack_ref.shape[0] // SIDE
    for i in range(SIDE):
        at = i * step
        stack_ref[at : at + 2 * n] = block_ref[...]
        share = sums_ref[i * quarter : (i + 1) * quarter].astype(BF16)
        stack_ref[at + 2 * n : at + step] = jnp.concatenate(
            jnp.split(share, SIDE, axis=0), axis=1
        )


def blend(place, tapped, rows, taps, upper, slab, came, inner):
    n, width = rows.shape
    ride = 2 * n // SIDE * 2 * upper.shape[0] // width
    vmem = pl.BlockSpec(memory_space=pltpu.VMEM)
    return pl.pallas_call(
        blend_kernel,
        out_shape=(
            jax.ShapeDtypeStruct((2 * n, width), BF16),
            jax.ShapeDtypeStruct((2 * n, 2 * upper.shape[0]), F32),
            jax.ShapeDtypeStruct((SIDE * (2 * n + ride), width), BF16),
        ),
        in_specs=[pl.BlockSpec(memory_space=pltpu.SMEM)] + [vmem] * 7,
        out_specs=(vmem,) * 3,
        name="blend",
    )(place, tapped, rows, taps, upper, slab, came, inner)


def widened(array, n):
    return jnp.concatenate(jnp.split(array, n, axis=0), axis=1)


def narrowed(array, n):
    return jnp.concatenate(jnp.split(array, n, axis=1), axis=0)


def joined_kernel(low_ref, high_ref, out_ref):
    n = low_ref.shape[0]
    out_ref[:n] = low_ref[...]
    out_ref[n:] = high_ref[...]


def joined(low, high):
    n, width = low.shape
    vmem = pl.BlockSpec(memory_space=pltpu.VMEM)
    return pl.pallas_call(
        joined_kernel,
        out_shape=jax.ShapeDtypeStruct((2 * n, width), BF16),
        in_specs=[vmem] * 2,
        out_specs=vmem,
        cost_estimate=pl.CostEstimate(flops=0, bytes_accessed=JOIN_WEIGHT, transcendentals=0),
        name="joined",
    )(low, high)


def ride_sum_kernel(rows, stack_ref, out_ref, rides, sems):
    n_ride = rides.shape[1]
    copies = []
    for i in range(SIDE):
        ride = stack_ref.at[pl.ds(i * (rows + n_ride) + rows, n_ride)]
        copies.append(pltpu.make_async_copy(ride, rides.at[i], sems.at[i]))
        copies[-1].start()
    for copy in copies:
        copy.wait()
    total = rides[0].astype(F32)
    for i in range(1, SIDE):
        total = total + rides[i].astype(F32)
    out_ref[...] = jnp.concatenate(jnp.split(total.astype(BF16), SIDE, axis=1), axis=0)


def ride_sum(stack, rows):
    n_ride, width = stack.shape[0] // SIDE - rows, stack.shape[1]
    return pl.pallas_call(
        functools.partial(ride_sum_kernel, rows),
        out_shape=jax.ShapeDtypeStruct((n_ride * SIDE, width // SIDE), BF16),
        in_specs=[pl.BlockSpec(memory_space=pl.ANY)],
        out_specs=pl.BlockSpec(memory_space=pltpu.VMEM),
        scratch_shapes=[
            pltpu.VMEM((SIDE, n_ride, width), BF16),
            pltpu.SemaphoreType.DMA((SIDE,)),
        ],
        name="ride_sum",
    )(stack)


def give_copies(parts, other, sources, out_ref, sems):
    width = out_ref.shape[1]
    columns = pl.ds(pl.multiple_of(other * width, width), width)
    copies, at = [], 0
    for i, (which, row, n) in enumerate(parts):
        source = sources[which].at[pl.ds(row, n), columns]
        copies.append(pltpu.make_async_copy(source, out_ref.at[pl.ds(at, n)], sems.at[i]))
        copies[-1].start()
        at += n
    return copies


def give_kernel(parts, core_ref, *refs):
    sources, (out_ref, sems) = refs[:-2], refs[-2:]
    for copy in give_copies(parts, 1 - core_ref[0], sources, out_ref, sems):
        copy.wait()


def give_half(core, arrays, rows):
    any_spec = pl.BlockSpec(memory_space=pl.ANY)
    parts = [(i, at, rows) for i, a in enumerate(arrays) for at in range(0, a.shape[0], rows)]
    return pl.pallas_call(
        functools.partial(give_kernel, parts),
        out_shape=jax.ShapeDtypeStruct((len(parts) * rows, arrays[0].shape[1] // 2), BF16),
        in_specs=[pl.BlockSpec(memory_space=pltpu.SMEM)] + [any_spec] * len(arrays),
        out_specs=pl.BlockSpec(memory_space=pltpu.VMEM),
        scratch_shapes=[pltpu.SemaphoreType.DMA((len(parts),))],
        name="give",
    )(core, *arrays)


def give_near_kernel(parts, at_ride, place_ref, quarter_ref, *refs):
    sources, (out_ref, sums_ref, rides, sems) = refs[:-4], refs[-4:]
    copies = give_copies(parts, 1 - place_ref[0], sources, out_ref, sems)
    for k, far in enumerate(sources[-3:]):
        ride = far.at[pl.ds(at_ride, rides.shape[1])]
        copies.append(pltpu.make_async_copy(ride, rides.at[k], sems.at[len(parts) + k]))
        copies[-1].start()
    n = quarter_ref.shape[0]
    sums_ref[pl.ds(pl.multiple_of(place_ref[1] * n, n), n)] = quarter_ref[...]
    for copy in copies:
        copy.wait()
    for k in range(3):
        source = (place_ref[1] + SIDE - 1 - k) % SIDE
        ride = jnp.concatenate(jnp.split(rides[k], SIDE, axis=1), axis=0)
        sums_ref[pl.ds(pl.multiple_of(source * n, n), n)] = ride
    at = sum(part[2] for part in parts)
    out_ref[at:] = jnp.concatenate(jnp.split(sums_ref[...], 2, axis=0), axis=1)


def give_near(place, quarter, arrays, steps, rows):
    width = arrays[0].shape[1]
    at_ride = arrays[-1].shape[0] // rows * rows
    n_ride = arrays[-1].shape[0] - at_ride
    n, columns = quarter.shape
    parts = [
        (i, at, rows)
        for i, (a, step) in enumerate(zip(arrays, steps))
        for at in range(0, a.shape[0] - rows + 1, step)
    ]
    vmem, any_spec = pl.BlockSpec(memory_space=pltpu.VMEM), pl.BlockSpec(memory_space=pl.ANY)
    n_sums = SIDE * n * columns * 2 // width
    return pl.pallas_call(
        functools.partial(give_near_kernel, parts, at_ride),
        out_shape=(
            jax.ShapeDtypeStruct((len(parts) * rows + n_sums, width // 2), BF16),
            jax.ShapeDtypeStruct((SIDE * n, columns), BF16),
        ),
        in_specs=[pl.BlockSpec(memory_space=pltpu.SMEM), vmem] + [any_spec] * len(arrays),
        out_specs=(vmem,) * 2,
        scratch_shapes=[
            pltpu.VMEM((3, n_ride, width), BF16),
            pltpu.SemaphoreType.DMA((len(parts) + 3,)),
        ],
        name="give_near",
    )(place, quarter, *arrays)


def frozen_kernel(n_held, parts, core_ref, order_ref, *refs):
    sources, (mine, other, own, came, sems) = refs[:-5], refs[-5:]
    rows, cols = mine.shape
    width = own.shape[1]
    blocks = own.shape[0] // rows
    columns = pl.ds(pl.multiple_of(core_ref[0] * width, width), width)
    copies, at = [], 0
    for i, (which, row) in enumerate(parts):
        target = (own if i < blocks else came).at[pl.ds(i % blocks * rows, rows)]
        source = sources[which].at[pl.ds(row, rows), columns if which < n_held else pl.ds(0, width)]
        copies.append(pltpu.make_async_copy(source, target, sems.at[i]))
    for copy in copies[blocks:] + copies[:blocks]:
        copy.start()
    for copy in copies[blocks:]:
        copy.wait()

    def matched(i):
        return came[pl.ds(pl.multiple_of(order_ref[i] * rows, rows), rows)]

    def held(i):
        copies[i].wait()
        return own[i * rows : (i + 1) * rows]

    def product(left, right):
        return lax.dot_general(left, right, NT, preferred_element_type=F32)

    @pl.when(core_ref[0] == 0)
    def _():
        total = product(held(0), matched(0))
        for i in range(1, blocks):
            total = total + product(held(i), matched(i))
        mine[...] = total[:, :cols]
        other[...] = total[:, cols:]

    @pl.when(core_ref[0] == 1)
    def _():
        total = product(matched(0), held(0))
        for i in range(1, blocks):
            total = total + product(matched(i), held(i))
        mine[...] = total[:, cols:]
        other[...] = total[:, :cols]


def frozen_product(core, order, own, came, rows):
    arrays = [a for a, _ in (*own, *came)]
    parts = []
    for i, (a, step) in enumerate((*own, *came)):
        parts += [(i, at) for at in range(0, a.shape[0] - rows + 1, step)]
    width = came[0][0].shape[1]
    held = pltpu.VMEM((len(parts) // 2 * rows, width), BF16)
    return pl.pallas_call(
        functools.partial(frozen_kernel, len(own), parts),
        out_shape=(jax.ShapeDtypeStruct((rows, rows // 2), F32),) * 2,
        in_specs=[pl.BlockSpec(memory_space=pltpu.SMEM)] * 2
        + [pl.BlockSpec(memory_space=pl.ANY)] * len(arrays),
        out_specs=(pl.BlockSpec(memory_space=pltpu.VMEM),) * 2,
        scratch_shapes=[held, held, pltpu.SemaphoreType.DMA((len(parts),))],
        compiler_params=pltpu.CompilerParams(vmem_limit_bytes=56 * 1024 * 1024),
        cost_estimate=pl.CostEstimate(
            flops=4 * rows * held.shape[0] * width, bytes_accessed=24 << 20, transcendentals=0
        ),
        name="frozen",
    )(core, order, *arrays)


def block_order(core, dp, tensor):
    stage = jnp.array([0] * 4 + [1, 2] * 4 + [3] * 4, jnp.int32)
    step = jnp.array([0, 1, 2, 3, 0, 0, 1, 1, 2, 2, 3, 3, 0, 1, 2, 3], jnp.int32)
    first = core == 0
    mine, theirs = jnp.where(first, tensor, dp) // SIDE, jnp.where(first, dp, tensor) // SIDE
    high = jnp.where(stage == 0, step, (mine - step) % SIDE)
    shift = jnp.where(stage == 2, 3, jnp.where(stage == 3, 2, stage))
    low = jnp.where(first, (tensor - shift) % SIDE, (dp % SIDE) ^ stage)
    back = (tensor - low) % SIDE
    back = jnp.where(back == 2, 3, jnp.where(back == 3, 2, back))
    stage = jnp.where(first, (dp % SIDE) ^ low, back)
    step = (theirs - high) % SIDE
    return jnp.where(
        stage == 0, high, jnp.where(stage == 3, 12 + step, 3 + stage + 2 * step)
    )


def window(i, rows):
    return max(i - 1, 0) * rows


def forward_kernel(
    scale, place_ref, q_ref, label_ref, lower_ref, keys_ref, values_ref, rows_ref, taps_ref,
    upper_ref, slab_ref, band_ref, out_ref, inner_ref, k_ref, v_ref, give_ref, sems,
):
    head = k_ref.shape[1]
    n, n_taps, (rank, width) = rows_ref.shape[0], taps_ref.shape[0], upper_ref.shape
    at_upper = n + n_taps
    at_inner = at_upper + rank // 2
    mine = pl.ds(pl.multiple_of(place_ref[2] * head, head), head)

    def copy(i, source, target):
        return pltpu.make_async_copy(source, target, sems.at[i])

    seen = [copy(0, keys_ref.at[:, mine], k_ref), copy(1, values_ref.at[:, mine], v_ref)]
    given = [copy(2, taps_ref, give_ref.at[pl.ds(n, n_taps)])]
    for i in range(2):
        target = give_ref.at[pl.ds(at_upper, rank // 2), pl.ds(i * width, width)]
        given.append(copy(3 + i, upper_ref.at[pl.ds(i * (rank // 2), rank // 2)], target))
    for one in seen + given:
        one.start()

    @pl.when(place_ref[0] == 0)
    def _():
        copy(5, slab_ref, give_ref.at[pl.ds(0, n)]).start()

    @pl.when(place_ref[0] == 1)
    def _():
        copy(5, rows_ref, give_ref.at[pl.ds(0, n)]).start()

    for one in seen:
        one.wait()
    rows = band_ref.shape[2] // 2
    labels = label_ref[...].astype(F32)
    ahead = lax.broadcasted_iota(jnp.int32, (rows, 2 * rows), 0)
    ahead = ahead - lax.broadcasted_iota(jnp.int32, (rows, 2 * rows), 1)
    for i in range(q_ref.shape[0] // rows):
        at, low = i * rows, window(i, rows)
        own = jnp.broadcast_to(labels[:, at : at + rows], (rows, rows)).T
        own = jnp.concatenate([own, own], axis=1)
        allowed = (ahead >= low - at) & (own == labels[:, low : low + 2 * rows])
        for h in range(band_ref.shape[0]):
            cols = slice(h * head, (h + 1) * head)
            scores = lax.dot_general(
                q_ref[at : at + rows, cols],
                k_ref[low : low + 2 * rows],
                NT,
                preferred_element_type=F32,
            )
            scores = jnp.where(allowed, scores * scale, -jnp.inf)
            probs = jnp.exp(scores - jnp.max(scores, axis=1, keepdims=True))
            probs = probs / jnp.sum(probs, axis=1, keepdims=True)
            band_ref[h, at : at + rows] = probs
            out_ref[at : at + rows, cols] = jnp.dot(
                probs.astype(BF16), v_ref[low : low + 2 * rows], preferred_element_type=F32
            ).astype(BF16)
    inner = lax.dot_general(out_ref[...], lower_ref[...], NT, preferred_element_type=F32)
    inner_ref[...] = inner
    inner = jnp.split(inner.astype(BF16), 2 * width // rank, axis=0)
    give_ref[at_inner:] = jnp.concatenate(inner, axis=1)
    for one in given:
        one.wait()
    copy(5, rows_ref, give_ref.at[pl.ds(0, n)]).wait()


def forward(place, queries, labels, lower, keys, values, rows, taps, upper, slab):
    n, width = queries.shape
    heads, rank = width // HEAD_WIDTH, lower.shape[0]
    any_spec = pl.BlockSpec(memory_space=pl.ANY)
    vmem = pl.BlockSpec(memory_space=pltpu.VMEM)
    n_give = rows.shape[0] + taps.shape[0] + rank // 2 + n * rank // rows.shape[1]
    return pl.pallas_call(
        functools.partial(forward_kernel, HEAD_WIDTH**-0.5),
        out_shape=(
            jax.ShapeDtypeStruct((heads, n, 2 * SEGMENT_MOST), F32),
            jax.ShapeDtypeStruct((n, width), BF16),
            jax.ShapeDtypeStruct((n, rank), F32),
            jax.ShapeDtypeStruct((n, HEAD_WIDTH), BF16),
            jax.ShapeDtypeStruct((n, HEAD_WIDTH), BF16),
            jax.ShapeDtypeStruct((n_give, rows.shape[1]), BF16),
        ),
        in_specs=[pl.BlockSpec(memory_space=pltpu.SMEM)] + [vmem] * 3 + [any_spec] * 6,
        out_specs=(vmem,) * 6,
        scratch_shapes=[pltpu.SemaphoreType.DMA((6,))],
        name="attention",
    )(place, queries, labels, lower, keys, values, rows, taps, upper, slab)


def backward_kernel(
    scale, core_ref, mine_ref, came_ref, adapter_ref, lower_ref, band_ref, out_ref, q_ref, k_ref,
    v_ref, query_ref, keep_ref, give_ref, key_sum, value_sum,
):
    rows = band_ref.shape[2] // 2
    head = k_ref.shape[1]
    key_sum[...] = jnp.zeros_like(key_sum)
    value_sum[...] = jnp.zeros_like(value_sum)
    for i in range(q_ref.shape[0] // rows):
        at, low = i * rows, window(i, rows)
        part, seen = slice(at, at + rows), slice(low, low + 2 * rows)
        adapter = adapter_ref[part, lower_ref.shape[0] :]
        lora = jnp.dot(adapter, lower_ref[...], preferred_element_type=F32)
        gradient = (mine_ref[part] + came_ref[part] + adapter_scale * lora).astype(BF16)
        for h in range(band_ref.shape[0]):
            cols = slice(h * head, (h + 1) * head)
            own = gradient[:, cols]
            probs = band_ref[h, part]
            terms = jnp.sum(
                own.astype(F32) * out_ref[part, cols].astype(F32), axis=1, keepdims=True
            )
            prob_grad = lax.dot_general(own, v_ref[seen], NT, preferred_element_type=F32)
            score_grad = (probs * (prob_grad - terms)).astype(BF16)
            query_grad = jnp.dot(score_grad, k_ref[seen], preferred_element_type=F32)
            query_ref[part, cols] = (scale * query_grad).astype(BF16)
            key_sum[seen] += lax.dot_general(
                score_grad, q_ref[part, cols], TN, preferred_element_type=F32
            )
            value_sum[seen] += lax.dot_general(
                probs.astype(BF16), own, TN, preferred_element_type=F32
            )
    quarter = head // 4
    for source, factor, at in ((key_sum, scale, 0), (value_sum, None, 2 * quarter)):
        total = source[...] if factor is None else source[...] * factor
        even = jnp.concatenate([total[:, :quarter], total[:, 2 * quarter : 3 * quarter]], axis=1)
        odd = jnp.concatenate([total[:, quarter : 2 * quarter], total[:, 3 * quarter :]], axis=1)
        first = core_ref[0] == 0
        keep_ref[:, at : at + 2 * quarter] = jnp.where(first, even, odd)
        give_ref[:, at : at + 2 * quarter] = jnp.where(first, odd, even)


def backward(core, mine, came, adapter, lower, band, out, queries, key_head, value_head):
    n, width = queries.shape
    half = jax.ShapeDtypeStruct((n, HEAD_WIDTH), F32)
    return pl.pallas_call(
        functools.partial(backward_kernel, HEAD_WIDTH**-0.5),
        out_shape=(jax.ShapeDtypeStruct((n, width), BF16), half, half),
        in_specs=[pl.BlockSpec(memory_space=pltpu.SMEM)]
        + [pl.BlockSpec(memory_space=pltpu.VMEM)] * 9,
        out_specs=(pl.BlockSpec(memory_space=pltpu.VMEM),) * 3,
        scratch_shapes=[pltpu.VMEM((n, HEAD_WIDTH), F32)] * 2,
        cost_estimate=pl.CostEstimate(
            flops=20 * n * width * 2 * SEGMENT_MOST, bytes_accessed=16 << 20, transcendentals=0
        ),
        name="attention_gradient",
    )(core, mine, came, adapter, lower, band, out, queries, key_head, value_head)


def quarters_kernel(chip_ref, keep_ref, came_ref, out_ref, give_ref):
    total = keep_ref[...] + came_ref[...]
    n, quarter = total.shape[0] // 2, total.shape[1] // 4
    even = jnp.concatenate([total[:, :quarter], total[:, 2 * quarter : 3 * quarter]], axis=1)
    odd = jnp.concatenate([total[:, quarter : 2 * quarter], total[:, 3 * quarter :]], axis=1)
    first = chip_ref[0] == 0
    out_ref[...] = jnp.where(first, even, odd)
    give = jnp.where(first, odd, even).astype(BF16)
    give_ref[...] = jnp.concatenate([give[:n], give[n:]], axis=1)


def quarters_kept(chip, keep, came):
    n, width = keep.shape
    return pl.pallas_call(
        quarters_kernel,
        out_shape=(
            jax.ShapeDtypeStruct((n, width // 2), F32),
            jax.ShapeDtypeStruct((n // 2, width), BF16),
        ),
        in_specs=[pl.BlockSpec(memory_space=pltpu.SMEM)]
        + [pl.BlockSpec(memory_space=pltpu.VMEM)] * 2,
        out_specs=(pl.BlockSpec(memory_space=pltpu.VMEM),) * 2,
        name="quarters",
    )(chip, keep, came)


def rounded_sum_kernel(keep_ref, came_ref, key_ref, value_ref):
    came = came_ref[...].astype(F32)
    quarter = key_ref.shape[0]
    came = jnp.concatenate([came[:, : 2 * quarter], came[:, 2 * quarter :]], axis=0)
    total = (keep_ref[...] + came).T.astype(BF16)
    key_ref[...] = total[:quarter]
    value_ref[...] = total[quarter:]


def rounded_sum(keep, came):
    n, width = keep.shape
    vmem = pl.BlockSpec(memory_space=pltpu.VMEM)
    return pl.pallas_call(
        rounded_sum_kernel,
        out_shape=(jax.ShapeDtypeStruct((width // 2, n), BF16),) * 2,
        in_specs=[vmem] * 2,
        out_specs=(vmem,) * 2,
        name="rounded_sum",
    )(keep, came)


def on_device(
    rotated_queries,
    rotated_keys,
    stored_values,
    segment_labels,
    output_gradient,
    draft_loss_gradients,
    tapped_row_index,
    output_projector,
    lower_factor_weight,
    upper_factor_weight,
):
    seq_len = rotated_queries.shape[1]
    head_size = HEAD_WIDTH
    heads_dev = rotated_queries.shape[2] // head_size
    group_size = QUERY_HEAD_COUNT // KVH
    score_scale = head_size ** (-0.5)
    core = lax.axis_index("draft")
    tensor = lax.axis_index("tensor")
    dp = lax.axis_index("dp")
    upper_core = core == 1
    rank_index = tensor * 2 + core
    kv_head = rank_index * heads_dev // group_size
    width = output_projector.shape[1] // 2
    rank = lower_factor_weight.shape[1]

    core_ref = core.reshape(1)
    y = tensor // SIDE
    place = jnp.stack([core, y, kv_head]).astype(jnp.int32)
    rows, taps = output_gradient[0], draft_loss_gradients[0]
    queries, lower = rotated_queries[0], lower_factor_weight.T
    band, output_flattened, inner_piece, key_head, value_head, give = forward(
        place,
        queries,
        segment_labels,
        lower,
        rotated_keys[0],
        stored_values[0],
        rows,
        taps,
        upper_factor_weight,
        output_projector,
    )
    block, _, stacked = blend(
        place,
        tapped_row_index,
        rows,
        taps,
        upper_factor_weight,
        output_projector,
        swapped(give, "draft", 1),
        inner_piece,
    )
    z1, z2 = near_move(block, 1, 1), near_move(block, 3, 2)

    half = seq_len // 2
    own_far = spread(stacked, AXES, far_groups())
    quarter = ride_sum(own_far, seq_len)
    from_z = [first_swapped(quarter, mask).astype(F32) for mask in (1, 2, 3)]
    quarter = ((quarter.astype(F32) + from_z[1]) + (from_z[0] + from_z[2])).astype(BF16)
    low = near_move(jnp.where(upper_core, block[:half], z1[:half]), 1, 3)
    high = near_move(jnp.where(upper_core, block[half:], z2[half:]), 3, 3)
    last = joined(low, high)
    near = jnp.concatenate([z1, z2, widened(quarter, SIDE)], axis=0)
    near_far = [far_move(near, k) for k in (1, 2, 3)]
    give, sums = give_near(
        place,
        after(quarter, last),
        [own_far, z1, z2, *near_far],
        [own_far.shape[0] // SIDE] + [seq_len] * 5,
        seq_len,
    )
    came_near = swapped(give, "draft", 1)
    residual = lax.dynamic_slice_in_dim(came_near, y * seq_len, seq_len, 0)
    residual = jnp.where(upper_core, residual, block[:, :width])
    last_far = [far_move(last, k) for k in (1, 2, 3)]
    sums = jnp.where(upper_core, narrowed(came_near[12 * seq_len :], 2), sums)
    adapter_inner, adapter_gradient = sums[:, :rank], sums[:, rank:]

    lower_piece = lax.dot_general(adapter_gradient, output_flattened, TN, preferred_element_type=F32)
    upper_piece = lax.dot_general(adapter_inner, residual, TN, preferred_element_type=F32)
    factor = jnp.concatenate([lower_piece, upper_piece], axis=0)
    factor = factor + swapped(factor, "dp", 1)
    from_dp = swapped(factor, "dp", 2)
    give = give_half(core_ref, [after(last, came_near, factor), *last_far], seq_len)
    came_last = swapped(give, "draft", 1)

    part_mine, part_other = frozen_product(
        core_ref,
        block_order(core, dp, tensor),
        [(own_far, own_far.shape[0] // SIDE)]
        + [(a, seq_len) for a in (z1, z2, *near_far, last, *last_far)],
        [(came_near, seq_len), (came_last, seq_len)],
        seq_len,
    )
    factor = factor + after(from_dp, part_mine)
    came = swapped(after(part_other, factor), "draft", 1)
    from_dp = swapped(factor, "dp", 4)
    query_grad, keep, give = backward(
        core_ref,
        part_mine,
        came,
        sums,
        lower,
        band,
        output_flattened,
        queries,
        key_head,
        value_head,
    )
    factor = factor + after(from_dp, give)
    came = swapped(after(give, factor), "draft", 1)
    from_dp = swapped(factor, "dp", 8)
    keep, give = quarters_kept((tensor & 1).reshape(1), keep, came)
    came = swapped(give, "tensor", 1)
    factor = factor + after(from_dp, give)
    factor = factor * (adapter_scale / lax.axis_size("dp"))
    lower_gradient, upper_gradient = factor[:rank].T, factor[rank:]
    key_grad, value_grad = rounded_sum(keep, came)
    key_grad, value_grad = key_grad.T[None], value_grad.T[None]
    query_grad = query_grad[None]
    return (query_grad, key_grad, value_grad, lower_gradient, upper_gradient)


def solution(mesh):
    in_specs = (
        P("dp", None, ("tensor", "draft")),
        P("dp", None, None),
        P("dp", None, None),
        P("dp", None),
        P("dp", "draft", "tensor"),
        P("dp", "draft", "tensor"),
        P("dp", None),
        P(("tensor", "draft"), "dp"),
        P(("tensor", "draft"), None),
        P(None, ("tensor", "draft")),
    )
    out_specs = (
        P("dp", None, ("tensor", "draft")),
        P("dp", None, ("tensor", "draft")),
        P("dp", None, ("tensor", "draft")),
        P(("tensor", "draft"), None),
        P(None, ("tensor", "draft")),
    )
    return jax.shard_map(
        on_device, mesh=mesh, in_specs=in_specs, out_specs=out_specs, check_vma=False
    )
```

time: 239 us -> 194 us (0.81); the launches traced: 235 us -> 193 us
  starting transfers between devices: 139 us -> 89.7 us
  Pallas kernels: 11.6 us -> 34.3 us
  matrix products: 10.7 us -> 1.53 us
  waiting for transfers between devices: 59.1 us -> 53.2 us
  other arithmetic: 7.24 us -> 3.2 us
  local copies, waits for them, and re-layouts: 5.82 us -> 9.35 us
    ppermute x20 -> x10, starting transfers between devices: 100 us -> 51.7 us  [swapped(): lax.ppermute(array, axis, [(i, i ^ mask) for i in range(lax.axis_size(axi...]
    pallas_call x2 -> x9, Pallas kernels: 9.49 us -> 31.3 us  [the longest x1 7.95 us: frozen_product(): pl.pallas_call(functools.partial(frozen_kernel, len(own), parts), out_sha...]
    ppermute x20 -> x10, waiting for transfers between devices: 27.1 us -> 11.3 us  [swapped(): lax.ppermute(array, axis, [(i, i ^ mask) for i in range(lax.axis_size(axi...]
    all_to_all x0 -> x1, waiting for transfers between devices: none -> 12.5 us  [spread(): lax.all_to_all(stacked, axes, 0, 0, axis_index_groups=groups, tiled=True)]
    dot_general x8 -> x0, matrix products: 7.05 us -> none  [the longest x1 2.14 us: on_device(): jnp.einsum('ihd,jd->hij', grad_heads, value_head, preferred_element_type=...]
    ppermute x12 -> x10, starting transfers between devices: 38.6 us -> 32.4 us  [moved(): return lax.ppermute(array, AXES, pairs)]
    unnamed x51 -> x44, local copies, waits for them, and re-layouts: 3.17 us -> 7.81 us
    all_to_all x0 -> x1, starting transfers between devices: none -> 3.62 us  [spread(): lax.all_to_all(stacked, axes, 0, 0, axis_index_groups=groups, tiled=True)]
  transfers between devices with their start and end apart: 32 -> 24, of which waited for: 14 -> 9; matrix products, arithmetic and copies ran while one was open for 9% -> 3% of each run, Pallas kernels for 0% -> 9%
where the time goes in v3:
time: 194 us; the launch traced here: 193 us
  starting transfers between devices  89.7 us (46%)
  waiting for transfers between devices  53.2 us (27%)
  Pallas kernels  34.3 us (18%)
  local copies, waits for them, and re-layouts  9.35 us (5%)
  other arithmetic  3.2 us (2%)
    ppermute x10, starting transfers between devices, swapped(): lax.ppermute(array, axis, [(i, i ^ mask) for i in range(lax.axis_size(axi...  51.7 us
    ppermute x10, starting transfers between devices, moved(): return lax.ppermute(array, AXES, pairs)  32.4 us
    ppermute x10, waiting for transfers between devices, moved(): return lax.ppermute(array, AXES, pairs)  29.5 us
    all_to_all x1, waiting for transfers between devices, spread(): lax.all_to_all(stacked, axes, 0, 0, axis_index_groups=groups, tiled=True)  12.5 us
    ppermute x10, waiting for transfers between devices, swapped(): lax.ppermute(array, axis, [(i, i ^ mask) for i in range(lax.axis_size(axi...  11.3 us
    pallas_call x1, Pallas kernels, frozen_product(): pl.pallas_call(functools.partial(frozen_kernel, len(own), parts), out_sha...  7.95 us
    unnamed x44, local copies, waits for them, and re-layouts  7.81 us
    pallas_call x1, Pallas kernels, backward(): pl.pallas_call(functools.partial(backward_kernel, HEAD_WIDTH ** (-0.5)),...  4.9 us
  transfers between devices with their start and end apart: 24, of which 9 were waited for; matrix products, arithmetic and copies ran while one was open for 3% of the time, Pallas kernels for 9%

profile of v3, /device:TPU:1, one launch (start us, length us, event | category | flops | bytes accessed | tf_op | source)
XLA Modules:
  0.0 192.7 jit_solution(14829574368328603148)
XLA Ops:
  0.7 0.6 pad_add_fusion.place_ref
  1.2 4.8 %attention.1 = (f32[2,512,256]{2,1,0:T(8,128)}, bf16[512,256]{1,0:T(8,128)(2,1)}, f32[512,64]{1,0:T(8,128)}, bf16[512,128]{1,0:T(8,128)(2,1)}, bf16[512,128]{1,0:T(8,128)(2,1)}, /*index=5*/bf16[416,512]{1,0:T(8,128)(2,1)}) custom-call(s32[3]{0:T(128)} %pad_add_fusion.place_ref, bf16[512,256]{1,0:T(8,128)(2,1)} %bitcast.26, s32[1,512]{1,0:T(1,128)} %label_ref.1, ...), custom_call_target="tpu_custom_call" | custom-call | tf_op jit(solution)/shard_map/attention/pallas_call | solution.py:430
  6.0 8.8 %collective-permute-start = (bf16[416,512]{1,0:T(8,128)(2,1)}, bf16[416,512]{1,0:T(8,128)(2,1)S(1)}, u32[]{:S(2)}, u32[]{:S(2)}) collective-permute-start(bf16[416,512]{1,0:T(8,128)(2,1)} %get-tuple-element.31), channel_id=1, source_target_pairs={{0,1},{1,0},{2,3},{3,2},{4,5},{5,4},{6,7},{7,6},{8,9},{9,8},{10,11... | collective-permute-start | bytes 1277960 | tf_op jit(solution)/shard_map/ppermute | solution.py:71
  14.8 1.6 collective-permute-done.came_ref
  16.4 0.8 copy-done.10
  17.2 3.0 %blend.1 = (bf16[512,512]{1,0:T(8,128)(2,1)}, f32[512,128]{1,0:T(8,128)}, bf16[2176,512]{1,0:T(8,128)(2,1)}) custom-call(s32[3]{0:T(128)} %pad_add_fusion.place_ref, s32[1,128]{1,0:T(1,128)} %tapped_ref.1, bf16[256,512]{1,0:T(8,128)(2,1)} %bitcast.29, bf16[64,512]{1,0:T(8,128)(2,1)} %bitcast.33, bf16[64,256]{1,0:T(8,128)(2,1)} %upper_ref.3, ...), custom_call_target="tpu_custom_call" | custom-call | tf_op jit(solution)/shard_map/blend/pallas_call | solution.py:126
  20.2 3.6 %all-to-all-start = ((bf16[4,544,512]{2,1,0:T(8,128)(2,1)}), bf16[4,544,512]{2,1,0:T(8,128)(2,1)S(1)}, u32[]{:S(2)}, u32[]{:S(2)}) async-start(bf16[4,544,512]{2,1,0:T(8,128)(2,1)} %bitcast.25), calls=%async_computation | async-start | bytes 4456448 | tf_op jit(solution)/shard_map/all_to_all | solution.py:39
  23.8 1.9 collective-permute-start.1
  25.7 1.9 collective-permute-start.2
  27.7 12.5 %all-to-all-done = bf16[4,544,512]{2,1,0:T(8,128)(2,1)S(1)} async-done(((bf16[4,544,512]{2,1,0:T(8,128)(2,1)}), bf16[4,544,512]{2,1,0:T(8,128)(2,1)S(1)}, u32[]{:S(2)}, u32[]{:S(2)}) %all-to-all-start) | async-done | bytes 2228256 | tf_op jit(solution)/shard_map/all_to_all | solution.py:39
  40.1 1.4 copy-done
  41.5 1.5 ride_sum.1
  43.0 0.7 collective-permute-start.3
  43.7 0.7 collective-permute-start.4
  44.4 0.7 collective-permute-start.5
  45.1 0.8 add_convert_fusion.quarter_ref
  45.9 19.5 %collective-permute-done.2.refs_2_ = bf16[512,512]{1,0:T(8,128)(2,1)S(1)} collective-permute-done((bf16[512,512]{1,0:T(8,128)(2,1)}, bf16[512,512]{1,0:T(8,128)(2,1)S(1)}, u32[]{:S(2)}, u32[]{:S(2)}) %collective-permute-start.2) | collective-permute-done | bytes 524320 | tf_op jit(solution)/shard_map/ppermute | solution.py:35
  65.4 0.1 maximum_maximum_fusion
  65.4 3.5 %collective-permute-start.6 = (bf16[1056,512]{1,0:T(8,128)(2,1)S(1)}, bf16[1056,512]{1,0:T(8,128)(2,1)}, u32[]{:S(2)}, u32[]{:S(2)}) collective-permute-start(bf16[1056,512]{1,0:T(8,128)(2,1)S(1)} %maximum_maximum_fusion), channel_id=1, source_target_pairs={{0,8},{1,129},{2,10},{3,131},{4,12},{5,133},{6,14},{7,135},{8,16},... | collective-permute-start | bytes 3244040 | tf_op jit(solution)/shard_map/ppermute | solution.py:35
  69.0 4.3 %collective-permute-start.7 = (bf16[1056,512]{1,0:T(8,128)(2,1)S(1)}, bf16[1056,512]{1,0:T(8,128)(2,1)}, u32[]{:S(2)}, u32[]{:S(2)}) collective-permute-start(bf16[1056,512]{1,0:T(8,128)(2,1)S(1)} %maximum_maximum_fusion), channel_id=1, source_target_pairs={{0,16},{1,257},{2,18},{3,259},{4,20},{5,261},{6,22},{7,263},{8,24}... | collective-permute-start | bytes 3244040 | tf_op jit(solution)/shard_map/ppermute | solution.py:35
  73.2 3.1 %collective-permute-start.8 = (bf16[1056,512]{1,0:T(8,128)(2,1)S(1)}, bf16[1056,512]{1,0:T(8,128)(2,1)}, u32[]{:S(2)}, u32[]{:S(2)}) collective-permute-start(bf16[1056,512]{1,0:T(8,128)(2,1)S(1)} %maximum_maximum_fusion), channel_id=1, source_target_pairs={{0,24},{1,385},{2,26},{3,387},{4,28},{5,389},{6,30},{7,391},{8,0},... | collective-permute-start | bytes 3244040 | tf_op jit(solution)/shard_map/ppermute | solution.py:35
  76.4 1.1 slice_select_fusion
  77.5 1.9 collective-permute-start.10
  79.4 5.2 %collective-permute-start.9 = (bf16[256,512]{1,0:T(8,128)(2,1)S(1)}, bf16[256,512]{1,0:T(8,128)(2,1)S(1)}, u32[]{:S(2)}, u32[]{:S(2)}) collective-permute-start(bf16[256,512]{1,0:T(8,128)(2,1)S(1)} %get-tuple-element.60), channel_id=1, source_target_pairs={{0,2},{1,97},{2,4},{3,99},{4,6},{5,101},{6,0},{7,103},{8,10},{9,10... | collective-permute-start | bytes 786440 | tf_op jit(solution)/shard_map/ppermute | solution.py:35
  84.6 2.0 %collective-permute-done.10.high_ref = bf16[256,512]{1,0:T(8,128)(2,1)S(1)} collective-permute-done((bf16[256,512]{1,0:T(8,128)(2,1)S(1)}, bf16[256,512]{1,0:T(8,128)(2,1)S(1)}, u32[]{:S(2)}, u32[]{:S(2)}) %collective-permute-start.10) | collective-permute-done | bytes 262176 | tf_op jit(solution)/shard_map/ppermute | solution.py:35
  86.5 3.9 %collective-permute-done.9.low_ref = bf16[256,512]{1,0:T(8,128)(2,1)S(1)} collective-permute-done((bf16[256,512]{1,0:T(8,128)(2,1)S(1)}, bf16[256,512]{1,0:T(8,128)(2,1)S(1)}, u32[]{:S(2)}, u32[]{:S(2)}) %collective-permute-start.9) | collective-permute-done | bytes 262176 | tf_op jit(solution)/shard_map/ppermute | solution.py:35
  90.4 0.7 copy-done.14
  91.2 1.9 joined.1.refs_0_.refs_6_
  93.0 2.8 %collective-permute-done.7.refs_4_ = bf16[1056,512]{1,0:T(8,128)(2,1)} collective-permute-done((bf16[1056,512]{1,0:T(8,128)(2,1)S(1)}, bf16[1056,512]{1,0:T(8,128)(2,1)}, u32[]{:S(2)}, u32[]{:S(2)}) %collective-permute-start.7) | collective-permute-done | bytes 1081376 | tf_op jit(solution)/shard_map/ppermute | solution.py:35
  95.8 1.4 collective-permute-done.8.refs_5_
  97.2 4.5 %give_near.1 = (bf16[6400,256]{1,0:T(8,128)(2,1)}, bf16[512,128]{1,0:T(8,128)(2,1)}) custom-call(s32[3]{0:T(128)} %pad_add_fusion.place_ref, bf16[128,128]{1,0:T(8,128)(2,1)} %copy-done.11, bf16[2176,512]{1,0:T(8,128)(2,1)} %bitcast.23, bf16[512,512]{1,0:T(8,128)(2,1)} %copy-done.1, bf16[512,512]{1,0:T(8,128)(2,1)} %copy-done.2, ...), custom_call_target="tpu_custom_call" | custom-call | tf_op jit(solution)/shard_map/give_near/pallas_call | solution.py:258
  101.7 9.3 %collective-permute-start.14 = (bf16[6400,256]{1,0:T(8,128)(2,1)}, bf16[6400,256]{1,0:T(8,128)(2,1)}, u32[]{:S(2)}, u32[]{:S(2)}) collective-permute-start(bf16[6400,256]{1,0:T(8,128)(2,1)} %get-tuple-element.36), channel_id=1, source_target_pairs={{0,1},{1,0},{2,3},{3,2},{4,5},{5,4},{6,7},{7,6},{8,9},{9,8},{10,11... | collective-permute-start | bytes 9830408 | tf_op jit(solution)/shard_map/ppermute | solution.py:71
  111.0 3.1 %collective-permute-start.11 = (bf16[512,512]{1,0:T(8,128)(2,1)S(1)}, bf16[512,512]{1,0:T(8,128)(2,1)S(1)}, u32[]{:S(2)}, u32[]{:S(2)}) collective-permute-start(bf16[512,512]{1,0:T(8,128)(2,1)S(1)} %copy-done.3), channel_id=1, source_target_pairs={{0,8},{1,129},{2,10},{3,131},{4,12},{5,133},{6,14},{7,135},{8,16},... | collective-permute-start | bytes 1572872 | tf_op jit(solution)/shard_map/ppermute | solution.py:35
  114.1 4.4 %collective-permute-start.12 = (bf16[512,512]{1,0:T(8,128)(2,1)S(1)}, bf16[512,512]{1,0:T(8,128)(2,1)S(1)}, u32[]{:S(2)}, u32[]{:S(2)}) collective-permute-start(bf16[512,512]{1,0:T(8,128)(2,1)S(1)} %copy-done.3), channel_id=1, source_target_pairs={{0,16},{1,257},{2,18},{3,259},{4,20},{5,261},{6,22},{7,263},{8,24}... | collective-permute-start | bytes 1572872 | tf_op jit(solution)/shard_map/ppermute | solution.py:35
  118.5 3.1 %collective-permute-start.13 = (bf16[512,512]{1,0:T(8,128)(2,1)S(1)}, bf16[512,512]{1,0:T(8,128)(2,1)S(1)}, u32[]{:S(2)}, u32[]{:S(2)}) collective-permute-start(bf16[512,512]{1,0:T(8,128)(2,1)S(1)} %copy-done.3), channel_id=1, source_target_pairs={{0,24},{1,385},{2,26},{3,387},{4,28},{5,389},{6,30},{7,391},{8,0},... | collective-permute-start | bytes 1572872 | tf_op jit(solution)/shard_map/ppermute | solution.py:35
  121.6 0.9 fusion.15
  122.6 0.3 fusion.6
  122.9 0.0 copy-start.17
  122.9 0.0 copy-start.18
  122.9 1.2 fusion
  124.2 8.9 %collective-permute-start.15 = (f32[128,256]{1,0:T(8,128)S(1)}, f32[128,256]{1,0:T(8,128)S(1)}, u32[]{:S(2)}, u32[]{:S(2)}) collective-permute-start(f32[128,256]{1,0:T(8,128)S(1)} %pad_maximum_fusion), channel_id=1, source_target_pairs={{0,32},{32,0},{64,96},{96,64},{128,160},{160,128},{192,224},{224,1... | collective-permute-start | bytes 393224 | tf_op jit(solution)/shard_map/ppermute | solution.py:71
  133.1 2.8 %collective-permute-done.15 = f32[128,256]{1,0:T(8,128)S(1)} collective-permute-done((f32[128,256]{1,0:T(8,128)S(1)}, f32[128,256]{1,0:T(8,128)S(1)}, u32[]{:S(2)}, u32[]{:S(2)}) %collective-permute-start.15) | collective-permute-done | bytes 131104 | tf_op jit(solution)/shard_map/ppermute | solution.py:71
  136.0 0.8 copy-done.7
  136.7 0.2 copy-done.8
  136.9 0.8 copy-done.9
  137.7 2.2 %give.1 = bf16[2048,256]{1,0:T(8,128)(2,1)} custom-call(s32[1]{0:T(128)} %bitcast.core_ref, bf16[512,512]{1,0:T(8,128)(2,1)} %joined.1.refs_0_.refs_6_, bf16[512,512]{1,0:T(8,128)(2,1)} %copy-done.7, bf16[512,512]{1,0:T(8,128)(2,1)} %copy-done.8, bf16[512,512]{1,0:T(8,128)(2,1)} %copy-done.9), custom_call_target="tpu_custom_call" | custom-call | tf_op jit(solution)/shard_map/give/pallas_call | solution.py:217
  139.9 3.6 %collective-permute-start.16 = (bf16[2048,256]{1,0:T(8,128)(2,1)}, bf16[2048,256]{1,0:T(8,128)(2,1)S(1)}, u32[]{:S(2)}, u32[]{:S(2)}) collective-permute-start(bf16[2048,256]{1,0:T(8,128)(2,1)} %give.1), channel_id=1, source_target_pairs={{0,1},{1,0},{2,3},{3,2},{4,5},{5,4},{6,7},{7,6},{8,9},{9,8},{10,11... | collective-permute-start | bytes 3145736 | tf_op jit(solution)/shard_map/ppermute | solution.py:71
  143.6 0.5 compare_select_fusion.10.order_ref
  144.2 4.3 %collective-permute-start.17 = (f32[128,256]{1,0:T(8,128)S(1)}, f32[128,256]{1,0:T(8,128)S(1)}, u32[]{:S(2)}, u32[]{:S(2)}) collective-permute-start(f32[128,256]{1,0:T(8,128)S(1)} %fusion.14), channel_id=1, source_target_pairs={{0,64},{32,96},{64,0},{96,32},{128,192},{160,224},{192,128},{224,1... | collective-permute-start | bytes 393224 | tf_op jit(solution)/shard_map/ppermute | solution.py:71
  148.5 1.0 copy-done.21
  149.4 8.0 %frozen.1 = (f32[512,256]{1,0:T(8,128)}, f32[512,256]{1,0:T(8,128)}) custom-call(s32[1]{0:T(128)} %bitcast.core_ref, s32[16]{0:T(128)} %compare_select_fusion.10.order_ref, bf16[2176,512]{1,0:T(8,128)(2,1)} %bitcast.24, bf16[512,512]{1,0:T(8,128)(2,1)} %copy-done.1, bf16[512,512]{1,0:T(8,128)(2,1)} %copy-done.2, ...), custom_call_target="tpu_custom_call" | custom-call | flops 4294967296 | bytes 25165824 | tf_op jit(solution)/shard_map/frozen/pallas_call | solution.py:324
  157.4 2.0 %collective-permute-start.18 = (f32[512,256]{1,0:T(8,128)}, f32[512,256]{1,0:T(8,128)S(1)}, u32[]{:S(2)}, u32[]{:S(2)}) collective-permute-start(f32[512,256]{1,0:T(8,128)} %get-tuple-element.43), channel_id=1, source_target_pairs={{0,1},{1,0},{2,3},{3,2},{4,5},{5,4},{6,7},{7,6},{8,9},{9,8},{10,11... | collective-permute-start | bytes 1572872 | tf_op jit(solution)/shard_map/ppermute | solution.py:71
  159.5 2.2 %collective-permute-start.19 = (f32[128,256]{1,0:T(8,128)S(1)}, f32[128,256]{1,0:T(8,128)S(1)}, u32[]{:S(2)}, u32[]{:S(2)}) collective-permute-start(f32[128,256]{1,0:T(8,128)S(1)} %add.77), channel_id=1, source_target_pairs={{0,128},{32,160},{64,192},{96,224},{128,0},{160,32},{192,64},{224,... | collective-permute-start | bytes 393224 | tf_op jit(solution)/shard_map/ppermute | solution.py:71
  161.7 0.8 copy-done.6
  162.5 4.9 %attention_gradient.1 = (bf16[512,256]{1,0:T(8,128)(2,1)}, f32[512,128]{1,0:T(8,128)}, f32[512,128]{1,0:T(8,128)}) custom-call(s32[1]{0:T(128)} %bitcast.core_ref, f32[512,256]{1,0:T(8,128)} %get-tuple-element.40.mine_ref, f32[512,256]{1,0:T(8,128)} %copy-done.6, bf16[512,128]{1,0:T(8,128)(2,1)} %copy-done.4, bf16[64,256]{1,0:T(8,128)(2,1)} %bitcast.35, ...), custom_call_target="tpu_custom_call" | custom-call | flops 671088640 | bytes 16777216 | tf_op jit(solution)/shard_map/attention_gradient/pallas_call | solution.py:491
  167.4 2.6 %collective-permute-start.20 = (f32[512,128]{1,0:T(8,128)}, f32[512,128]{1,0:T(8,128)S(1)}, u32[]{:S(2)}, u32[]{:S(2)}) collective-permute-start(f32[512,128]{1,0:T(8,128)} %get-tuple-element.51), channel_id=1, source_target_pairs={{0,1},{1,0},{2,3},{3,2},{4,5},{5,4},{6,7},{7,6},{8,9},{9,8},{10,11... | collective-permute-start | bytes 786440 | tf_op jit(solution)/shard_map/ppermute | solution.py:71
  170.0 3.9 %collective-permute-start.22 = (f32[128,256]{1,0:T(8,128)S(1)}, f32[128,256]{1,0:T(8,128)S(1)}, u32[]{:S(2)}, u32[]{:S(2)}) collective-permute-start(f32[128,256]{1,0:T(8,128)S(1)} %add.78), channel_id=1, source_target_pairs={{0,256},{32,288},{64,320},{96,352},{128,384},{160,416},{192,448},{... | collective-permute-start | bytes 393224 | tf_op jit(solution)/shard_map/ppermute | solution.py:71
  173.9 0.7 copy-done.12
  174.6 2.0 %quarters.1 = (f32[512,64]{1,0:T(8,128)}, bf16[256,128]{1,0:T(8,128)(2,1)}) custom-call(s32[1]{0:T(128)} %bitcast.12.chip_ref, f32[512,128]{1,0:T(8,128)} %get-tuple-element.48.keep_ref, f32[512,128]{1,0:T(8,128)} %copy-done.12), custom_call_target="tpu_custom_call" | custom-call | tf_op jit(solution)/shard_map/quarters/pallas_call | solution.py:518
  176.6 6.1 %collective-permute-start.21 = (bf16[256,128]{1,0:T(8,128)(2,1)}, bf16[256,128]{1,0:T(8,128)(2,1)S(1)}, u32[]{:S(2)}, u32[]{:S(2)}) collective-permute-start(bf16[256,128]{1,0:T(8,128)(2,1)} %get-tuple-element.53), channel_id=1, source_target_pairs={{0,2},{2,0},{4,6},{6,4},{8,10},{10,8},{12,14},{14,12},{16,18},{18,... | collective-permute-start | bytes 196616 | tf_op jit(solution)/shard_map/ppermute | solution.py:71
  182.8 0.7 fusion.16
  183.4 6.9 %collective-permute-done.21.came_ref = bf16[256,128]{1,0:T(8,128)(2,1)S(1)} collective-permute-done((bf16[256,128]{1,0:T(8,128)(2,1)}, bf16[256,128]{1,0:T(8,128)(2,1)S(1)}, u32[]{:S(2)}, u32[]{:S(2)}) %collective-permute-start.21) | collective-permute-done | bytes 65568 | tf_op jit(solution)/shard_map/ppermute | solution.py:71
  190.3 0.6 copy-done.15
  190.9 1.7 rounded_sum.1
  (54 shorter events, 0.3 us)
Async XLA Ops:
  6.0 10.4 %collective-permute-start = (bf16[416,512]{1,0:T(8,128)(2,1)}, bf16[416,512]{1,0:T(8,128)(2,1)S(1)}, u32[]{:S(2)}, u32[]{:S(2)}) collective-permute-start(bf16[416,512]{1,0:T(8,128)(2,1)} %get-tuple-element.31), channel_id=1, source_target_pairs={{0,1},{1,0},{2,3},{3,2},{4,5},{5,4},{6,7},{7,6},{8,9},{9,8},{10,11... | collective-permute-start | bytes 1277960 | tf_op jit(solution)/shard_map/ppermute | solution.py:71
  16.4 0.8 copy-start.10
  20.2 19.9 %all-to-all-start = ((bf16[4,544,512]{2,1,0:T(8,128)(2,1)}), bf16[4,544,512]{2,1,0:T(8,128)(2,1)S(1)}, u32[]{:S(2)}, u32[]{:S(2)}) async-start(bf16[4,544,512]{2,1,0:T(8,128)(2,1)} %bitcast.25), calls=%async_computation | async-start | bytes 4456448 | tf_op jit(solution)/shard_map/all_to_all | solution.py:39
  23.8 22.1 %collective-permute-start.1 = (bf16[512,512]{1,0:T(8,128)(2,1)}, bf16[512,512]{1,0:T(8,128)(2,1)S(1)}, u32[]{:S(2)}, u32[]{:S(2)}) collective-permute-start(bf16[512,512]{1,0:T(8,128)(2,1)} %get-tuple-element.34), channel_id=1, source_target_pairs={{0,2},{1,33},{2,4},{3,35},{4,6},{5,37},{6,0},{7,39},{8,10},{9,41},... | collective-permute-start | bytes 1572872 | tf_op jit(solution)/shard_map/ppermute | solution.py:35
  25.7 39.6 %collective-permute-start.2 = (bf16[512,512]{1,0:T(8,128)(2,1)}, bf16[512,512]{1,0:T(8,128)(2,1)S(1)}, u32[]{:S(2)}, u32[]{:S(2)}) collective-permute-start(bf16[512,512]{1,0:T(8,128)(2,1)} %get-tuple-element.34), channel_id=1, source_target_pairs={{0,6},{1,65},{2,0},{3,67},{4,2},{5,69},{6,4},{7,71},{8,14},{9,73},... | collective-permute-start | bytes 1572872 | tf_op jit(solution)/shard_map/ppermute | solution.py:35
  40.1 1.4 copy-start
  43.0 2.0 %collective-permute-start.3 = (bf16[128,128]{1,0:T(8,128)(2,1)}, bf16[128,128]{1,0:T(8,128)(2,1)S(1)}, u32[]{:S(2)}, u32[]{:S(2)}) collective-permute-start(bf16[128,128]{1,0:T(8,128)(2,1)} %ride_sum.1), channel_id=1, source_target_pairs={{0,4},{2,6},{4,0},{6,2},{8,12},{10,14},{12,8},{14,10},{16,20},{18,... | collective-permute-start | bytes 98312 | tf_op jit(solution)/shard_map/ppermute | solution.py:67
  43.7 1.4 collective-permute-start.4
  44.4 0.7 collective-permute-start.5
  45.9 47.2 %copy-start.11 = (bf16[128,128]{1,0:T(8,128)(2,1)}, bf16[128,128]{1,0:T(8,128)(2,1)S(1)}, u32[]{:S(2)}) copy-start(bf16[128,128]{1,0:T(8,128)(2,1)S(1)} %add_convert_fusion.quarter_ref) | copy-start | bytes 98308
  45.9 47.1 %copy-start.1 = (bf16[512,512]{1,0:T(8,128)(2,1)}, bf16[512,512]{1,0:T(8,128)(2,1)S(1)}, u32[]{:S(2)}) copy-start(bf16[512,512]{1,0:T(8,128)(2,1)S(1)} %collective-permute-done.1.refs_1_) | copy-start | bytes 1572868
  65.4 27.6 %copy-start.2 = (bf16[512,512]{1,0:T(8,128)(2,1)}, bf16[512,512]{1,0:T(8,128)(2,1)S(1)}, u32[]{:S(2)}) copy-start(bf16[512,512]{1,0:T(8,128)(2,1)S(1)} %collective-permute-done.2.refs_2_) | copy-start | bytes 1572868
  65.4 27.6 %collective-permute-start.6 = (bf16[1056,512]{1,0:T(8,128)(2,1)S(1)}, bf16[1056,512]{1,0:T(8,128)(2,1)}, u32[]{:S(2)}, u32[]{:S(2)}) collective-permute-start(bf16[1056,512]{1,0:T(8,128)(2,1)S(1)} %maximum_maximum_fusion), channel_id=1, source_target_pairs={{0,8},{1,129},{2,10},{3,131},{4,12},{5,133},{6,14},{7,135},{8,16},... | collective-permute-start | bytes 3244040 | tf_op jit(solution)/shard_map/ppermute | solution.py:35
  69.0 26.9 %collective-permute-start.7 = (bf16[1056,512]{1,0:T(8,128)(2,1)S(1)}, bf16[1056,512]{1,0:T(8,128)(2,1)}, u32[]{:S(2)}, u32[]{:S(2)}) collective-permute-start(bf16[1056,512]{1,0:T(8,128)(2,1)S(1)} %maximum_maximum_fusion), channel_id=1, source_target_pairs={{0,16},{1,257},{2,18},{3,259},{4,20},{5,261},{6,22},{7,263},{8,24}... | collective-permute-start | bytes 3244040 | tf_op jit(solution)/shard_map/ppermute | solution.py:35
  73.2 23.9 %collective-permute-start.8 = (bf16[1056,512]{1,0:T(8,128)(2,1)S(1)}, bf16[1056,512]{1,0:T(8,128)(2,1)}, u32[]{:S(2)}, u32[]{:S(2)}) collective-permute-start(bf16[1056,512]{1,0:T(8,128)(2,1)S(1)} %maximum_maximum_fusion), channel_id=1, source_target_pairs={{0,24},{1,385},{2,26},{3,387},{4,28},{5,389},{6,30},{7,391},{8,0},... | collective-permute-start | bytes 3244040 | tf_op jit(solution)/shard_map/ppermute | solution.py:35
  77.5 9.1 %collective-permute-start.10 = (bf16[256,512]{1,0:T(8,128)(2,1)S(1)}, bf16[256,512]{1,0:T(8,128)(2,1)S(1)}, u32[]{:S(2)}, u32[]{:S(2)}) collective-permute-start(bf16[256,512]{1,0:T(8,128)(2,1)S(1)} %get-tuple-element.59), channel_id=1, source_target_pairs={{0,6},{1,97},{2,0},{3,99},{4,2},{5,101},{6,4},{7,103},{8,14},{9,10... | collective-permute-start | bytes 786440 | tf_op jit(solution)/shard_map/ppermute | solution.py:35
  79.4 11.1 %collective-permute-start.9 = (bf16[256,512]{1,0:T(8,128)(2,1)S(1)}, bf16[256,512]{1,0:T(8,128)(2,1)S(1)}, u32[]{:S(2)}, u32[]{:S(2)}) collective-permute-start(bf16[256,512]{1,0:T(8,128)(2,1)S(1)} %get-tuple-element.60), channel_id=1, source_target_pairs={{0,2},{1,97},{2,4},{3,99},{4,6},{5,101},{6,0},{7,103},{8,10},{9,10... | collective-permute-start | bytes 786440 | tf_op jit(solution)/shard_map/ppermute | solution.py:35
  86.5 3.9 %copy-start.13 = (bf16[256,512]{1,0:T(8,128)(2,1)}, bf16[256,512]{1,0:T(8,128)(2,1)S(1)}, u32[]{:S(2)}) copy-start(bf16[256,512]{1,0:T(8,128)(2,1)S(1)} %collective-permute-done.10.high_ref) | copy-start | bytes 786436
  90.4 0.7 copy-start.14
  93.0 18.0 %copy-start.3 = (bf16[512,512]{1,0:T(8,128)(2,1)S(1)}, bf16[512,512]{1,0:T(8,128)(2,1)}, u32[]{:S(2)}) copy-start(bf16[512,512]{1,0:T(8,128)(2,1)} %joined.1.refs_0_.refs_6_) | copy-start | bytes 1572868
  93.0 29.5 %copy-start.5 = (bf16[512,256]{1,0:T(8,128)(2,1)S(1)}, bf16[512,256]{1,0:T(8,128)(2,1)}, u32[]{:S(2)}) copy-start(bf16[512,256]{1,0:T(8,128)(2,1)} %get-tuple-element.38.out_ref) | copy-start | bytes 786436
  101.7 19.9 %collective-permute-start.14 = (bf16[6400,256]{1,0:T(8,128)(2,1)}, bf16[6400,256]{1,0:T(8,128)(2,1)}, u32[]{:S(2)}, u32[]{:S(2)}) collective-permute-start(bf16[6400,256]{1,0:T(8,128)(2,1)} %get-tuple-element.36), channel_id=1, source_target_pairs={{0,1},{1,0},{2,3},{3,2},{4,5},{5,4},{6,7},{7,6},{8,9},{9,8},{10,11... | collective-permute-start | bytes 9830408 | tf_op jit(solution)/shard_map/ppermute | solution.py:71
  111.0 24.9 %collective-permute-start.11 = (bf16[512,512]{1,0:T(8,128)(2,1)S(1)}, bf16[512,512]{1,0:T(8,128)(2,1)S(1)}, u32[]{:S(2)}, u32[]{:S(2)}) collective-permute-start(bf16[512,512]{1,0:T(8,128)(2,1)S(1)} %copy-done.3), channel_id=1, source_target_pairs={{0,8},{1,129},{2,10},{3,131},{4,12},{5,133},{6,14},{7,135},{8,16},... | collective-permute-start | bytes 1572872 | tf_op jit(solution)/shard_map/ppermute | solution.py:35
  114.1 21.8 %collective-permute-start.12 = (bf16[512,512]{1,0:T(8,128)(2,1)S(1)}, bf16[512,512]{1,0:T(8,128)(2,1)S(1)}, u32[]{:S(2)}, u32[]{:S(2)}) collective-permute-start(bf16[512,512]{1,0:T(8,128)(2,1)S(1)} %copy-done.3), channel_id=1, source_target_pairs={{0,16},{1,257},{2,18},{3,259},{4,20},{5,261},{6,22},{7,263},{8,24}... | collective-permute-start | bytes 1572872 | tf_op jit(solution)/shard_map/ppermute | solution.py:35
  118.5 17.4 %collective-permute-start.13 = (bf16[512,512]{1,0:T(8,128)(2,1)S(1)}, bf16[512,512]{1,0:T(8,128)(2,1)S(1)}, u32[]{:S(2)}, u32[]{:S(2)}) collective-permute-start(bf16[512,512]{1,0:T(8,128)(2,1)S(1)} %copy-done.3), channel_id=1, source_target_pairs={{0,24},{1,385},{2,26},{3,387},{4,28},{5,389},{6,30},{7,391},{8,0},... | collective-permute-start | bytes 1572872 | tf_op jit(solution)/shard_map/ppermute | solution.py:35
  122.5 17.4 %copy-start.4 = (bf16[512,128]{1,0:T(8,128)(2,1)}, bf16[512,128]{1,0:T(8,128)(2,1)S(1)}, u32[]{:S(2)}) copy-start(bf16[512,128]{1,0:T(8,128)(2,1)S(1)} %maximum_select_fusion.adapter_ref) | copy-start | bytes 393220
  122.8 20.7 %copy-start.16 = (s32[16]{0:T(128)S(1)}, s32[16]{0:T(128)}, u32[]{:S(2)}) copy-start(s32[16]{0:T(128)} %constant.106.clone) | copy-start | bytes 196
  122.9 20.7 %copy-start.17 = (s32[16]{0:T(128)S(1)}, s32[16]{0:T(128)}, u32[]{:S(2)}) copy-start(s32[16]{0:T(128)} %constant.107.clone) | copy-start | bytes 196
  122.9 20.7 %copy-start.18 = (pred[16]{0:T(512)(128)(4,1)S(1)}, pred[16]{0:T(512)(128)(4,1)}, u32[]{:S(2)}) copy-start(pred[16]{0:T(512)(128)(4,1)} %constant.119) | copy-start | bytes 52
  122.9 20.7 %copy-start.19 = (s32[16]{0:T(128)S(1)}, s32[16]{0:T(128)}, u32[]{:S(2)}) copy-start(s32[16]{0:T(128)} %constant.120) | copy-start | bytes 196
  122.9 20.7 %copy-start.20 = (s32[16]{0:T(128)S(1)}, s32[16]{0:T(128)}, u32[]{:S(2)}) copy-start(s32[16]{0:T(128)} %constant.121) | copy-start | bytes 196
  124.2 11.7 %collective-permute-start.15 = (f32[128,256]{1,0:T(8,128)S(1)}, f32[128,256]{1,0:T(8,128)S(1)}, u32[]{:S(2)}, u32[]{:S(2)}) collective-permute-start(f32[128,256]{1,0:T(8,128)S(1)} %pad_maximum_fusion), channel_id=1, source_target_pairs={{0,32},{32,0},{64,96},{96,64},{128,160},{160,128},{192,224},{224,1... | collective-permute-start | bytes 393224 | tf_op jit(solution)/shard_map/ppermute | solution.py:71
  135.9 0.8 copy-start.7
  135.9 1.0 copy-start.8
  136.9 0.8 copy-start.9
  139.9 8.5 %collective-permute-start.16 = (bf16[2048,256]{1,0:T(8,128)(2,1)}, bf16[2048,256]{1,0:T(8,128)(2,1)S(1)}, u32[]{:S(2)}, u32[]{:S(2)}) collective-permute-start(bf16[2048,256]{1,0:T(8,128)(2,1)} %give.1), channel_id=1, source_target_pairs={{0,1},{1,0},{2,3},{3,2},{4,5},{5,4},{6,7},{7,6},{8,9},{9,8},{10,11... | collective-permute-start | bytes 3145736 | tf_op jit(solution)/shard_map/ppermute | solution.py:71
  144.2 13.2 %collective-permute-start.17 = (f32[128,256]{1,0:T(8,128)S(1)}, f32[128,256]{1,0:T(8,128)S(1)}, u32[]{:S(2)}, u32[]{:S(2)}) collective-permute-start(f32[128,256]{1,0:T(8,128)S(1)} %fusion.14), channel_id=1, source_target_pairs={{0,64},{32,96},{64,0},{96,32},{128,192},{160,224},{192,128},{224,1... | collective-permute-start | bytes 393224 | tf_op jit(solution)/shard_map/ppermute | solution.py:71
  148.5 1.0 copy-start.21
  157.4 4.2 %collective-permute-start.18 = (f32[512,256]{1,0:T(8,128)}, f32[512,256]{1,0:T(8,128)S(1)}, u32[]{:S(2)}, u32[]{:S(2)}) collective-permute-start(f32[512,256]{1,0:T(8,128)} %get-tuple-element.43), channel_id=1, source_target_pairs={{0,1},{1,0},{2,3},{3,2},{4,5},{5,4},{6,7},{7,6},{8,9},{9,8},{10,11... | collective-permute-start | bytes 1572872 | tf_op jit(solution)/shard_map/ppermute | solution.py:71
  159.5 7.9 %collective-permute-start.19 = (f32[128,256]{1,0:T(8,128)S(1)}, f32[128,256]{1,0:T(8,128)S(1)}, u32[]{:S(2)}, u32[]{:S(2)}) collective-permute-start(f32[128,256]{1,0:T(8,128)S(1)} %add.77), channel_id=1, source_target_pairs={{0,128},{32,160},{64,192},{96,224},{128,0},{160,32},{192,64},{224,... | collective-permute-start | bytes 393224 | tf_op jit(solution)/shard_map/ppermute | solution.py:71
  161.7 0.8 copy-start.6
  167.4 6.5 %collective-permute-start.20 = (f32[512,128]{1,0:T(8,128)}, f32[512,128]{1,0:T(8,128)S(1)}, u32[]{:S(2)}, u32[]{:S(2)}) collective-permute-start(f32[512,128]{1,0:T(8,128)} %get-tuple-element.51), channel_id=1, source_target_pairs={{0,1},{1,0},{2,3},{3,2},{4,5},{5,4},{6,7},{7,6},{8,9},{9,8},{10,11... | collective-permute-start | bytes 786440 | tf_op jit(solution)/shard_map/ppermute | solution.py:71
  170.0 12.8 %collective-permute-start.22 = (f32[128,256]{1,0:T(8,128)S(1)}, f32[128,256]{1,0:T(8,128)S(1)}, u32[]{:S(2)}, u32[]{:S(2)}) collective-permute-start(f32[128,256]{1,0:T(8,128)S(1)} %add.78), channel_id=1, source_target_pairs={{0,256},{32,288},{64,320},{96,352},{128,384},{160,416},{192,448},{... | collective-permute-start | bytes 393224 | tf_op jit(solution)/shard_map/ppermute | solution.py:71
  173.9 0.7 copy-start.12
  176.6 13.7 %collective-permute-start.21 = (bf16[256,128]{1,0:T(8,128)(2,1)}, bf16[256,128]{1,0:T(8,128)(2,1)S(1)}, u32[]{:S(2)}, u32[]{:S(2)}) collective-permute-start(bf16[256,128]{1,0:T(8,128)(2,1)} %get-tuple-element.53), channel_id=1, source_target_pairs={{0,2},{2,0},{4,6},{6,4},{8,10},{10,8},{12,14},{14,12},{16,18},{18,... | collective-permute-start | bytes 196616 | tf_op jit(solution)/shard_map/ppermute | solution.py:71
  190.3 0.6 copy-start.15

commit v4 on v3

--- a/solution.py
+++ b/solution.py
@@ -12,7 +12,6 @@
 HEAD_WIDTH = 128
 SIDE = 4
 SEGMENT_MOST = 128
-JOIN_WEIGHT = 96 << 20
 
 adapter_scale = 2.0
 
@@ -144,25 +143,6 @@
     return jnp.concatenate(jnp.split(array, n, axis=1), axis=0)
 
 
-def joined_kernel(low_ref, high_ref, out_ref):
-    n = low_ref.shape[0]
-    out_ref[:n] = low_ref[...]
-    out_ref[n:] = high_ref[...]
-
-
-def joined(low, high):
-    n, width = low.shape
-    vmem = pl.BlockSpec(memory_space=pltpu.VMEM)
-    return pl.pallas_call(
-        joined_kernel,
-        out_shape=jax.ShapeDtypeStruct((2 * n, width), BF16),
-        in_specs=[vmem] * 2,
-        out_specs=vmem,
-        cost_estimate=pl.CostEstimate(flops=0, bytes_accessed=JOIN_WEIGHT, transcendentals=0),
-        name="joined",
-    )(low, high)
-
-
 def ride_sum_kernel(rows, stack_ref, out_ref, rides, sems):
     n_ride = rides.shape[1]
     copies = []
@@ -271,56 +251,59 @@
     )(place, quarter, *arrays)
 
 
-def frozen_kernel(n_held, parts, core_ref, order_ref, *refs):
+def frozen_kernel(n_held, parts, core_ref, place_ref, *refs):
     sources, (mine, other, own, came, sems) = refs[:-5], refs[-5:]
     rows, cols = mine.shape
-    width = own.shape[1]
-    blocks = own.shape[0] // rows
+    blocks = len(parts) // 2
+    width = own.shape[1] // blocks
     columns = pl.ds(pl.multiple_of(core_ref[0] * width, width), width)
-    copies, at = [], 0
+    copies = []
     for i, (which, row) in enumerate(parts):
-        target = (own if i < blocks else came).at[pl.ds(i % blocks * rows, rows)]
+        if i < blocks:
+            target = own.at[:, pl.ds(i * width, width)]
+        else:
+            at = pl.multiple_of(place_ref[i - blocks] * width, width)
+            target = came.at[:, pl.ds(at, width)]
         source = sources[which].at[pl.ds(row, rows), columns if which < n_held else pl.ds(0, width)]
         copies.append(pltpu.make_async_copy(source, target, sems.at[i]))
     for copy in copies[blocks:] + copies[:blocks]:
         copy.start()
     for copy in copies[blocks:]:
         copy.wait()
-
-    def matched(i):
-        return came[pl.ds(pl.multiple_of(order_ref[i] * rows, rows), rows)]
-
-    def held(i):
-        copies[i].wait()
-        return own[i * rows : (i + 1) * rows]
-
-    def product(left, right):
-        return lax.dot_general(left, right, NT, preferred_element_type=F32)
+    together = blocks // 4
+
+    def total(first, second):
+        result = None
+        for i in range(0, blocks, together):
+            for copy in copies[i : i + together]:
+                copy.wait()
+            depth = slice(i * width, (i + together) * width)
+            term = lax.dot_general(
+                first[:, depth], second[:, depth], NT, preferred_element_type=F32
+            )
+            result = term if result is None else result + term
+        return result
 
     @pl.when(core_ref[0] == 0)
     def _():
-        total = product(held(0), matched(0))
-        for i in range(1, blocks):
-            total = total + product(held(i), matched(i))
-        mine[...] = total[:, :cols]
-        other[...] = total[:, cols:]
+        product = total(own, came)
+        mine[...] = product[:, :cols]
+        other[...] = product[:, cols:]
 
     @pl.when(core_ref[0] == 1)
     def _():
-        total = product(matched(0), held(0))
-        for i in range(1, blocks):
-            total = total + product(matched(i), held(i))
-        mine[...] = total[:, cols:]
-        other[...] = total[:, :cols]
-
-
-def frozen_product(core, order, own, came, rows):
+        product = total(came, own)
+        mine[...] = product[:, cols:]
+        other[...] = product[:, :cols]
+
+
+def frozen_product(core, place, own, came, rows):
     arrays = [a for a, _ in (*own, *came)]
     parts = []
     for i, (a, step) in enumerate((*own, *came)):
         parts += [(i, at) for at in range(0, a.shape[0] - rows + 1, step)]
     width = came[0][0].shape[1]
-    held = pltpu.VMEM((len(parts) // 2 * rows, width), BF16)
+    held = pltpu.VMEM((rows, len(parts) // 2 * width), BF16)
     return pl.pallas_call(
         functools.partial(frozen_kernel, len(own), parts),
         out_shape=(jax.ShapeDtypeStruct((rows, rows // 2), F32),) * 2,
@@ -330,10 +313,10 @@
         scratch_shapes=[held, held, pltpu.SemaphoreType.DMA((len(parts),))],
         compiler_params=pltpu.CompilerParams(vmem_limit_bytes=56 * 1024 * 1024),
         cost_estimate=pl.CostEstimate(
-            flops=4 * rows * held.shape[0] * width, bytes_accessed=24 << 20, transcendentals=0
+            flops=4 * rows * rows * held.shape[1], bytes_accessed=24 << 20, transcendentals=0
         ),
         name="frozen",
-    )(core, order, *arrays)
+    )(core, place, *arrays)
 
 
 def block_order(core, dp, tensor):
@@ -392,26 +375,37 @@
     labels = label_ref[...].astype(F32)
     ahead = lax.broadcasted_iota(jnp.int32, (rows, 2 * rows), 0)
     ahead = ahead - lax.broadcasted_iota(jnp.int32, (rows, 2 * rows), 1)
+    tiles = [(i, h) for i in range(q_ref.shape[0] // rows) for h in range(band_ref.shape[0])]
+    scores = {}
+    for i, h in tiles:
+        at, low = i * rows, window(i, rows)
+        scores[i, h] = lax.dot_general(
+            q_ref[at : at + rows, h * head : (h + 1) * head],
+            k_ref[low : low + 2 * rows],
+            NT,
+            preferred_element_type=F32,
+        )
+    allowed = {}
     for i in range(q_ref.shape[0] // rows):
         at, low = i * rows, window(i, rows)
         own = jnp.broadcast_to(labels[:, at : at + rows], (rows, rows)).T
         own = jnp.concatenate([own, own], axis=1)
-        allowed = (ahead >= low - at) & (own == labels[:, low : low + 2 * rows])
-        for h in range(band_ref.shape[0]):
-            cols = slice(h * head, (h + 1) * head)
-            scores = lax.dot_general(
-                q_ref[at : at + rows, cols],
-                k_ref[low : low + 2 * rows],
-                NT,
-                preferred_element_type=F32,
-            )
-            scores = jnp.where(allowed, scores * scale, -jnp.inf)
-            probs = jnp.exp(scores - jnp.max(scores, axis=1, keepdims=True))
-            probs = probs / jnp.sum(probs, axis=1, keepdims=True)
-            band_ref[h, at : at + rows] = probs
-            out_ref[at : at + rows, cols] = jnp.dot(
-                probs.astype(BF16), v_ref[low : low + 2 * rows], preferred_element_type=F32
-            ).astype(BF16)
+        allowed[i] = (ahead >= low - at) & (own == labels[:, low : low + 2 * rows])
+    probs = {}
+    for i, h in tiles:
+        masked = jnp.where(allowed[i], scores[i, h] * scale, -jnp.inf)
+        raised = jnp.exp(masked - jnp.max(masked, axis=1, keepdims=True))
+        probs[i, h] = raised / jnp.sum(raised, axis=1, keepdims=True)
+    outs = {}
+    for i, h in tiles:
+        low = window(i, rows)
+        outs[i, h] = jnp.dot(
+            probs[i, h].astype(BF16), v_ref[low : low + 2 * rows], preferred_element_type=F32
+        ).astype(BF16)
+    for i, h in tiles:
+        at = i * rows
+        band_ref[h, at : at + rows] = probs[i, h]
+        out_ref[at : at + rows, h * head : (h + 1) * head] = outs[i, h]
     inner = lax.dot_general(out_ref[...], lower_ref[...], NT, preferred_element_type=F32)
     inner_ref[...] = inner
     inner = jnp.split(inner.astype(BF16), 2 * width // rank, axis=0)
@@ -450,51 +444,75 @@
 ):
     rows = band_ref.shape[2] // 2
     head = k_ref.shape[1]
-    key_sum[...] = jnp.zeros_like(key_sum)
-    value_sum[...] = jnp.zeros_like(value_sum)
-    for i in range(q_ref.shape[0] // rows):
-        at, low = i * rows, window(i, rows)
-        part, seen = slice(at, at + rows), slice(low, low + 2 * rows)
-        adapter = adapter_ref[part, lower_ref.shape[0] :]
-        lora = jnp.dot(adapter, lower_ref[...], preferred_element_type=F32)
-        gradient = (mine_ref[part] + came_ref[part] + adapter_scale * lora).astype(BF16)
-        for h in range(band_ref.shape[0]):
-            cols = slice(h * head, (h + 1) * head)
-            own = gradient[:, cols]
-            probs = band_ref[h, part]
-            terms = jnp.sum(
-                own.astype(F32) * out_ref[part, cols].astype(F32), axis=1, keepdims=True
-            )
-            prob_grad = lax.dot_general(own, v_ref[seen], NT, preferred_element_type=F32)
-            score_grad = (probs * (prob_grad - terms)).astype(BF16)
-            query_grad = jnp.dot(score_grad, k_ref[seen], preferred_element_type=F32)
-            query_ref[part, cols] = (scale * query_grad).astype(BF16)
-            key_sum[seen] += lax.dot_general(
-                score_grad, q_ref[part, cols], TN, preferred_element_type=F32
-            )
-            value_sum[seen] += lax.dot_general(
-                probs.astype(BF16), own, TN, preferred_element_type=F32
-            )
+    n = q_ref.shape[0] // rows
+    tiles = [(i, h) for i in range(n) for h in range(band_ref.shape[0])]
+
+    def part(i):
+        return slice(i * rows, (i + 1) * rows)
+
+    def seen(i):
+        return slice(window(i, rows), window(i, rows) + 2 * rows)
+
+    def cols(h):
+        return slice(h * head, (h + 1) * head)
+
+    adapter = adapter_ref[:, lower_ref.shape[0] :]
+    lora = jnp.dot(adapter, lower_ref[...], preferred_element_type=F32)
+    gradient = (mine_ref[...] + came_ref[...] + adapter_scale * lora).astype(BF16)
+    own = {(i, h): gradient[part(i), cols(h)] for i, h in tiles}
+    prob_grad, terms, score_grad = {}, {}, {}
+    for i, h in tiles:
+        prob_grad[i, h] = lax.dot_general(
+            own[i, h], v_ref[seen(i)], NT, preferred_element_type=F32
+        )
+    for i, h in tiles:
+        product = own[i, h].astype(F32) * out_ref[part(i), cols(h)].astype(F32)
+        terms[i, h] = jnp.sum(product, axis=1, keepdims=True)
+    probs = {(i, h): band_ref[h, part(i)] for i, h in tiles}
+    for i, h in tiles:
+        score_grad[i, h] = (probs[i, h] * (prob_grad[i, h] - terms[i, h])).astype(BF16)
+    for i, h in tiles:
+        query_grad = jnp.dot(score_grad[i, h], k_ref[seen(i)], preferred_element_type=F32)
+        query_ref[part(i), cols(h)] = (scale * query_grad).astype(BF16)
+    for j in range(n):
+        sees = [(j, 0 if j == 0 else 1)] + [(i, 0) for i in (j + 1,) if i < n]
+        key_total, value_total = None, None
+        for i, side in sees:
+            for h in range(band_ref.shape[0]):
+                key_part = lax.dot_general(
+                    q_ref[part(i), cols(h)], score_grad[i, h][:, part(side)], TN,
+                    preferred_element_type=F32,
+                )
+                value_part = lax.dot_general(
+                    own[i, h], probs[i, h][:, part(side)].astype(BF16), TN,
+                    preferred_element_type=F32,
+                )
+                key_total = key_part if key_total is None else key_total + key_part
+                value_total = value_part if value_total is None else value_total + value_part
+        key_sum[:, part(j)] = key_total
+        value_sum[:, part(j)] = value_total
     quarter = head // 4
+    first = core_ref[0] == 0
     for source, factor, at in ((key_sum, scale, 0), (value_sum, None, 2 * quarter)):
         total = source[...] if factor is None else source[...] * factor
-        even = jnp.concatenate([total[:, :quarter], total[:, 2 * quarter : 3 * quarter]], axis=1)
-        odd = jnp.concatenate([total[:, quarter : 2 * quarter], total[:, 3 * quarter :]], axis=1)
-        first = core_ref[0] == 0
-        keep_ref[:, at : at + 2 * quarter] = jnp.where(first, even, odd)
-        give_ref[:, at : at + 2 * quarter] = jnp.where(first, odd, even)
+        for i in (0, 1):
+            even = total[2 * i * quarter : (2 * i + 1) * quarter]
+            odd = total[(2 * i + 1) * quarter : (2 * i + 2) * quarter]
+            rows = slice(at + i * quarter, at + (i + 1) * quarter)
+            keep_ref[rows] = jnp.where(first, even, odd)
+            give_ref[rows] = jnp.where(first, odd, even)
 
 
 def backward(core, mine, came, adapter, lower, band, out, queries, key_head, value_head):
     n, width = queries.shape
-    half = jax.ShapeDtypeStruct((n, HEAD_WIDTH), F32)
+    half = jax.ShapeDtypeStruct((HEAD_WIDTH, n), F32)
     return pl.pallas_call(
         functools.partial(backward_kernel, HEAD_WIDTH**-0.5),
         out_shape=(jax.ShapeDtypeStruct((n, width), BF16), half, half),
         in_specs=[pl.BlockSpec(memory_space=pltpu.SMEM)]
         + [pl.BlockSpec(memory_space=pltpu.VMEM)] * 9,
         out_specs=(pl.BlockSpec(memory_space=pltpu.VMEM),) * 3,
-        scratch_shapes=[pltpu.VMEM((n, HEAD_WIDTH), F32)] * 2,
+        scratch_shapes=[pltpu.VMEM((HEAD_WIDTH, n), F32)] * 2,
         cost_estimate=pl.CostEstimate(
             flops=20 * n * width * 2 * SEGMENT_MOST, bytes_accessed=16 << 20, transcendentals=0
         ),
@@ -503,14 +521,15 @@
 
 
 def quarters_kernel(chip_ref, keep_ref, came_ref, out_ref, give_ref):
-    total = keep_ref[...] + came_ref[...]
-    n, quarter = total.shape[0] // 2, total.shape[1] // 4
-    even = jnp.concatenate([total[:, :quarter], total[:, 2 * quarter : 3 * quarter]], axis=1)
-    odd = jnp.concatenate([total[:, quarter : 2 * quarter], total[:, 3 * quarter :]], axis=1)
+    quarter = keep_ref.shape[0] // 4
     first = chip_ref[0] == 0
-    out_ref[...] = jnp.where(first, even, odd)
-    give = jnp.where(first, odd, even).astype(BF16)
-    give_ref[...] = jnp.concatenate([give[:n], give[n:]], axis=1)
+    for i in (0, 1):
+        at = 2 * i * quarter
+        even = keep_ref[at : at + quarter] + came_ref[at : at + quarter]
+        odd = keep_ref[at + quarter : at + 2 * quarter] + came_ref[at + quarter : at + 2 * quarter]
+        rows = slice(i * quarter, (i + 1) * quarter)
+        out_ref[rows] = jnp.where(first, even, odd)
+        give_ref[rows] = jnp.where(first, odd, even).astype(BF16)
 
 
 def quarters_kept(chip, keep, came):
@@ -518,7 +537,7 @@
     return pl.pallas_call(
         quarters_kernel,
         out_shape=(
-            jax.ShapeDtypeStruct((n, width // 2), F32),
+            jax.ShapeDtypeStruct((n // 2, width), F32),
             jax.ShapeDtypeStruct((n // 2, width), BF16),
         ),
         in_specs=[pl.BlockSpec(memory_space=pltpu.SMEM)]
@@ -526,27 +545,6 @@
         out_specs=(pl.BlockSpec(memory_space=pltpu.VMEM),) * 2,
         name="quarters",
     )(chip, keep, came)
-
-
-def rounded_sum_kernel(keep_ref, came_ref, key_ref, value_ref):
-    came = came_ref[...].astype(F32)
-    quarter = key_ref.shape[0]
-    came = jnp.concatenate([came[:, : 2 * quarter], came[:, 2 * quarter :]], axis=0)
-    total = (keep_ref[...] + came).T.astype(BF16)
-    key_ref[...] = total[:quarter]
-    value_ref[...] = total[quarter:]
-
-
-def rounded_sum(keep, came):
-    n, width = keep.shape
-    vmem = pl.BlockSpec(memory_space=pltpu.VMEM)
-    return pl.pallas_call(
-        rounded_sum_kernel,
-        out_shape=(jax.ShapeDtypeStruct((width // 2, n), BF16),) * 2,
-        in_specs=[vmem] * 2,
-        out_specs=(vmem,) * 2,
-        name="rounded_sum",
-    )(keep, came)
 
 
 def on_device(
@@ -611,7 +609,7 @@
     quarter = ((quarter.astype(F32) + from_z[1]) + (from_z[0] + from_z[2])).astype(BF16)
     low = near_move(jnp.where(upper_core, block[:half], z1[:half]), 1, 3)
     high = near_move(jnp.where(upper_core, block[half:], z2[half:]), 3, 3)
-    last = joined(low, high)
+    last = jnp.concatenate([low, high], axis=0)
     near = jnp.concatenate([z1, z2, widened(quarter, SIDE)], axis=0)
     near_far = [far_move(near, k) for k in (1, 2, 3)]
     give, sums = give_near(
@@ -638,7 +636,7 @@
 
     part_mine, part_other = frozen_product(
         core_ref,
-        block_order(core, dp, tensor),
+        block_order(1 - core, dp, tensor),
         [(own_far, own_far.shape[0] // SIDE)]
         + [(a, seq_len) for a in (z1, z2, *near_far, last, *last_far)],
         [(came_near, seq_len), (came_last, seq_len)],
@@ -667,8 +665,9 @@
     factor = factor + after(from_dp, give)
     factor = factor * (adapter_scale / lax.axis_size("dp"))
     lower_gradient, upper_gradient = factor[:rank].T, factor[rank:]
-    key_grad, value_grad = rounded_sum(keep, came)
-    key_grad, value_grad = key_grad.T[None], value_grad.T[None]
+    total = (keep + came.astype(F32)).astype(BF16)
+    quarter = head_size // 4
+    key_grad, value_grad = total[:quarter].T[None], total[quarter:].T[None]
     query_grad = query_grad[None]
     return (query_grad, key_grad, value_grad, lower_gradient, upper_gradient)
 

time: 194 us -> 189 us (0.974)
  waiting for transfers between devices: 53.2 us -> 60.1 us
  Pallas kernels: 34.3 us -> 28 us
  starting transfers between devices: 89.7 us -> 85.2 us
    ppermute x10, waiting for transfers between devices: 29.5 us -> 34.4 us  [moved(): return lax.ppermute(array, AXES, pairs)]
    pallas_call x3 -> x1, Pallas kernels: 5.55 us -> 1.73 us  [quarters_kept(): pl.pallas_call(quarters_kernel, out_shape=(jax.ShapeDtypeStruct((n // 2,...]
    ppermute x10, starting transfers between devices: 51.7 us -> 49.4 us  [swapped(): lax.ppermute(array, axis, [(i, i ^ mask) for i in range(lax.axis_size(axi...]
    unnamed x44 -> x39, local copies, waits for them, and re-layouts: 7.81 us -> 5.57 us
    ppermute x10, starting transfers between devices: 32.4 us -> 30.2 us  [moved(): return lax.ppermute(array, AXES, pairs)]
    ppermute x10, waiting for transfers between devices: 11.3 us -> 13.2 us  [swapped(): lax.ppermute(array, axis, [(i, i ^ mask) for i in range(lax.axis_size(axi...]
  transfers between devices with their start and end apart: 24 -> 24, of which waited for: 9 -> 12; matrix products, arithmetic and copies ran while one was open for 3% -> 3% of each run, Pallas kernels for 9% -> 7%
where the time goes in v4:
time: 189 us; the launch traced here: 188 us
  starting transfers between devices  85.2 us (45%)
  waiting for transfers between devices  60.1 us (32%)
  Pallas kernels  28 us (15%)
  local copies, waits for them, and re-layouts  7.77 us (4%)
  other arithmetic  4.12 us (2%)
    ppermute x10, starting transfers between devices, swapped(): lax.ppermute(array, axis, [(i, i ^ mask) for i in range(lax.axis_size(axi...  49.4 us
    ppermute x10, waiting for transfers between devices, moved(): return lax.ppermute(array, AXES, pairs)  34.4 us
    ppermute x10, starting transfers between devices, moved(): return lax.ppermute(array, AXES, pairs)  30.2 us
    ppermute x10, waiting for transfers between devices, swapped(): lax.ppermute(array, axis, [(i, i ^ mask) for i in range(lax.axis_size(axi...  13.2 us
    all_to_all x1, waiting for transfers between devices, spread(): lax.all_to_all(stacked, axes, 0, 0, axis_index_groups=groups, tiled=True)  12.5 us
    pallas_call x1, Pallas kernels, frozen_product(): pl.pallas_call(functools.partial(frozen_kernel, len(own), parts), out_sha...  7.26 us
    unnamed x39, local copies, waits for them, and re-layouts  5.57 us
    pallas_call x1, Pallas kernels, give_near(): pl.pallas_call(functools.partial(give_near_kernel, parts, at_ride), out_s...  4.51 us
  transfers between devices with their start and end apart: 24, of which 12 were waited for; matrix products, arithmetic and copies ran while one was open for 3% of the time, Pallas kernels for 7%

profile of v4, /device:TPU:1, one launch (start us, length us, event | category | flops | bytes accessed | tf_op | source)
XLA Modules:
  0.0 188.1 jit_solution(3198027665437646216)
XLA Ops:
  0.7 0.6 pad_add_fusion.place_ref
  1.2 4.4 %attention.1 = (f32[2,512,256]{2,1,0:T(8,128)}, bf16[512,256]{1,0:T(8,128)(2,1)}, f32[512,64]{1,0:T(8,128)}, bf16[512,128]{1,0:T(8,128)(2,1)}, bf16[512,128]{1,0:T(8,128)(2,1)}, /*index=5*/bf16[416,512]{1,0:T(8,128)(2,1)}) custom-call(s32[3]{0:T(128)} %pad_add_fusion.place_ref, bf16[512,256]{1,0:T(8,128)(2,1)} %bitcast.28, s32[1,512]{1,0:T(1,128)} %label_ref.1, ...), custom_call_target="tpu_custom_call" | custom-call | tf_op jit(solution)/shard_map/attention/pallas_call | solution.py:424
  5.6 8.8 %collective-permute-start = (bf16[416,512]{1,0:T(8,128)(2,1)}, bf16[416,512]{1,0:T(8,128)(2,1)S(1)}, u32[]{:S(2)}, u32[]{:S(2)}) collective-permute-start(bf16[416,512]{1,0:T(8,128)(2,1)} %get-tuple-element.29), channel_id=1, source_target_pairs={{0,1},{1,0},{2,3},{3,2},{4,5},{5,4},{6,7},{7,6},{8,9},{9,8},{10,11... | collective-permute-start | bytes 1277960 | tf_op jit(solution)/shard_map/ppermute | solution.py:70
  14.4 1.6 collective-permute-done.came_ref
  16.0 0.8 copy-done.10
  16.8 3.0 %blend.1 = (bf16[512,512]{1,0:T(8,128)(2,1)}, f32[512,128]{1,0:T(8,128)}, bf16[2176,512]{1,0:T(8,128)(2,1)}) custom-call(s32[3]{0:T(128)} %pad_add_fusion.place_ref, s32[1,128]{1,0:T(1,128)} %tapped_ref.1, bf16[256,512]{1,0:T(8,128)(2,1)} %bitcast.31, bf16[64,512]{1,0:T(8,128)(2,1)} %bitcast.35, bf16[64,256]{1,0:T(8,128)(2,1)} %upper_ref.3, ...), custom_call_target="tpu_custom_call" | custom-call | tf_op jit(solution)/shard_map/blend/pallas_call | solution.py:125
  19.8 3.6 %all-to-all-start = ((bf16[4,544,512]{2,1,0:T(8,128)(2,1)}), bf16[4,544,512]{2,1,0:T(8,128)(2,1)S(1)}, u32[]{:S(2)}, u32[]{:S(2)}) async-start(bf16[4,544,512]{2,1,0:T(8,128)(2,1)} %bitcast.27), calls=%async_computation | async-start | bytes 4456448 | tf_op jit(solution)/shard_map/all_to_all | solution.py:38
  23.4 1.9 %collective-permute-start.1 = (bf16[512,512]{1,0:T(8,128)(2,1)}, bf16[512,512]{1,0:T(8,128)(2,1)S(1)}, u32[]{:S(2)}, u32[]{:S(2)}) collective-permute-start(bf16[512,512]{1,0:T(8,128)(2,1)} %get-tuple-element.32), channel_id=1, source_target_pairs={{0,2},{1,33},{2,4},{3,35},{4,6},{5,37},{6,0},{7,39},{8,10},{9,41},... | collective-permute-start | bytes 1572872 | tf_op jit(solution)/shard_map/ppermute | solution.py:34
  25.3 1.9 %collective-permute-start.2 = (bf16[512,512]{1,0:T(8,128)(2,1)}, bf16[512,512]{1,0:T(8,128)(2,1)S(1)}, u32[]{:S(2)}, u32[]{:S(2)}) collective-permute-start(bf16[512,512]{1,0:T(8,128)(2,1)} %get-tuple-element.32), channel_id=1, source_target_pairs={{0,6},{1,65},{2,0},{3,67},{4,2},{5,69},{6,4},{7,71},{8,14},{9,73},... | collective-permute-start | bytes 1572872 | tf_op jit(solution)/shard_map/ppermute | solution.py:34
  27.2 12.5 %all-to-all-done = bf16[4,544,512]{2,1,0:T(8,128)(2,1)S(1)} async-done(((bf16[4,544,512]{2,1,0:T(8,128)(2,1)}), bf16[4,544,512]{2,1,0:T(8,128)(2,1)S(1)}, u32[]{:S(2)}, u32[]{:S(2)}) %all-to-all-start) | async-done | bytes 2228256 | tf_op jit(solution)/shard_map/all_to_all | solution.py:38
  39.7 1.4 copy-done
  41.1 1.5 ride_sum.1
  42.6 0.7 collective-permute-start.3
  43.3 0.7 collective-permute-start.4
  44.0 0.7 collective-permute-start.5
  44.7 0.8 add_convert_fusion.1.quarter_ref
  45.5 19.4 %collective-permute-done.2.refs_2_ = bf16[512,512]{1,0:T(8,128)(2,1)S(1)} collective-permute-done((bf16[512,512]{1,0:T(8,128)(2,1)}, bf16[512,512]{1,0:T(8,128)(2,1)S(1)}, u32[]{:S(2)}, u32[]{:S(2)}) %collective-permute-start.2) | collective-permute-done | bytes 524320 | tf_op jit(solution)/shard_map/ppermute | solution.py:34
  64.9 0.1 maximum_maximum_fusion
  65.0 3.5 %collective-permute-start.6 = (bf16[1056,512]{1,0:T(8,128)(2,1)S(1)}, bf16[1056,512]{1,0:T(8,128)(2,1)}, u32[]{:S(2)}, u32[]{:S(2)}) collective-permute-start(bf16[1056,512]{1,0:T(8,128)(2,1)S(1)} %maximum_maximum_fusion), channel_id=1, source_target_pairs={{0,8},{1,129},{2,10},{3,131},{4,12},{5,133},{6,14},{7,135},{8,16},... | collective-permute-start | bytes 3244040 | tf_op jit(solution)/shard_map/ppermute | solution.py:34
  68.5 4.2 %collective-permute-start.7 = (bf16[1056,512]{1,0:T(8,128)(2,1)S(1)}, bf16[1056,512]{1,0:T(8,128)(2,1)}, u32[]{:S(2)}, u32[]{:S(2)}) collective-permute-start(bf16[1056,512]{1,0:T(8,128)(2,1)S(1)} %maximum_maximum_fusion), channel_id=1, source_target_pairs={{0,16},{1,257},{2,18},{3,259},{4,20},{5,261},{6,22},{7,263},{8,24}... | collective-permute-start | bytes 3244040 | tf_op jit(solution)/shard_map/ppermute | solution.py:34
  72.8 3.1 %collective-permute-start.8 = (bf16[1056,512]{1,0:T(8,128)(2,1)S(1)}, bf16[1056,512]{1,0:T(8,128)(2,1)}, u32[]{:S(2)}, u32[]{:S(2)}) collective-permute-start(bf16[1056,512]{1,0:T(8,128)(2,1)S(1)} %maximum_maximum_fusion), channel_id=1, source_target_pairs={{0,24},{1,385},{2,26},{3,387},{4,28},{5,389},{6,30},{7,391},{8,0},... | collective-permute-start | bytes 3244040 | tf_op jit(solution)/shard_map/ppermute | solution.py:34
  75.9 1.1 slice_select_fusion
  77.0 1.9 %collective-permute-start.9 = (bf16[256,512]{1,0:T(8,128)(2,1)S(1)}, bf16[256,512]{1,0:T(8,128)(2,1)S(1)}, u32[]{:S(2)}, u32[]{:S(2)}) collective-permute-start(bf16[256,512]{1,0:T(8,128)(2,1)S(1)} %get-tuple-element.56), channel_id=1, source_target_pairs={{0,2},{1,97},{2,4},{3,99},{4,6},{5,101},{6,0},{7,103},{8,10},{9,10... | collective-permute-start | bytes 786440 | tf_op jit(solution)/shard_map/ppermute | solution.py:34
  78.9 5.2 %collective-permute-start.10 = (bf16[256,512]{1,0:T(8,128)(2,1)S(1)}, bf16[256,512]{1,0:T(8,128)(2,1)S(1)}, u32[]{:S(2)}, u32[]{:S(2)}) collective-permute-start(bf16[256,512]{1,0:T(8,128)(2,1)S(1)} %get-tuple-element.55), channel_id=1, source_target_pairs={{0,6},{1,97},{2,0},{3,99},{4,2},{5,101},{6,4},{7,103},{8,14},{9,10... | collective-permute-start | bytes 786440 | tf_op jit(solution)/shard_map/ppermute | solution.py:34
  84.1 2.0 %collective-permute-done.9 = bf16[256,512]{1,0:T(8,128)(2,1)S(1)} collective-permute-done((bf16[256,512]{1,0:T(8,128)(2,1)S(1)}, bf16[256,512]{1,0:T(8,128)(2,1)S(1)}, u32[]{:S(2)}, u32[]{:S(2)}) %collective-permute-start.9) | collective-permute-done | bytes 262176 | tf_op jit(solution)/shard_map/ppermute | solution.py:34
  86.1 3.1 %collective-permute-done.10 = bf16[256,512]{1,0:T(8,128)(2,1)S(1)} collective-permute-done((bf16[256,512]{1,0:T(8,128)(2,1)S(1)}, bf16[256,512]{1,0:T(8,128)(2,1)S(1)}, u32[]{:S(2)}, u32[]{:S(2)}) %collective-permute-start.10) | collective-permute-done | bytes 262176 | tf_op jit(solution)/shard_map/ppermute | solution.py:34
  89.3 6.1 %collective-permute-done.7.refs_4_ = bf16[1056,512]{1,0:T(8,128)(2,1)} collective-permute-done((bf16[1056,512]{1,0:T(8,128)(2,1)S(1)}, bf16[1056,512]{1,0:T(8,128)(2,1)}, u32[]{:S(2)}, u32[]{:S(2)}) %collective-permute-start.7) | collective-permute-done | bytes 1081376 | tf_op jit(solution)/shard_map/ppermute | solution.py:34
  95.4 1.4 collective-permute-done.8.refs_5_
  96.7 4.5 %give_near.1 = (bf16[6400,256]{1,0:T(8,128)(2,1)}, bf16[512,128]{1,0:T(8,128)(2,1)}) custom-call(s32[3]{0:T(128)} %pad_add_fusion.place_ref, bf16[128,128]{1,0:T(8,128)(2,1)} %copy-done.11, bf16[2176,512]{1,0:T(8,128)(2,1)} %bitcast.25, bf16[512,512]{1,0:T(8,128)(2,1)} %copy-done.1, bf16[512,512]{1,0:T(8,128)(2,1)} %copy-done.2, ...), custom_call_target="tpu_custom_call" | custom-call | tf_op jit(solution)/shard_map/give_near/pallas_call | solution.py:238
  101.3 17.0 %collective-permute-start.14 = (bf16[6400,256]{1,0:T(8,128)(2,1)}, bf16[6400,256]{1,0:T(8,128)(2,1)}, u32[]{:S(2)}, u32[]{:S(2)}) collective-permute-start(bf16[6400,256]{1,0:T(8,128)(2,1)} %get-tuple-element.34), channel_id=1, source_target_pairs={{0,1},{1,0},{2,3},{3,2},{4,5},{5,4},{6,7},{7,6},{8,9},{9,8},{10,11... | collective-permute-start | bytes 9830408 | tf_op jit(solution)/shard_map/ppermute | solution.py:70
  118.2 1.9 %collective-permute-start.11 = (bf16[512,512]{1,0:T(8,128)(2,1)S(1)}, bf16[512,512]{1,0:T(8,128)(2,1)S(1)}, u32[]{:S(2)}, u32[]{:S(2)}) collective-permute-start(bf16[512,512]{1,0:T(8,128)(2,1)S(1)} %constant_dynamic-update-slice_fusion.refs_0_.refs_6_), channel_id=1, source_target_pairs={{0,8},{1,129},{2,10},{3,131},{4,12},{5,133},{6,14},{7,135},{8,16},... | collective-permute-start | bytes 1572872 | tf_op jit(solution)/shard_map/ppermute | solution.py:34
  120.2 1.9 %collective-permute-start.12 = (bf16[512,512]{1,0:T(8,128)(2,1)S(1)}, bf16[512,512]{1,0:T(8,128)(2,1)S(1)}, u32[]{:S(2)}, u32[]{:S(2)}) collective-permute-start(bf16[512,512]{1,0:T(8,128)(2,1)S(1)} %constant_dynamic-update-slice_fusion.refs_0_.refs_6_), channel_id=1, source_target_pairs={{0,16},{1,257},{2,18},{3,259},{4,20},{5,261},{6,22},{7,263},{8,24}... | collective-permute-start | bytes 1572872 | tf_op jit(solution)/shard_map/ppermute | solution.py:34
  122.1 4.6 %collective-permute-start.13 = (bf16[512,512]{1,0:T(8,128)(2,1)S(1)}, bf16[512,512]{1,0:T(8,128)(2,1)S(1)}, u32[]{:S(2)}, u32[]{:S(2)}) collective-permute-start(bf16[512,512]{1,0:T(8,128)(2,1)S(1)} %constant_dynamic-update-slice_fusion.refs_0_.refs_6_), channel_id=1, source_target_pairs={{0,24},{1,385},{2,26},{3,387},{4,28},{5,389},{6,30},{7,391},{8,0},... | collective-permute-start | bytes 1572872 | tf_op jit(solution)/shard_map/ppermute | solution.py:34
  126.7 0.9 fusion.15
  127.6 0.3 fusion.6
  127.9 0.0 copy-start.13
  127.9 0.0 copy-start.14
  128.0 0.0 copy-start.15
  128.0 1.3 fusion
  129.3 3.0 %collective-permute-start.15 = (f32[128,256]{1,0:T(8,128)S(1)}, f32[128,256]{1,0:T(8,128)S(1)}, u32[]{:S(2)}, u32[]{:S(2)}) collective-permute-start(f32[128,256]{1,0:T(8,128)S(1)} %pad_maximum_fusion), channel_id=1, source_target_pairs={{0,32},{32,0},{64,96},{96,64},{128,160},{160,128},{192,224},{224,1... | collective-permute-start | bytes 393224 | tf_op jit(solution)/shard_map/ppermute | solution.py:70
  132.3 3.0 %collective-permute-done.15 = f32[128,256]{1,0:T(8,128)S(1)} collective-permute-done((f32[128,256]{1,0:T(8,128)S(1)}, f32[128,256]{1,0:T(8,128)S(1)}, u32[]{:S(2)}, u32[]{:S(2)}) %collective-permute-start.15) | collective-permute-done | bytes 131104 | tf_op jit(solution)/shard_map/ppermute | solution.py:70
  135.3 2.5 %collective-permute-done.13.refs_3_.refs_9_ = bf16[512,512]{1,0:T(8,128)(2,1)S(1)} collective-permute-done((bf16[512,512]{1,0:T(8,128)(2,1)S(1)}, bf16[512,512]{1,0:T(8,128)(2,1)S(1)}, u32[]{:S(2)}, u32[]{:S(2)}) %collective-permute-start.13) | collective-permute-done | bytes 524320 | tf_op jit(solution)/shard_map/ppermute | solution.py:34
  137.8 0.8 copy-done.9
  138.6 2.2 %give.1 = bf16[2048,256]{1,0:T(8,128)(2,1)} custom-call(s32[1]{0:T(128)} %bitcast.core_ref, bf16[512,512]{1,0:T(8,128)(2,1)} %copy-done.4, bf16[512,512]{1,0:T(8,128)(2,1)} %copy-done.7, bf16[512,512]{1,0:T(8,128)(2,1)} %copy-done.8, bf16[512,512]{1,0:T(8,128)(2,1)} %copy-done.9), custom_call_target="tpu_custom_call" | custom-call | tf_op jit(solution)/shard_map/give/pallas_call | solution.py:197
  140.8 3.7 %collective-permute-start.16 = (bf16[2048,256]{1,0:T(8,128)(2,1)}, bf16[2048,256]{1,0:T(8,128)(2,1)S(1)}, u32[]{:S(2)}, u32[]{:S(2)}) collective-permute-start(bf16[2048,256]{1,0:T(8,128)(2,1)} %give.1), channel_id=1, source_target_pairs={{0,1},{1,0},{2,3},{3,2},{4,5},{5,4},{6,7},{7,6},{8,9},{9,8},{10,11... | collective-permute-start | bytes 3145736 | tf_op jit(solution)/shard_map/ppermute | solution.py:70
  144.6 0.5 compare_select_fusion.10.place_ref
  145.1 1.9 %collective-permute-start.17 = (f32[128,256]{1,0:T(8,128)S(1)}, f32[128,256]{1,0:T(8,128)S(1)}, u32[]{:S(2)}, u32[]{:S(2)}) collective-permute-start(f32[128,256]{1,0:T(8,128)S(1)} %fusion.14), channel_id=1, source_target_pairs={{0,64},{32,96},{64,0},{96,32},{128,192},{160,224},{192,128},{224,1... | collective-permute-start | bytes 393224 | tf_op jit(solution)/shard_map/ppermute | solution.py:70
  147.1 1.0 copy-done.18
  148.0 7.3 %frozen.1 = (f32[512,256]{1,0:T(8,128)}, f32[512,256]{1,0:T(8,128)}) custom-call(s32[1]{0:T(128)} %bitcast.core_ref, s32[16]{0:T(128)} %compare_select_fusion.10.place_ref, bf16[2176,512]{1,0:T(8,128)(2,1)} %bitcast.26, bf16[512,512]{1,0:T(8,128)(2,1)} %copy-done.1, bf16[512,512]{1,0:T(8,128)(2,1)} %copy-done.2, ...), custom_call_target="tpu_custom_call" | custom-call | flops 4294967296 | bytes 25165824 | tf_op jit(solution)/shard_map/frozen/pallas_call | solution.py:307
  155.3 0.3 collective-permute-done.17
  155.7 2.3 %collective-permute-start.18 = (f32[512,256]{1,0:T(8,128)}, f32[512,256]{1,0:T(8,128)S(1)}, u32[]{:S(2)}, u32[]{:S(2)}) collective-permute-start(f32[512,256]{1,0:T(8,128)} %get-tuple-element.41), channel_id=1, source_target_pairs={{0,1},{1,0},{2,3},{3,2},{4,5},{5,4},{6,7},{7,6},{8,9},{9,8},{10,11... | collective-permute-start | bytes 1572872 | tf_op jit(solution)/shard_map/ppermute | solution.py:70
  158.0 1.9 %collective-permute-start.19 = (f32[128,256]{1,0:T(8,128)S(1)}, f32[128,256]{1,0:T(8,128)S(1)}, u32[]{:S(2)}, u32[]{:S(2)}) collective-permute-start(f32[128,256]{1,0:T(8,128)S(1)} %add.80), channel_id=1, source_target_pairs={{0,128},{32,160},{64,192},{96,224},{128,0},{160,32},{192,64},{224,... | collective-permute-start | bytes 393224 | tf_op jit(solution)/shard_map/ppermute | solution.py:70
  160.0 0.8 copy-done.6
  160.8 3.4 %attention_gradient.1 = (bf16[512,256]{1,0:T(8,128)(2,1)}, f32[128,512]{1,0:T(8,128)}, f32[128,512]{1,0:T(8,128)}) custom-call(s32[1]{0:T(128)} %bitcast.core_ref, f32[512,256]{1,0:T(8,128)} %get-tuple-element.38.mine_ref, f32[512,256]{1,0:T(8,128)} %copy-done.6, bf16[512,128]{1,0:T(8,128)(2,1)} %copy-done.3, bf16[64,256]{1,0:T(8,128)(2,1)} %bitcast.37, ...), custom_call_target="tpu_custom_call" | custom-call | flops 671088640 | bytes 16777216 | tf_op jit(solution)/shard_map/attention_gradient/pallas_call | solution.py:509
  164.2 0.8 collective-permute-done.19
  165.0 2.8 %collective-permute-start.20 = (f32[128,512]{1,0:T(8,128)}, f32[128,512]{1,0:T(8,128)S(1)}, u32[]{:S(2)}, u32[]{:S(2)}) collective-permute-start(f32[128,512]{1,0:T(8,128)} %get-tuple-element.49), channel_id=1, source_target_pairs={{0,1},{1,0},{2,3},{3,2},{4,5},{5,4},{6,7},{7,6},{8,9},{9,8},{10,11... | collective-permute-start | bytes 786440 | tf_op jit(solution)/shard_map/ppermute | solution.py:70
  167.8 3.3 %collective-permute-start.22 = (f32[128,256]{1,0:T(8,128)S(1)}, f32[128,256]{1,0:T(8,128)S(1)}, u32[]{:S(2)}, u32[]{:S(2)}) collective-permute-start(f32[128,256]{1,0:T(8,128)S(1)} %add.81), channel_id=1, source_target_pairs={{0,256},{32,288},{64,320},{96,352},{128,384},{160,416},{192,448},{... | collective-permute-start | bytes 393224 | tf_op jit(solution)/shard_map/ppermute | solution.py:70
  171.1 0.7 copy-done.12
  171.8 1.7 quarters.1
  173.5 4.8 %collective-permute-start.21 = (bf16[64,512]{1,0:T(8,128)(2,1)}, bf16[64,512]{1,0:T(8,128)(2,1)S(1)}, u32[]{:S(2)}, u32[]{:S(2)}) collective-permute-start(bf16[64,512]{1,0:T(8,128)(2,1)} %get-tuple-element.51), channel_id=1, source_target_pairs={{0,2},{2,0},{4,6},{6,4},{8,10},{10,8},{12,14},{14,12},{16,18},{18,... | collective-permute-start | bytes 196616 | tf_op jit(solution)/shard_map/ppermute | solution.py:70
  178.4 0.7 fusion.16
  179.0 7.5 %collective-permute-done.21 = bf16[64,512]{1,0:T(8,128)(2,1)S(1)} collective-permute-done((bf16[64,512]{1,0:T(8,128)(2,1)}, bf16[64,512]{1,0:T(8,128)(2,1)S(1)}, u32[]{:S(2)}, u32[]{:S(2)}) %collective-permute-start.21) | collective-permute-done | bytes 65568 | tf_op jit(solution)/shard_map/ppermute | solution.py:70
  186.5 0.9 add_convert_fusion
  187.5 0.6 slice_bitcast_fusion.1
  (50 shorter events, 0.3 us)
Async XLA Ops:
  5.6 10.4 %collective-permute-start = (bf16[416,512]{1,0:T(8,128)(2,1)}, bf16[416,512]{1,0:T(8,128)(2,1)S(1)}, u32[]{:S(2)}, u32[]{:S(2)}) collective-permute-start(bf16[416,512]{1,0:T(8,128)(2,1)} %get-tuple-element.29), channel_id=1, source_target_pairs={{0,1},{1,0},{2,3},{3,2},{4,5},{5,4},{6,7},{7,6},{8,9},{9,8},{10,11... | collective-permute-start | bytes 1277960 | tf_op jit(solution)/shard_map/ppermute | solution.py:70
  16.0 0.8 copy-start.10
  19.8 19.9 %all-to-all-start = ((bf16[4,544,512]{2,1,0:T(8,128)(2,1)}), bf16[4,544,512]{2,1,0:T(8,128)(2,1)S(1)}, u32[]{:S(2)}, u32[]{:S(2)}) async-start(bf16[4,544,512]{2,1,0:T(8,128)(2,1)} %bitcast.27), calls=%async_computation | async-start | bytes 4456448 | tf_op jit(solution)/shard_map/all_to_all | solution.py:38
  23.4 22.1 %collective-permute-start.1 = (bf16[512,512]{1,0:T(8,128)(2,1)}, bf16[512,512]{1,0:T(8,128)(2,1)S(1)}, u32[]{:S(2)}, u32[]{:S(2)}) collective-permute-start(bf16[512,512]{1,0:T(8,128)(2,1)} %get-tuple-element.32), channel_id=1, source_target_pairs={{0,2},{1,33},{2,4},{3,35},{4,6},{5,37},{6,0},{7,39},{8,10},{9,41},... | collective-permute-start | bytes 1572872 | tf_op jit(solution)/shard_map/ppermute | solution.py:34
  25.3 39.6 %collective-permute-start.2 = (bf16[512,512]{1,0:T(8,128)(2,1)}, bf16[512,512]{1,0:T(8,128)(2,1)S(1)}, u32[]{:S(2)}, u32[]{:S(2)}) collective-permute-start(bf16[512,512]{1,0:T(8,128)(2,1)} %get-tuple-element.32), channel_id=1, source_target_pairs={{0,6},{1,65},{2,0},{3,67},{4,2},{5,69},{6,4},{7,71},{8,14},{9,73},... | collective-permute-start | bytes 1572872 | tf_op jit(solution)/shard_map/ppermute | solution.py:34
  39.7 1.4 copy-start
  42.6 2.0 %collective-permute-start.3 = (bf16[128,128]{1,0:T(8,128)(2,1)}, bf16[128,128]{1,0:T(8,128)(2,1)S(1)}, u32[]{:S(2)}, u32[]{:S(2)}) collective-permute-start(bf16[128,128]{1,0:T(8,128)(2,1)} %ride_sum.1), channel_id=1, source_target_pairs={{0,4},{2,6},{4,0},{6,2},{8,12},{10,14},{12,8},{14,10},{16,20},{18,... | collective-permute-start | bytes 98312 | tf_op jit(solution)/shard_map/ppermute | solution.py:66
  43.3 1.4 collective-permute-start.4
  44.0 0.7 collective-permute-start.5
  45.5 40.6 %copy-start.11 = (bf16[128,128]{1,0:T(8,128)(2,1)}, bf16[128,128]{1,0:T(8,128)(2,1)S(1)}, u32[]{:S(2)}) copy-start(bf16[128,128]{1,0:T(8,128)(2,1)S(1)} %add_convert_fusion.1.quarter_ref) | copy-start | bytes 98308
  45.5 43.7 %copy-start.1 = (bf16[512,512]{1,0:T(8,128)(2,1)}, bf16[512,512]{1,0:T(8,128)(2,1)S(1)}, u32[]{:S(2)}) copy-start(bf16[512,512]{1,0:T(8,128)(2,1)S(1)} %collective-permute-done.1.refs_1_) | copy-start | bytes 1572868
  64.9 24.3 %copy-start.2 = (bf16[512,512]{1,0:T(8,128)(2,1)}, bf16[512,512]{1,0:T(8,128)(2,1)S(1)}, u32[]{:S(2)}) copy-start(bf16[512,512]{1,0:T(8,128)(2,1)S(1)} %collective-permute-done.2.refs_2_) | copy-start | bytes 1572868
  65.0 24.2 %collective-permute-start.6 = (bf16[1056,512]{1,0:T(8,128)(2,1)S(1)}, bf16[1056,512]{1,0:T(8,128)(2,1)}, u32[]{:S(2)}, u32[]{:S(2)}) collective-permute-start(bf16[1056,512]{1,0:T(8,128)(2,1)S(1)} %maximum_maximum_fusion), channel_id=1, source_target_pairs={{0,8},{1,129},{2,10},{3,131},{4,12},{5,133},{6,14},{7,135},{8,16},... | collective-permute-start | bytes 3244040 | tf_op jit(solution)/shard_map/ppermute | solution.py:34
  68.5 26.8 %collective-permute-start.7 = (bf16[1056,512]{1,0:T(8,128)(2,1)S(1)}, bf16[1056,512]{1,0:T(8,128)(2,1)}, u32[]{:S(2)}, u32[]{:S(2)}) collective-permute-start(bf16[1056,512]{1,0:T(8,128)(2,1)S(1)} %maximum_maximum_fusion), channel_id=1, source_target_pairs={{0,16},{1,257},{2,18},{3,259},{4,20},{5,261},{6,22},{7,263},{8,24}... | collective-permute-start | bytes 3244040 | tf_op jit(solution)/shard_map/ppermute | solution.py:34
  72.8 23.9 %collective-permute-start.8 = (bf16[1056,512]{1,0:T(8,128)(2,1)S(1)}, bf16[1056,512]{1,0:T(8,128)(2,1)}, u32[]{:S(2)}, u32[]{:S(2)}) collective-permute-start(bf16[1056,512]{1,0:T(8,128)(2,1)S(1)} %maximum_maximum_fusion), channel_id=1, source_target_pairs={{0,24},{1,385},{2,26},{3,387},{4,28},{5,389},{6,30},{7,391},{8,0},... | collective-permute-start | bytes 3244040 | tf_op jit(solution)/shard_map/ppermute | solution.py:34
  77.0 9.1 %collective-permute-start.9 = (bf16[256,512]{1,0:T(8,128)(2,1)S(1)}, bf16[256,512]{1,0:T(8,128)(2,1)S(1)}, u32[]{:S(2)}, u32[]{:S(2)}) collective-permute-start(bf16[256,512]{1,0:T(8,128)(2,1)S(1)} %get-tuple-element.56), channel_id=1, source_target_pairs={{0,2},{1,97},{2,4},{3,99},{4,6},{5,101},{6,0},{7,103},{8,10},{9,10... | collective-permute-start | bytes 786440 | tf_op jit(solution)/shard_map/ppermute | solution.py:34
  78.9 10.2 %collective-permute-start.10 = (bf16[256,512]{1,0:T(8,128)(2,1)S(1)}, bf16[256,512]{1,0:T(8,128)(2,1)S(1)}, u32[]{:S(2)}, u32[]{:S(2)}) collective-permute-start(bf16[256,512]{1,0:T(8,128)(2,1)S(1)} %get-tuple-element.55), channel_id=1, source_target_pairs={{0,6},{1,97},{2,0},{3,99},{4,2},{5,101},{6,4},{7,103},{8,14},{9,10... | collective-permute-start | bytes 786440 | tf_op jit(solution)/shard_map/ppermute | solution.py:34
  89.2 32.9 %copy-start.4 = (bf16[512,512]{1,0:T(8,128)(2,1)}, bf16[512,512]{1,0:T(8,128)(2,1)S(1)}, u32[]{:S(2)}) copy-start(bf16[512,512]{1,0:T(8,128)(2,1)S(1)} %constant_dynamic-update-slice_fusion.refs_0_.refs_6_) | copy-start | bytes 1572868
  89.2 38.4 %copy-start.5 = (bf16[512,256]{1,0:T(8,128)(2,1)S(1)}, bf16[512,256]{1,0:T(8,128)(2,1)}, u32[]{:S(2)}) copy-start(bf16[512,256]{1,0:T(8,128)(2,1)} %get-tuple-element.36.out_ref) | copy-start | bytes 786436
  101.3 25.4 %collective-permute-start.14 = (bf16[6400,256]{1,0:T(8,128)(2,1)}, bf16[6400,256]{1,0:T(8,128)(2,1)}, u32[]{:S(2)}, u32[]{:S(2)}) collective-permute-start(bf16[6400,256]{1,0:T(8,128)(2,1)} %get-tuple-element.34), channel_id=1, source_target_pairs={{0,1},{1,0},{2,3},{3,2},{4,5},{5,4},{6,7},{7,6},{8,9},{9,8},{10,11... | collective-permute-start | bytes 9830408 | tf_op jit(solution)/shard_map/ppermute | solution.py:70
  118.2 17.1 %collective-permute-start.11 = (bf16[512,512]{1,0:T(8,128)(2,1)S(1)}, bf16[512,512]{1,0:T(8,128)(2,1)S(1)}, u32[]{:S(2)}, u32[]{:S(2)}) collective-permute-start(bf16[512,512]{1,0:T(8,128)(2,1)S(1)} %constant_dynamic-update-slice_fusion.refs_0_.refs_6_), channel_id=1, source_target_pairs={{0,8},{1,129},{2,10},{3,131},{4,12},{5,133},{6,14},{7,135},{8,16},... | collective-permute-start | bytes 1572872 | tf_op jit(solution)/shard_map/ppermute | solution.py:34
  120.2 15.2 %collective-permute-start.12 = (bf16[512,512]{1,0:T(8,128)(2,1)S(1)}, bf16[512,512]{1,0:T(8,128)(2,1)S(1)}, u32[]{:S(2)}, u32[]{:S(2)}) collective-permute-start(bf16[512,512]{1,0:T(8,128)(2,1)S(1)} %constant_dynamic-update-slice_fusion.refs_0_.refs_6_), channel_id=1, source_target_pairs={{0,16},{1,257},{2,18},{3,259},{4,20},{5,261},{6,22},{7,263},{8,24}... | collective-permute-start | bytes 1572872 | tf_op jit(solution)/shard_map/ppermute | solution.py:34
  122.1 15.7 %collective-permute-start.13 = (bf16[512,512]{1,0:T(8,128)(2,1)S(1)}, bf16[512,512]{1,0:T(8,128)(2,1)S(1)}, u32[]{:S(2)}, u32[]{:S(2)}) collective-permute-start(bf16[512,512]{1,0:T(8,128)(2,1)S(1)} %constant_dynamic-update-slice_fusion.refs_0_.refs_6_), channel_id=1, source_target_pairs={{0,24},{1,385},{2,26},{3,387},{4,28},{5,389},{6,30},{7,391},{8,0},... | collective-permute-start | bytes 1572872 | tf_op jit(solution)/shard_map/ppermute | solution.py:34
  127.6 13.2 %copy-start.3 = (bf16[512,128]{1,0:T(8,128)(2,1)}, bf16[512,128]{1,0:T(8,128)(2,1)S(1)}, u32[]{:S(2)}) copy-start(bf16[512,128]{1,0:T(8,128)(2,1)S(1)} %maximum_select_fusion.adapter_ref) | copy-start | bytes 393220
  127.9 16.6 %copy-start.13 = (s32[16]{0:T(128)S(1)}, s32[16]{0:T(128)}, u32[]{:S(2)}) copy-start(s32[16]{0:T(128)} %constant.106.clone) | copy-start | bytes 196
  127.9 16.6 %copy-start.14 = (s32[16]{0:T(128)S(1)}, s32[16]{0:T(128)}, u32[]{:S(2)}) copy-start(s32[16]{0:T(128)} %constant.107.clone) | copy-start | bytes 196
  128.0 16.6 %copy-start.15 = (pred[16]{0:T(512)(128)(4,1)S(1)}, pred[16]{0:T(512)(128)(4,1)}, u32[]{:S(2)}) copy-start(pred[16]{0:T(512)(128)(4,1)} %constant.119) | copy-start | bytes 52
  128.0 16.6 %copy-start.16 = (s32[16]{0:T(128)S(1)}, s32[16]{0:T(128)}, u32[]{:S(2)}) copy-start(s32[16]{0:T(128)} %constant.120) | copy-start | bytes 196
  128.0 16.6 %copy-start.17 = (s32[16]{0:T(128)S(1)}, s32[16]{0:T(128)}, u32[]{:S(2)}) copy-start(s32[16]{0:T(128)} %constant.121) | copy-start | bytes 196
  129.3 6.0 %collective-permute-start.15 = (f32[128,256]{1,0:T(8,128)S(1)}, f32[128,256]{1,0:T(8,128)S(1)}, u32[]{:S(2)}, u32[]{:S(2)}) collective-permute-start(f32[128,256]{1,0:T(8,128)S(1)} %pad_maximum_fusion), channel_id=1, source_target_pairs={{0,32},{32,0},{64,96},{96,64},{128,160},{160,128},{192,224},{224,1... | collective-permute-start | bytes 393224 | tf_op jit(solution)/shard_map/ppermute | solution.py:70
  135.3 2.5 %copy-start.7 = (bf16[512,512]{1,0:T(8,128)(2,1)}, bf16[512,512]{1,0:T(8,128)(2,1)S(1)}, u32[]{:S(2)}) copy-start(bf16[512,512]{1,0:T(8,128)(2,1)S(1)} %collective-permute-done.11.refs_1_.refs_7_) | copy-start | bytes 1572868
  135.3 2.5 %copy-start.8 = (bf16[512,512]{1,0:T(8,128)(2,1)}, bf16[512,512]{1,0:T(8,128)(2,1)S(1)}, u32[]{:S(2)}) copy-start(bf16[512,512]{1,0:T(8,128)(2,1)S(1)} %collective-permute-done.12.refs_2_.refs_8_) | copy-start | bytes 1572868
  137.8 0.8 copy-start.9
  140.8 6.2 %collective-permute-start.16 = (bf16[2048,256]{1,0:T(8,128)(2,1)}, bf16[2048,256]{1,0:T(8,128)(2,1)S(1)}, u32[]{:S(2)}, u32[]{:S(2)}) collective-permute-start(bf16[2048,256]{1,0:T(8,128)(2,1)} %give.1), channel_id=1, source_target_pairs={{0,1},{1,0},{2,3},{3,2},{4,5},{5,4},{6,7},{7,6},{8,9},{9,8},{10,11... | collective-permute-start | bytes 3145736 | tf_op jit(solution)/shard_map/ppermute | solution.py:70
  145.1 10.5 %collective-permute-start.17 = (f32[128,256]{1,0:T(8,128)S(1)}, f32[128,256]{1,0:T(8,128)S(1)}, u32[]{:S(2)}, u32[]{:S(2)}) collective-permute-start(f32[128,256]{1,0:T(8,128)S(1)} %fusion.14), channel_id=1, source_target_pairs={{0,64},{32,96},{64,0},{96,32},{128,192},{160,224},{192,128},{224,1... | collective-permute-start | bytes 393224 | tf_op jit(solution)/shard_map/ppermute | solution.py:70
  147.1 1.0 copy-start.18
  155.7 4.3 %collective-permute-start.18 = (f32[512,256]{1,0:T(8,128)}, f32[512,256]{1,0:T(8,128)S(1)}, u32[]{:S(2)}, u32[]{:S(2)}) collective-permute-start(f32[512,256]{1,0:T(8,128)} %get-tuple-element.41), channel_id=1, source_target_pairs={{0,1},{1,0},{2,3},{3,2},{4,5},{5,4},{6,7},{7,6},{8,9},{9,8},{10,11... | collective-permute-start | bytes 1572872 | tf_op jit(solution)/shard_map/ppermute | solution.py:70
  158.0 6.9 %collective-permute-start.19 = (f32[128,256]{1,0:T(8,128)S(1)}, f32[128,256]{1,0:T(8,128)S(1)}, u32[]{:S(2)}, u32[]{:S(2)}) collective-permute-start(f32[128,256]{1,0:T(8,128)S(1)} %add.80), channel_id=1, source_target_pairs={{0,128},{32,160},{64,192},{96,224},{128,0},{160,32},{192,64},{224,... | collective-permute-start | bytes 393224 | tf_op jit(solution)/shard_map/ppermute | solution.py:70
  160.0 0.8 copy-start.6
  165.0 6.1 %collective-permute-start.20 = (f32[128,512]{1,0:T(8,128)}, f32[128,512]{1,0:T(8,128)S(1)}, u32[]{:S(2)}, u32[]{:S(2)}) collective-permute-start(f32[128,512]{1,0:T(8,128)} %get-tuple-element.49), channel_id=1, source_target_pairs={{0,1},{1,0},{2,3},{3,2},{4,5},{5,4},{6,7},{7,6},{8,9},{9,8},{10,11... | collective-permute-start | bytes 786440 | tf_op jit(solution)/shard_map/ppermute | solution.py:70
  167.8 10.6 %collective-permute-start.22 = (f32[128,256]{1,0:T(8,128)S(1)}, f32[128,256]{1,0:T(8,128)S(1)}, u32[]{:S(2)}, u32[]{:S(2)}) collective-permute-start(f32[128,256]{1,0:T(8,128)S(1)} %add.81), channel_id=1, source_target_pairs={{0,256},{32,288},{64,320},{96,352},{128,384},{160,416},{192,448},{... | collective-permute-start | bytes 393224 | tf_op jit(solution)/shard_map/ppermute | solution.py:70
  171.1 0.7 copy-start.12
  173.5 13.1 %collective-permute-start.21 = (bf16[64,512]{1,0:T(8,128)(2,1)}, bf16[64,512]{1,0:T(8,128)(2,1)S(1)}, u32[]{:S(2)}, u32[]{:S(2)}) collective-permute-start(bf16[64,512]{1,0:T(8,128)(2,1)} %get-tuple-element.51), channel_id=1, source_target_pairs={{0,2},{2,0},{4,6},{6,4},{8,10},{10,8},{12,14},{14,12},{16,18},{18,... | collective-permute-start | bytes 196616 | tf_op jit(solution)/shard_map/ppermute | solution.py:70

commit v5 on v4

--- a/solution.py
+++ b/solution.py
@@ -12,6 +12,7 @@
 HEAD_WIDTH = 128
 SIDE = 4
 SEGMENT_MOST = 128
+ROOMY = pltpu.CompilerParams(vmem_limit_bytes=16 * 1024 * 1024)
 
 adapter_scale = 2.0
 
@@ -131,6 +132,7 @@
         ),
         in_specs=[pl.BlockSpec(memory_space=pltpu.SMEM)] + [vmem] * 7,
         out_specs=(vmem,) * 3,
+        compiler_params=ROOMY,
         name="blend",
     )(place, tapped, rows, taps, upper, slab, came, inner)
 
@@ -169,6 +171,7 @@
             pltpu.VMEM((SIDE, n_ride, width), BF16),
             pltpu.SemaphoreType.DMA((SIDE,)),
         ],
+        compiler_params=ROOMY,
         name="ride_sum",
     )(stack)
 
@@ -200,6 +203,7 @@
         in_specs=[pl.BlockSpec(memory_space=pltpu.SMEM)] + [any_spec] * len(arrays),
         out_specs=pl.BlockSpec(memory_space=pltpu.VMEM),
         scratch_shapes=[pltpu.SemaphoreType.DMA((len(parts),))],
+        compiler_params=ROOMY,
         name="give",
     )(core, *arrays)
 
@@ -247,6 +251,7 @@
             pltpu.VMEM((3, n_ride, width), BF16),
             pltpu.SemaphoreType.DMA((len(parts) + 3,)),
         ],
+        compiler_params=ROOMY,
         name="give_near",
     )(place, quarter, *arrays)
 
@@ -516,6 +521,7 @@
         cost_estimate=pl.CostEstimate(
             flops=20 * n * width * 2 * SEGMENT_MOST, bytes_accessed=16 << 20, transcendentals=0
         ),
+        compiler_params=ROOMY,
         name="attention_gradient",
     )(core, mine, came, adapter, lower, band, out, queries, key_head, value_head)
 
@@ -543,6 +549,7 @@
         in_specs=[pl.BlockSpec(memory_space=pltpu.SMEM)]
         + [pl.BlockSpec(memory_space=pltpu.VMEM)] * 2,
         out_specs=(pl.BlockSpec(memory_space=pltpu.VMEM),) * 2,
+        compiler_params=ROOMY,
         name="quarters",
     )(chip, keep, came)
 

time: 189 us -> 183 us (0.968)
  the two profiles are of different devices: /device:TPU:1 before, /device:TPU:9 now
where the time goes in v5:
time: 183 us; the launch traced here: 182 us
  starting transfers between devices  93.1 us (51%)
  waiting for transfers between devices  54.2 us (30%)
  Pallas kernels  19.9 us (11%)
  local copies, waits for them, and re-layouts  8.5 us (5%)
  other arithmetic  3.57 us (2%)
    ppermute x10, starting transfers between devices, swapped(): lax.ppermute(array, axis, [(i, i ^ mask) for i in range(lax.axis_size(axi...  50.2 us
    ppermute x10, starting transfers between devices, moved(): return lax.ppermute(array, AXES, pairs)  36.9 us
    ppermute x10, waiting for transfers between devices, moved(): return lax.ppermute(array, AXES, pairs)  33.3 us
    ppermute x10, waiting for transfers between devices, swapped(): lax.ppermute(array, axis, [(i, i ^ mask) for i in range(lax.axis_size(axi...  13 us
    all_to_all x1, waiting for transfers between devices, spread(): lax.all_to_all(stacked, axes, 0, 0, axis_index_groups=groups, tiled=True)  7.91 us
    pallas_call x1, Pallas kernels, frozen_product(): pl.pallas_call(functools.partial(frozen_kernel, len(own), parts), out_sha...  7.33 us
    unnamed x59, local copies, waits for them, and re-layouts  5.59 us
    pallas_call x1, Pallas kernels, forward(): pl.pallas_call(functools.partial(forward_kernel, HEAD_WIDTH ** (-0.5)), o...  4.36 us
  transfers between devices with their start and end apart: 24, of which 10 were waited for; matrix products, arithmetic and copies ran while one was open for 3% of the time, Pallas kernels for 5%

profile of v5, /device:TPU:9, one launch (start us, length us, event | category | flops | bytes accessed | tf_op | source)
XLA Modules:
  0.0 182.2 jit_solution(16899628900740133113)
XLA Ops:
  0.7 0.0 copy-start.8
  0.7 0.0 copy-start.18
  0.7 0.6 pad_add_fusion.place_ref
  1.3 4.4 %attention.1 = (f32[2,512,256]{2,1,0:T(8,128)}, bf16[512,256]{1,0:T(8,128)(2,1)}, f32[512,64]{1,0:T(8,128)}, bf16[512,128]{1,0:T(8,128)(2,1)}, bf16[512,128]{1,0:T(8,128)(2,1)}, /*index=5*/bf16[416,512]{1,0:T(8,128)(2,1)}) custom-call(s32[3]{0:T(128)} %pad_add_fusion.place_ref, bf16[512,256]{1,0:T(8,128)(2,1)} %bitcast.28, s32[1,512]{1,0:T(1,128)} %label_ref.1, ...), custom_call_target="tpu_custom_call" | custom-call | tf_op jit(solution)/shard_map/attention/pallas_call | solution.py:429
  5.7 2.6 %collective-permute-start = (bf16[416,512]{1,0:T(8,128)(2,1)}, bf16[416,512]{1,0:T(8,128)(2,1)S(1)}, u32[]{:S(2)}, u32[]{:S(2)}) collective-permute-start(bf16[416,512]{1,0:T(8,128)(2,1)} %get-tuple-element.29), channel_id=1, source_target_pairs={{0,1},{1,0},{2,3},{3,2},{4,5},{5,4},{6,7},{7,6},{8,9},{9,8},{10,11... | collective-permute-start | bytes 1277960 | tf_op jit(solution)/shard_map/ppermute | solution.py:71
  8.3 1.6 collective-permute-done.came_ref
  9.9 0.9 copy-done.16
  10.8 1.5 blend.1
  12.3 1.4 copy-done.3
  13.7 4.0 %all-to-all-start = ((bf16[4,544,512]{2,1,0:T(8,128)(2,1)}), bf16[4,544,512]{2,1,0:T(8,128)(2,1)S(1)}, u32[]{:S(2)}, u32[]{:S(2)}) async-start(bf16[4,544,512]{2,1,0:T(8,128)(2,1)} %bitcast.27), calls=%async_computation | async-start | bytes 4456448 | tf_op jit(solution)/shard_map/all_to_all | solution.py:39
  17.7 3.5 %collective-permute-start.1 = (bf16[512,512]{1,0:T(8,128)(2,1)}, bf16[512,512]{1,0:T(8,128)(2,1)S(1)}, u32[]{:S(2)}, u32[]{:S(2)}) collective-permute-start(bf16[512,512]{1,0:T(8,128)(2,1)} %get-tuple-element.32), channel_id=1, source_target_pairs={{0,2},{1,33},{2,4},{3,35},{4,6},{5,37},{6,0},{7,39},{8,10},{9,41},... | collective-permute-start | bytes 1572872 | tf_op jit(solution)/shard_map/ppermute | solution.py:35
  21.2 4.9 %collective-permute-start.2 = (bf16[512,512]{1,0:T(8,128)(2,1)}, bf16[512,512]{1,0:T(8,128)(2,1)S(1)}, u32[]{:S(2)}, u32[]{:S(2)}) collective-permute-start(bf16[512,512]{1,0:T(8,128)(2,1)} %get-tuple-element.32), channel_id=1, source_target_pairs={{0,6},{1,65},{2,0},{3,67},{4,2},{5,69},{6,4},{7,71},{8,14},{9,73},... | collective-permute-start | bytes 1572872 | tf_op jit(solution)/shard_map/ppermute | solution.py:35
  26.2 7.9 %all-to-all-done = bf16[4,544,512]{2,1,0:T(8,128)(2,1)S(1)} async-done(((bf16[4,544,512]{2,1,0:T(8,128)(2,1)}), bf16[4,544,512]{2,1,0:T(8,128)(2,1)S(1)}, u32[]{:S(2)}, u32[]{:S(2)}) %all-to-all-start) | async-done | bytes 2228256 | tf_op jit(solution)/shard_map/all_to_all | solution.py:39
  34.1 0.2 ride_sum.1
  34.3 0.7 collective-permute-start.3
  35.0 0.7 collective-permute-start.4
  35.6 0.7 collective-permute-start.5
  36.4 21.8 %collective-permute-done.2.refs_2_ = bf16[512,512]{1,0:T(8,128)(2,1)S(1)} collective-permute-done((bf16[512,512]{1,0:T(8,128)(2,1)}, bf16[512,512]{1,0:T(8,128)(2,1)S(1)}, u32[]{:S(2)}, u32[]{:S(2)}) %collective-permute-start.2) | collective-permute-done | bytes 524320 | tf_op jit(solution)/shard_map/ppermute | solution.py:35
  58.2 1.2 maximum_maximum_fusion
  59.4 3.5 %collective-permute-start.6 = (bf16[1056,512]{1,0:T(8,128)(2,1)}, bf16[1056,512]{1,0:T(8,128)(2,1)}, u32[]{:S(2)}, u32[]{:S(2)}) collective-permute-start(bf16[1056,512]{1,0:T(8,128)(2,1)} %maximum_maximum_fusion), channel_id=1, source_target_pairs={{0,8},{1,129},{2,10},{3,131},{4,12},{5,133},{6,14},{7,135},{8,16},... | collective-permute-start | bytes 3244040 | tf_op jit(solution)/shard_map/ppermute | solution.py:35
  62.9 4.3 %collective-permute-start.7 = (bf16[1056,512]{1,0:T(8,128)(2,1)}, bf16[1056,512]{1,0:T(8,128)(2,1)}, u32[]{:S(2)}, u32[]{:S(2)}) collective-permute-start(bf16[1056,512]{1,0:T(8,128)(2,1)} %maximum_maximum_fusion), channel_id=1, source_target_pairs={{0,16},{1,257},{2,18},{3,259},{4,20},{5,261},{6,22},{7,263},{8,24}... | collective-permute-start | bytes 3244040 | tf_op jit(solution)/shard_map/ppermute | solution.py:35
  67.2 3.1 %collective-permute-start.8 = (bf16[1056,512]{1,0:T(8,128)(2,1)}, bf16[1056,512]{1,0:T(8,128)(2,1)}, u32[]{:S(2)}, u32[]{:S(2)}) collective-permute-start(bf16[1056,512]{1,0:T(8,128)(2,1)} %maximum_maximum_fusion), channel_id=1, source_target_pairs={{0,24},{1,385},{2,26},{3,387},{4,28},{5,389},{6,30},{7,391},{8,0},... | collective-permute-start | bytes 3244040 | tf_op jit(solution)/shard_map/ppermute | solution.py:35
  70.3 1.1 slice_select_fusion
  71.4 3.0 %collective-permute-start.9 = (bf16[256,512]{1,0:T(8,128)(2,1)S(1)}, bf16[256,512]{1,0:T(8,128)(2,1)S(1)}, u32[]{:S(2)}, u32[]{:S(2)}) collective-permute-start(bf16[256,512]{1,0:T(8,128)(2,1)S(1)} %get-tuple-element.56), channel_id=1, source_target_pairs={{0,2},{1,97},{2,4},{3,99},{4,6},{5,101},{6,0},{7,103},{8,10},{9,10... | collective-permute-start | bytes 786440 | tf_op jit(solution)/shard_map/ppermute | solution.py:35
  74.4 4.1 %collective-permute-start.10 = (bf16[256,512]{1,0:T(8,128)(2,1)S(1)}, bf16[256,512]{1,0:T(8,128)(2,1)S(1)}, u32[]{:S(2)}, u32[]{:S(2)}) collective-permute-start(bf16[256,512]{1,0:T(8,128)(2,1)S(1)} %get-tuple-element.55), channel_id=1, source_target_pairs={{0,6},{1,97},{2,0},{3,99},{4,2},{5,101},{6,4},{7,103},{8,14},{9,10... | collective-permute-start | bytes 786440 | tf_op jit(solution)/shard_map/ppermute | solution.py:35
  78.5 1.9 %collective-permute-done.9 = bf16[256,512]{1,0:T(8,128)(2,1)S(1)} collective-permute-done((bf16[256,512]{1,0:T(8,128)(2,1)S(1)}, bf16[256,512]{1,0:T(8,128)(2,1)S(1)}, u32[]{:S(2)}, u32[]{:S(2)}) %collective-permute-start.9) | collective-permute-done | bytes 262176 | tf_op jit(solution)/shard_map/ppermute | solution.py:35
  80.4 0.7 constant_dynamic-update-slice_fusion.1
  81.2 2.2 %collective-permute-done.10 = bf16[256,512]{1,0:T(8,128)(2,1)S(1)} collective-permute-done((bf16[256,512]{1,0:T(8,128)(2,1)S(1)}, bf16[256,512]{1,0:T(8,128)(2,1)S(1)}, u32[]{:S(2)}, u32[]{:S(2)}) %collective-permute-start.10) | collective-permute-done | bytes 262176 | tf_op jit(solution)/shard_map/ppermute | solution.py:35
  83.4 0.7 constant_dynamic-update-slice_fusion.refs_0_.refs_6_
  84.1 5.8 %collective-permute-done.7.refs_4_ = bf16[1056,512]{1,0:T(8,128)(2,1)} collective-permute-done((bf16[1056,512]{1,0:T(8,128)(2,1)}, bf16[1056,512]{1,0:T(8,128)(2,1)}, u32[]{:S(2)}, u32[]{:S(2)}) %collective-permute-start.7) | collective-permute-done | bytes 1081376 | tf_op jit(solution)/shard_map/ppermute | solution.py:35
  89.9 1.5 collective-permute-done.8.refs_5_
  91.4 0.7 copy-done.14
  92.2 3.9 %give_near.1 = (bf16[6400,256]{1,0:T(8,128)(2,1)}, bf16[512,128]{1,0:T(8,128)(2,1)S(1)}) custom-call(s32[3]{0:T(128)S(1)} %copy-done.22, bf16[128,128]{1,0:T(8,128)(2,1)S(1)} %copy-done.14, bf16[2176,512]{1,0:T(8,128)(2,1)S(1)} %bitcast.25, bf16[512,512]{1,0:T(8,128)(2,1)S(1)} %collective-permute-done.1.refs_1_, ...), custom_call_target="tpu_custom_call" | custom-call | tf_op jit(solution)/shard_map/give_near/pallas_call | solution.py:242
  96.1 0.6 copy-done.21
  96.7 10.9 %collective-permute-start.14 = (bf16[6400,256]{1,0:T(8,128)(2,1)}, bf16[6400,256]{1,0:T(8,128)(2,1)}, u32[]{:S(2)}, u32[]{:S(2)}) collective-permute-start(bf16[6400,256]{1,0:T(8,128)(2,1)} %get-tuple-element.34), channel_id=1, source_target_pairs={{0,1},{1,0},{2,3},{3,2},{4,5},{5,4},{6,7},{7,6},{8,9},{9,8},{10,11... | collective-permute-start | bytes 9830408 | tf_op jit(solution)/shard_map/ppermute | solution.py:71
  107.6 3.1 %collective-permute-start.11 = (bf16[512,512]{1,0:T(8,128)(2,1)}, bf16[512,512]{1,0:T(8,128)(2,1)S(1)}, u32[]{:S(2)}, u32[]{:S(2)}) collective-permute-start(bf16[512,512]{1,0:T(8,128)(2,1)} %constant_dynamic-update-slice_fusion.refs_0_.refs_6_), channel_id=1, source_target_pairs={{0,8},{1,129},{2,10},{3,131},{4,12},{5,133},{6,14},{7,135},{8,16},... | collective-permute-start | bytes 1572872 | tf_op jit(solution)/shard_map/ppermute | solution.py:35
  110.7 4.4 %collective-permute-start.12 = (bf16[512,512]{1,0:T(8,128)(2,1)}, bf16[512,512]{1,0:T(8,128)(2,1)S(1)}, u32[]{:S(2)}, u32[]{:S(2)}) collective-permute-start(bf16[512,512]{1,0:T(8,128)(2,1)} %constant_dynamic-update-slice_fusion.refs_0_.refs_6_), channel_id=1, source_target_pairs={{0,16},{1,257},{2,18},{3,259},{4,20},{5,261},{6,22},{7,263},{8,24}... | collective-permute-start | bytes 1572872 | tf_op jit(solution)/shard_map/ppermute | solution.py:35
  115.1 3.0 %collective-permute-start.13 = (bf16[512,512]{1,0:T(8,128)(2,1)}, bf16[512,512]{1,0:T(8,128)(2,1)S(1)}, u32[]{:S(2)}, u32[]{:S(2)}) collective-permute-start(bf16[512,512]{1,0:T(8,128)(2,1)} %constant_dynamic-update-slice_fusion.refs_0_.refs_6_), channel_id=1, source_target_pairs={{0,24},{1,385},{2,26},{3,387},{4,28},{5,389},{6,30},{7,391},{8,0},... | collective-permute-start | bytes 1572872 | tf_op jit(solution)/shard_map/ppermute | solution.py:35
  118.2 0.9 fusion.15
  119.1 0.3 fusion.6
  119.4 0.0 copy-start.24
  119.4 0.0 copy-start.25
  119.4 0.0 copy-start.26
  119.4 0.0 copy-start.27
  119.5 0.0 copy-start.28
  119.5 1.2 fusion
  120.7 12.1 %collective-permute-start.15 = (f32[128,256]{1,0:T(8,128)S(1)}, f32[128,256]{1,0:T(8,128)S(1)}, u32[]{:S(2)}, u32[]{:S(2)}) collective-permute-start(f32[128,256]{1,0:T(8,128)S(1)} %pad_maximum_fusion), channel_id=1, source_target_pairs={{0,32},{32,0},{64,96},{96,64},{128,160},{160,128},{192,224},{224,1... | collective-permute-start | bytes 393224 | tf_op jit(solution)/shard_map/ppermute | solution.py:71
  132.9 3.2 %collective-permute-done.15 = f32[128,256]{1,0:T(8,128)S(1)} collective-permute-done((f32[128,256]{1,0:T(8,128)S(1)}, f32[128,256]{1,0:T(8,128)S(1)}, u32[]{:S(2)}, u32[]{:S(2)}) %collective-permute-start.15) | collective-permute-done | bytes 131104 | tf_op jit(solution)/shard_map/ppermute | solution.py:71
  136.2 1.2 give.1
  137.4 2.1 %collective-permute-start.16 = (bf16[2048,256]{1,0:T(8,128)(2,1)S(1)}, bf16[2048,256]{1,0:T(8,128)(2,1)}, u32[]{:S(2)}, u32[]{:S(2)}) collective-permute-start(bf16[2048,256]{1,0:T(8,128)(2,1)S(1)} %give.1), channel_id=1, source_target_pairs={{0,1},{1,0},{2,3},{3,2},{4,5},{5,4},{6,7},{7,6},{8,9},{9,8},{10,11... | collective-permute-start | bytes 3145736 | tf_op jit(solution)/shard_map/ppermute | solution.py:71
  139.7 0.5 compare_select_fusion.10.place_ref
  140.2 2.1 %collective-permute-start.17 = (f32[128,256]{1,0:T(8,128)S(1)}, f32[128,256]{1,0:T(8,128)S(1)}, u32[]{:S(2)}, u32[]{:S(2)}) collective-permute-start(f32[128,256]{1,0:T(8,128)S(1)} %fusion.14), channel_id=1, source_target_pairs={{0,64},{32,96},{64,0},{96,32},{128,192},{160,224},{192,128},{224,1... | collective-permute-start | bytes 393224 | tf_op jit(solution)/shard_map/ppermute | solution.py:71
  142.3 7.3 %frozen.1 = (f32[512,256]{1,0:T(8,128)}, f32[512,256]{1,0:T(8,128)}) custom-call(s32[1]{0:T(128)} %bitcast.core_ref, s32[16]{0:T(128)} %compare_select_fusion.10.place_ref, bf16[2176,512]{1,0:T(8,128)(2,1)} %bitcast.26, bf16[512,512]{1,0:T(8,128)(2,1)} %copy-done.1, bf16[512,512]{1,0:T(8,128)(2,1)} %copy-done.2, ...), custom_call_target="tpu_custom_call" | custom-call | flops 4294967296 | bytes 25165824 | tf_op jit(solution)/shard_map/frozen/pallas_call | solution.py:312
  149.7 4.1 %collective-permute-start.18 = (f32[512,256]{1,0:T(8,128)}, f32[512,256]{1,0:T(8,128)S(1)}, u32[]{:S(2)}, u32[]{:S(2)}) collective-permute-start(f32[512,256]{1,0:T(8,128)} %get-tuple-element.41), channel_id=1, source_target_pairs={{0,1},{1,0},{2,3},{3,2},{4,5},{5,4},{6,7},{7,6},{8,9},{9,8},{10,11... | collective-permute-start | bytes 1572872 | tf_op jit(solution)/shard_map/ppermute | solution.py:71
  153.8 3.2 %collective-permute-start.19 = (f32[128,256]{1,0:T(8,128)S(1)}, f32[128,256]{1,0:T(8,128)S(1)}, u32[]{:S(2)}, u32[]{:S(2)}) collective-permute-start(f32[128,256]{1,0:T(8,128)S(1)} %add.80), channel_id=1, source_target_pairs={{0,128},{32,160},{64,192},{96,224},{128,0},{160,32},{192,64},{224,... | collective-permute-start | bytes 393224 | tf_op jit(solution)/shard_map/ppermute | solution.py:71
  157.0 1.0 copy-done.9
  158.1 1.4 attention_gradient.1
  159.4 1.4 collective-permute-done.19
  160.8 2.7 %collective-permute-start.20 = (f32[128,512]{1,0:T(8,128)S(1)}, f32[128,512]{1,0:T(8,128)S(1)}, u32[]{:S(2)}, u32[]{:S(2)}) collective-permute-start(f32[128,512]{1,0:T(8,128)S(1)} %get-tuple-element.49), channel_id=1, source_target_pairs={{0,1},{1,0},{2,3},{3,2},{4,5},{5,4},{6,7},{7,6},{8,9},{9,8},{10,11... | collective-permute-start | bytes 786440 | tf_op jit(solution)/shard_map/ppermute | solution.py:71
  163.5 3.9 %collective-permute-start.22 = (f32[128,256]{1,0:T(8,128)S(1)}, f32[128,256]{1,0:T(8,128)S(1)}, u32[]{:S(2)}, u32[]{:S(2)}) collective-permute-start(f32[128,256]{1,0:T(8,128)S(1)} %add.81), channel_id=1, source_target_pairs={{0,256},{32,288},{64,320},{96,352},{128,384},{160,416},{192,448},{... | collective-permute-start | bytes 393224 | tf_op jit(solution)/shard_map/ppermute | solution.py:71
  167.5 6.5 %collective-permute-start.21 = (bf16[64,512]{1,0:T(8,128)(2,1)S(1)}, bf16[64,512]{1,0:T(8,128)(2,1)S(1)}, u32[]{:S(2)}, u32[]{:S(2)}) collective-permute-start(bf16[64,512]{1,0:T(8,128)(2,1)S(1)} %get-tuple-element.51), channel_id=1, source_target_pairs={{0,2},{2,0},{4,6},{6,4},{8,10},{10,8},{12,14},{14,12},{16,18},{18,... | collective-permute-start | bytes 196616 | tf_op jit(solution)/shard_map/ppermute | solution.py:71
  174.1 0.7 fusion.16
  174.8 6.8 %collective-permute-done.21 = bf16[64,512]{1,0:T(8,128)(2,1)S(1)} collective-permute-done((bf16[64,512]{1,0:T(8,128)(2,1)S(1)}, bf16[64,512]{1,0:T(8,128)(2,1)S(1)}, u32[]{:S(2)}, u32[]{:S(2)}) %collective-permute-start.21) | collective-permute-done | bytes 65568 | tf_op jit(solution)/shard_map/ppermute | solution.py:71
  181.6 0.6 slice_bitcast_fusion.1
  (70 shorter events, 0.3 us)
Async XLA Ops:
  0.6 9.2 %copy-start.7 = (bf16[1,256,512]{2,1,0:T(8,128)(2,1)S(1)}, bf16[1,256,512]{2,1,0:T(8,128)(2,1)}, u32[]{:S(2)}) copy-start(bf16[1,256,512]{2,1,0:T(8,128)(2,1)} %param.16) | copy-start | bytes 786436
  0.6 9.2 %copy-start.15 = (bf16[1,64,512]{2,1,0:T(8,128)(2,1)S(1)}, bf16[1,64,512]{2,1,0:T(8,128)(2,1)}, u32[]{:S(2)}) copy-start(bf16[1,64,512]{2,1,0:T(8,128)(2,1)} %param.17) | copy-start | bytes 196612
  0.7 9.2 %copy-start.8 = (bf16[256,512]{1,0:T(8,128)(2,1)S(1)}, bf16[256,512]{1,0:T(8,128)(2,1)}, u32[]{:S(2)}) copy-start(bf16[256,512]{1,0:T(8,128)(2,1)} %slab_ref.3) | copy-start | bytes 786436
  0.7 9.2 %copy-start.18 = (bf16[64,256]{1,0:T(8,128)(2,1)S(1)}, bf16[64,256]{1,0:T(8,128)(2,1)}, u32[]{:S(2)}) copy-start(bf16[64,256]{1,0:T(8,128)(2,1)} %upper_ref.3) | copy-start | bytes 98308
  0.7 9.2 %copy-start.23 = (s32[1,128]{1,0:T(1,128)S(1)}, s32[1,128]{1,0:T(1,128)}, u32[]{:S(2)}) copy-start(s32[1,128]{1,0:T(1,128)} %tapped_ref.1) | copy-start | bytes 1540
  1.3 8.6 %copy-start.22 = (s32[3]{0:T(128)S(1)}, s32[3]{0:T(128)}, u32[]{:S(2)}) copy-start(s32[3]{0:T(128)} %pad_add_fusion.place_ref) | copy-start | bytes 40
  5.7 4.2 %collective-permute-start = (bf16[416,512]{1,0:T(8,128)(2,1)}, bf16[416,512]{1,0:T(8,128)(2,1)S(1)}, u32[]{:S(2)}, u32[]{:S(2)}) collective-permute-start(bf16[416,512]{1,0:T(8,128)(2,1)} %get-tuple-element.29), channel_id=1, source_target_pairs={{0,1},{1,0},{2,3},{3,2},{4,5},{5,4},{6,7},{7,6},{8,9},{9,8},{10,11... | collective-permute-start | bytes 1277960 | tf_op jit(solution)/shard_map/ppermute | solution.py:71
  9.9 1.0 copy-start.16
  12.3 1.4 copy-start.3
  13.7 20.4 %all-to-all-start = ((bf16[4,544,512]{2,1,0:T(8,128)(2,1)}), bf16[4,544,512]{2,1,0:T(8,128)(2,1)S(1)}, u32[]{:S(2)}, u32[]{:S(2)}) async-start(bf16[4,544,512]{2,1,0:T(8,128)(2,1)} %bitcast.27), calls=%async_computation | async-start | bytes 4456448 | tf_op jit(solution)/shard_map/all_to_all | solution.py:39
  17.7 18.7 %collective-permute-start.1 = (bf16[512,512]{1,0:T(8,128)(2,1)}, bf16[512,512]{1,0:T(8,128)(2,1)S(1)}, u32[]{:S(2)}, u32[]{:S(2)}) collective-permute-start(bf16[512,512]{1,0:T(8,128)(2,1)} %get-tuple-element.32), channel_id=1, source_target_pairs={{0,2},{1,33},{2,4},{3,35},{4,6},{5,37},{6,0},{7,39},{8,10},{9,41},... | collective-permute-start | bytes 1572872 | tf_op jit(solution)/shard_map/ppermute | solution.py:35
  21.2 37.0 %collective-permute-start.2 = (bf16[512,512]{1,0:T(8,128)(2,1)}, bf16[512,512]{1,0:T(8,128)(2,1)S(1)}, u32[]{:S(2)}, u32[]{:S(2)}) collective-permute-start(bf16[512,512]{1,0:T(8,128)(2,1)} %get-tuple-element.32), channel_id=1, source_target_pairs={{0,6},{1,65},{2,0},{3,67},{4,2},{5,69},{6,4},{7,71},{8,14},{9,73},... | collective-permute-start | bytes 1572872 | tf_op jit(solution)/shard_map/ppermute | solution.py:35
  34.1 57.3 %copy-start = (bf16[4,544,512]{2,1,0:T(8,128)(2,1)}, bf16[4,544,512]{2,1,0:T(8,128)(2,1)S(1)}, u32[]{:S(2)}) copy-start(bf16[4,544,512]{2,1,0:T(8,128)(2,1)S(1)} %all-to-all-done) | copy-start | bytes 6684676
  34.3 2.0 %collective-permute-start.3 = (bf16[128,128]{1,0:T(8,128)(2,1)S(1)}, bf16[128,128]{1,0:T(8,128)(2,1)S(1)}, u32[]{:S(2)}, u32[]{:S(2)}) collective-permute-start(bf16[128,128]{1,0:T(8,128)(2,1)S(1)} %ride_sum.1), channel_id=1, source_target_pairs={{0,4},{2,6},{4,0},{6,2},{8,12},{10,14},{12,8},{14,10},{16,20},{18,... | collective-permute-start | bytes 98312 | tf_op jit(solution)/shard_map/ppermute | solution.py:67
  35.0 1.4 collective-permute-start.4
  35.6 0.7 collective-permute-start.5
  36.4 21.9 %copy-start.13 = (bf16[128,128]{1,0:T(8,128)(2,1)}, bf16[128,128]{1,0:T(8,128)(2,1)S(1)}, u32[]{:S(2)}) copy-start(bf16[128,128]{1,0:T(8,128)(2,1)S(1)} %add_convert_fusion.1.quarter_ref) | copy-start | bytes 98308
  36.4 55.0 %copy-start.1 = (bf16[512,512]{1,0:T(8,128)(2,1)}, bf16[512,512]{1,0:T(8,128)(2,1)S(1)}, u32[]{:S(2)}) copy-start(bf16[512,512]{1,0:T(8,128)(2,1)S(1)} %collective-permute-done.1.refs_1_) | copy-start | bytes 1572868
  58.2 33.2 %copy-start.2 = (bf16[512,512]{1,0:T(8,128)(2,1)}, bf16[512,512]{1,0:T(8,128)(2,1)S(1)}, u32[]{:S(2)}) copy-start(bf16[512,512]{1,0:T(8,128)(2,1)S(1)} %collective-permute-done.2.refs_2_) | copy-start | bytes 1572868
  59.4 24.7 %collective-permute-start.6 = (bf16[1056,512]{1,0:T(8,128)(2,1)}, bf16[1056,512]{1,0:T(8,128)(2,1)}, u32[]{:S(2)}, u32[]{:S(2)}) collective-permute-start(bf16[1056,512]{1,0:T(8,128)(2,1)} %maximum_maximum_fusion), channel_id=1, source_target_pairs={{0,8},{1,129},{2,10},{3,131},{4,12},{5,133},{6,14},{7,135},{8,16},... | collective-permute-start | bytes 3244040 | tf_op jit(solution)/shard_map/ppermute | solution.py:35
  62.9 27.0 %collective-permute-start.7 = (bf16[1056,512]{1,0:T(8,128)(2,1)}, bf16[1056,512]{1,0:T(8,128)(2,1)}, u32[]{:S(2)}, u32[]{:S(2)}) collective-permute-start(bf16[1056,512]{1,0:T(8,128)(2,1)} %maximum_maximum_fusion), channel_id=1, source_target_pairs={{0,16},{1,257},{2,18},{3,259},{4,20},{5,261},{6,22},{7,263},{8,24}... | collective-permute-start | bytes 3244040 | tf_op jit(solution)/shard_map/ppermute | solution.py:35
  67.2 24.2 %collective-permute-start.8 = (bf16[1056,512]{1,0:T(8,128)(2,1)}, bf16[1056,512]{1,0:T(8,128)(2,1)}, u32[]{:S(2)}, u32[]{:S(2)}) collective-permute-start(bf16[1056,512]{1,0:T(8,128)(2,1)} %maximum_maximum_fusion), channel_id=1, source_target_pairs={{0,24},{1,385},{2,26},{3,387},{4,28},{5,389},{6,30},{7,391},{8,0},... | collective-permute-start | bytes 3244040 | tf_op jit(solution)/shard_map/ppermute | solution.py:35
  71.4 9.0 %collective-permute-start.9 = (bf16[256,512]{1,0:T(8,128)(2,1)S(1)}, bf16[256,512]{1,0:T(8,128)(2,1)S(1)}, u32[]{:S(2)}, u32[]{:S(2)}) collective-permute-start(bf16[256,512]{1,0:T(8,128)(2,1)S(1)} %get-tuple-element.56), channel_id=1, source_target_pairs={{0,2},{1,97},{2,4},{3,99},{4,6},{5,101},{6,0},{7,103},{8,10},{9,10... | collective-permute-start | bytes 786440 | tf_op jit(solution)/shard_map/ppermute | solution.py:35
  74.4 9.0 %collective-permute-start.10 = (bf16[256,512]{1,0:T(8,128)(2,1)S(1)}, bf16[256,512]{1,0:T(8,128)(2,1)S(1)}, u32[]{:S(2)}, u32[]{:S(2)}) collective-permute-start(bf16[256,512]{1,0:T(8,128)(2,1)S(1)} %get-tuple-element.55), channel_id=1, source_target_pairs={{0,6},{1,97},{2,0},{3,99},{4,2},{5,101},{6,4},{7,103},{8,14},{9,10... | collective-permute-start | bytes 786440 | tf_op jit(solution)/shard_map/ppermute | solution.py:35
  84.1 35.0 %copy-start.6 = (bf16[512,256]{1,0:T(8,128)(2,1)S(1)}, bf16[512,256]{1,0:T(8,128)(2,1)}, u32[]{:S(2)}) copy-start(bf16[512,256]{1,0:T(8,128)(2,1)} %get-tuple-element.36.out_ref) | copy-start | bytes 786436
  91.4 0.8 copy-start.14
  96.1 0.6 copy-start.21
  96.7 21.4 %collective-permute-start.14 = (bf16[6400,256]{1,0:T(8,128)(2,1)}, bf16[6400,256]{1,0:T(8,128)(2,1)}, u32[]{:S(2)}, u32[]{:S(2)}) collective-permute-start(bf16[6400,256]{1,0:T(8,128)(2,1)} %get-tuple-element.34), channel_id=1, source_target_pairs={{0,1},{1,0},{2,3},{3,2},{4,5},{5,4},{6,7},{7,6},{8,9},{9,8},{10,11... | collective-permute-start | bytes 9830408 | tf_op jit(solution)/shard_map/ppermute | solution.py:71
  107.6 28.5 %collective-permute-start.11 = (bf16[512,512]{1,0:T(8,128)(2,1)}, bf16[512,512]{1,0:T(8,128)(2,1)S(1)}, u32[]{:S(2)}, u32[]{:S(2)}) collective-permute-start(bf16[512,512]{1,0:T(8,128)(2,1)} %constant_dynamic-update-slice_fusion.refs_0_.refs_6_), channel_id=1, source_target_pairs={{0,8},{1,129},{2,10},{3,131},{4,12},{5,133},{6,14},{7,135},{8,16},... | collective-permute-start | bytes 1572872 | tf_op jit(solution)/shard_map/ppermute | solution.py:35
  110.7 25.4 %collective-permute-start.12 = (bf16[512,512]{1,0:T(8,128)(2,1)}, bf16[512,512]{1,0:T(8,128)(2,1)S(1)}, u32[]{:S(2)}, u32[]{:S(2)}) collective-permute-start(bf16[512,512]{1,0:T(8,128)(2,1)} %constant_dynamic-update-slice_fusion.refs_0_.refs_6_), channel_id=1, source_target_pairs={{0,16},{1,257},{2,18},{3,259},{4,20},{5,261},{6,22},{7,263},{8,24}... | collective-permute-start | bytes 1572872 | tf_op jit(solution)/shard_map/ppermute | solution.py:35
  115.1 21.1 %collective-permute-start.13 = (bf16[512,512]{1,0:T(8,128)(2,1)}, bf16[512,512]{1,0:T(8,128)(2,1)S(1)}, u32[]{:S(2)}, u32[]{:S(2)}) collective-permute-start(bf16[512,512]{1,0:T(8,128)(2,1)} %constant_dynamic-update-slice_fusion.refs_0_.refs_6_), channel_id=1, source_target_pairs={{0,24},{1,385},{2,26},{3,387},{4,28},{5,389},{6,30},{7,391},{8,0},... | collective-permute-start | bytes 1572872 | tf_op jit(solution)/shard_map/ppermute | solution.py:35
  119.4 20.2 %copy-start.24 = (s32[16]{0:T(128)S(1)}, s32[16]{0:T(128)}, u32[]{:S(2)}) copy-start(s32[16]{0:T(128)} %constant.106.clone) | copy-start | bytes 196
  119.4 20.2 %copy-start.25 = (s32[16]{0:T(128)S(1)}, s32[16]{0:T(128)}, u32[]{:S(2)}) copy-start(s32[16]{0:T(128)} %constant.107.clone) | copy-start | bytes 196
  119.4 20.2 %copy-start.26 = (pred[16]{0:T(512)(128)(4,1)S(1)}, pred[16]{0:T(512)(128)(4,1)}, u32[]{:S(2)}) copy-start(pred[16]{0:T(512)(128)(4,1)} %constant.119) | copy-start | bytes 52
  119.4 20.2 %copy-start.27 = (s32[16]{0:T(128)S(1)}, s32[16]{0:T(128)}, u32[]{:S(2)}) copy-start(s32[16]{0:T(128)} %constant.120) | copy-start | bytes 196
  119.5 20.2 %copy-start.28 = (s32[16]{0:T(128)S(1)}, s32[16]{0:T(128)}, u32[]{:S(2)}) copy-start(s32[16]{0:T(128)} %constant.121) | copy-start | bytes 196
  120.7 15.4 %collective-permute-start.15 = (f32[128,256]{1,0:T(8,128)S(1)}, f32[128,256]{1,0:T(8,128)S(1)}, u32[]{:S(2)}, u32[]{:S(2)}) collective-permute-start(f32[128,256]{1,0:T(8,128)S(1)} %pad_maximum_fusion), channel_id=1, source_target_pairs={{0,32},{32,0},{64,96},{96,64},{128,160},{160,128},{192,224},{224,1... | collective-permute-start | bytes 393224 | tf_op jit(solution)/shard_map/ppermute | solution.py:71
  136.2 6.1 %copy-start.10 = (bf16[512,512]{1,0:T(8,128)(2,1)}, bf16[512,512]{1,0:T(8,128)(2,1)S(1)}, u32[]{:S(2)}) copy-start(bf16[512,512]{1,0:T(8,128)(2,1)S(1)} %collective-permute-done.11.refs_1_.refs_7_) | copy-start | bytes 1572868
  136.2 6.1 %copy-start.11 = (bf16[512,512]{1,0:T(8,128)(2,1)}, bf16[512,512]{1,0:T(8,128)(2,1)S(1)}, u32[]{:S(2)}) copy-start(bf16[512,512]{1,0:T(8,128)(2,1)S(1)} %collective-permute-done.12.refs_2_.refs_8_) | copy-start | bytes 1572868
  136.2 6.1 %copy-start.12 = (bf16[512,512]{1,0:T(8,128)(2,1)}, bf16[512,512]{1,0:T(8,128)(2,1)S(1)}, u32[]{:S(2)}) copy-start(bf16[512,512]{1,0:T(8,128)(2,1)S(1)} %collective-permute-done.13.refs_3_.refs_9_) | copy-start | bytes 1572868
  137.4 4.9 %collective-permute-start.16 = (bf16[2048,256]{1,0:T(8,128)(2,1)S(1)}, bf16[2048,256]{1,0:T(8,128)(2,1)}, u32[]{:S(2)}, u32[]{:S(2)}) collective-permute-start(bf16[2048,256]{1,0:T(8,128)(2,1)S(1)} %give.1), channel_id=1, source_target_pairs={{0,1},{1,0},{2,3},{3,2},{4,5},{5,4},{6,7},{7,6},{8,9},{9,8},{10,11... | collective-permute-start | bytes 3145736 | tf_op jit(solution)/shard_map/ppermute | solution.py:71
  140.2 16.8 %copy-start.4 = (f32[2,512,256]{2,1,0:T(8,128)S(1)}, f32[2,512,256]{2,1,0:T(8,128)}, u32[]{:S(2)}) copy-start(f32[2,512,256]{2,1,0:T(8,128)} %get-tuple-element.42.band_ref) | copy-start | bytes 3145732
  140.2 16.8 %copy-start.5 = (bf16[1,512,256]{2,1,0:T(8,128)(2,1)S(1)}, bf16[1,512,256]{2,1,0:T(8,128)(2,1)}, u32[]{:S(2)}) copy-start(bf16[1,512,256]{2,1,0:T(8,128)(2,1)} %param.12) | copy-start | bytes 786436
  140.2 16.8 %copy-start.17 = (bf16[256,64]{0,1:T(8,128)(2,1)S(1)}, bf16[256,64]{0,1:T(8,128)(2,1)}, u32[]{:S(2)}) copy-start(bf16[256,64]{0,1:T(8,128)(2,1)} %param.20) | copy-start | bytes 98308
  140.2 16.8 %copy-start.19 = (bf16[512,128]{1,0:T(8,128)(2,1)S(1)}, bf16[512,128]{1,0:T(8,128)(2,1)}, u32[]{:S(2)}) copy-start(bf16[512,128]{1,0:T(8,128)(2,1)} %get-tuple-element.43.k_ref) | copy-start | bytes 393220
  140.2 16.8 %copy-start.20 = (bf16[512,128]{1,0:T(8,128)(2,1)S(1)}, bf16[512,128]{1,0:T(8,128)(2,1)}, u32[]{:S(2)}) copy-start(bf16[512,128]{1,0:T(8,128)(2,1)} %get-tuple-element.44.v_ref) | copy-start | bytes 393220
  140.2 9.4 %collective-permute-start.17 = (f32[128,256]{1,0:T(8,128)S(1)}, f32[128,256]{1,0:T(8,128)S(1)}, u32[]{:S(2)}, u32[]{:S(2)}) collective-permute-start(f32[128,256]{1,0:T(8,128)S(1)} %fusion.14), channel_id=1, source_target_pairs={{0,64},{32,96},{64,0},{96,32},{128,192},{160,224},{192,128},{224,1... | collective-permute-start | bytes 393224 | tf_op jit(solution)/shard_map/ppermute | solution.py:71
  149.7 7.3 %collective-permute-start.18 = (f32[512,256]{1,0:T(8,128)}, f32[512,256]{1,0:T(8,128)S(1)}, u32[]{:S(2)}, u32[]{:S(2)}) collective-permute-start(f32[512,256]{1,0:T(8,128)} %get-tuple-element.41), channel_id=1, source_target_pairs={{0,1},{1,0},{2,3},{3,2},{4,5},{5,4},{6,7},{7,6},{8,9},{9,8},{10,11... | collective-permute-start | bytes 1572872 | tf_op jit(solution)/shard_map/ppermute | solution.py:71
  153.8 7.0 %collective-permute-start.19 = (f32[128,256]{1,0:T(8,128)S(1)}, f32[128,256]{1,0:T(8,128)S(1)}, u32[]{:S(2)}, u32[]{:S(2)}) collective-permute-start(f32[128,256]{1,0:T(8,128)S(1)} %add.80), channel_id=1, source_target_pairs={{0,128},{32,160},{64,192},{96,224},{128,0},{160,32},{192,64},{224,... | collective-permute-start | bytes 393224 | tf_op jit(solution)/shard_map/ppermute | solution.py:71
  157.0 1.0 copy-start.9
  160.8 6.7 %collective-permute-start.20 = (f32[128,512]{1,0:T(8,128)S(1)}, f32[128,512]{1,0:T(8,128)S(1)}, u32[]{:S(2)}, u32[]{:S(2)}) collective-permute-start(f32[128,512]{1,0:T(8,128)S(1)} %get-tuple-element.49), channel_id=1, source_target_pairs={{0,1},{1,0},{2,3},{3,2},{4,5},{5,4},{6,7},{7,6},{8,9},{9,8},{10,11... | collective-permute-start | bytes 786440 | tf_op jit(solution)/shard_map/ppermute | solution.py:71
  163.5 10.5 %collective-permute-start.22 = (f32[128,256]{1,0:T(8,128)S(1)}, f32[128,256]{1,0:T(8,128)S(1)}, u32[]{:S(2)}, u32[]{:S(2)}) collective-permute-start(f32[128,256]{1,0:T(8,128)S(1)} %add.81), channel_id=1, source_target_pairs={{0,256},{32,288},{64,320},{96,352},{128,384},{160,416},{192,448},{... | collective-permute-start | bytes 393224 | tf_op jit(solution)/shard_map/ppermute | solution.py:71
  167.5 14.1 %collective-permute-start.21 = (bf16[64,512]{1,0:T(8,128)(2,1)S(1)}, bf16[64,512]{1,0:T(8,128)(2,1)S(1)}, u32[]{:S(2)}, u32[]{:S(2)}) collective-permute-start(bf16[64,512]{1,0:T(8,128)(2,1)S(1)} %get-tuple-element.51), channel_id=1, source_target_pairs={{0,2},{2,0},{4,6},{6,4},{8,10},{10,8},{12,14},{14,12},{16,18},{18,... | collective-permute-start | bytes 196616 | tf_op jit(solution)/shard_map/ppermute | solution.py:71

commit v6 on v5

--- a/solution.py
+++ b/solution.py
@@ -55,6 +55,10 @@
 def far_move(array, k):
     step = lambda i: (i + k * SIDE) % (SIDE * SIDE)
     return moved(array, step, step)
+
+
+def in_step_order(arrays):
+    return [arrays[1], arrays[0], arrays[2]]
 
 
 def near_move(array, shift, mask):
@@ -346,14 +350,17 @@
 
 
 def forward_kernel(
-    scale, place_ref, q_ref, label_ref, lower_ref, keys_ref, values_ref, rows_ref, taps_ref,
+    scale, q_ref, label_ref, lower_ref, keys_ref, values_ref, rows_ref, taps_ref,
     upper_ref, slab_ref, band_ref, out_ref, inner_ref, k_ref, v_ref, give_ref, sems,
 ):
     head = k_ref.shape[1]
     n, n_taps, (rank, width) = rows_ref.shape[0], taps_ref.shape[0], upper_ref.shape
     at_upper = n + n_taps
     at_inner = at_upper + rank // 2
-    mine = pl.ds(pl.multiple_of(place_ref[2] * head, head), head)
+    core = lax.axis_index("draft")
+    heads = q_ref.shape[1] // head
+    kv_head = (lax.axis_index("tensor") * 2 + core) * heads // (QUERY_HEAD_COUNT // KVH)
+    mine = pl.ds(pl.multiple_of(kv_head * head, head), head)
 
     def copy(i, source, target):
         return pltpu.make_async_copy(source, target, sems.at[i])
@@ -366,11 +373,11 @@
     for one in seen + given:
         one.start()
 
-    @pl.when(place_ref[0] == 0)
+    @pl.when(core == 0)
     def _():
         copy(5, slab_ref, give_ref.at[pl.ds(0, n)]).start()
 
-    @pl.when(place_ref[0] == 1)
+    @pl.when(core == 1)
     def _():
         copy(5, rows_ref, give_ref.at[pl.ds(0, n)]).start()
 
@@ -420,7 +427,7 @@
     copy(5, rows_ref, give_ref.at[pl.ds(0, n)]).wait()
 
 
-def forward(place, queries, labels, lower, keys, values, rows, taps, upper, slab):
+def forward(queries, labels, lower, keys, values, rows, taps, upper, slab):
     n, width = queries.shape
     heads, rank = width // HEAD_WIDTH, lower.shape[0]
     any_spec = pl.BlockSpec(memory_space=pl.ANY)
@@ -436,11 +443,11 @@
             jax.ShapeDtypeStruct((n, HEAD_WIDTH), BF16),
             jax.ShapeDtypeStruct((n_give, rows.shape[1]), BF16),
         ),
-        in_specs=[pl.BlockSpec(memory_space=pltpu.SMEM)] + [vmem] * 3 + [any_spec] * 6,
+        in_specs=[vmem] * 3 + [any_spec] * 6,
         out_specs=(vmem,) * 6,
         scratch_shapes=[pltpu.SemaphoreType.DMA((6,))],
         name="attention",
-    )(place, queries, labels, lower, keys, values, rows, taps, upper, slab)
+    )(queries, labels, lower, keys, values, rows, taps, upper, slab)
 
 
 def backward_kernel(
@@ -586,7 +593,6 @@
     rows, taps = output_gradient[0], draft_loss_gradients[0]
     queries, lower = rotated_queries[0], lower_factor_weight.T
     band, output_flattened, inner_piece, key_head, value_head, give = forward(
-        place,
         queries,
         segment_labels,
         lower,
@@ -618,7 +624,7 @@
     high = near_move(jnp.where(upper_core, block[half:], z2[half:]), 3, 3)
     last = jnp.concatenate([low, high], axis=0)
     near = jnp.concatenate([z1, z2, widened(quarter, SIDE)], axis=0)
-    near_far = [far_move(near, k) for k in (1, 2, 3)]
+    near_far = in_step_order([far_move(near, k) for k in (2, 1, 3)])
     give, sums = give_near(
         place,
         after(quarter, last),
@@ -629,7 +635,7 @@
     came_near = swapped(give, "draft", 1)
     residual = lax.dynamic_slice_in_dim(came_near, y * seq_len, seq_len, 0)
     residual = jnp.where(upper_core, residual, block[:, :width])
-    last_far = [far_move(last, k) for k in (1, 2, 3)]
+    last_far = in_step_order([far_move(last, k) for k in (2, 1, 3)])
     sums = jnp.where(upper_core, narrowed(came_near[12 * seq_len :], 2), sums)
     adapter_inner, adapter_gradient = sums[:, :rank], sums[:, rank:]
 

time: 183 us -> 183 us (level)
    unnamed x59 -> x57, local copies, waits for them, and re-layouts: 5.59 us -> 5.57 us
where the time goes in v6:
time: 183 us; the launch traced here: 182 us
  starting transfers between devices  93.1 us (51%)
  waiting for transfers between devices  54.1 us (30%)
  Pallas kernels  19.9 us (11%)
  local copies, waits for them, and re-layouts  8.47 us (5%)
  other arithmetic  3.05 us (2%)
    ppermute x10, starting transfers between devices, swapped(): lax.ppermute(array, axis, [(i, i ^ mask) for i in range(lax.axis_size(axi...  50.2 us
    ppermute x10, starting transfers between devices, moved(): return lax.ppermute(array, AXES, pairs)  36.9 us
    ppermute x10, waiting for transfers between devices, moved(): return lax.ppermute(array, AXES, pairs)  33.3 us
    ppermute x10, waiting for transfers between devices, swapped(): lax.ppermute(array, axis, [(i, i ^ mask) for i in range(lax.axis_size(axi...  12.9 us
    all_to_all x1, waiting for transfers between devices, spread(): lax.all_to_all(stacked, axes, 0, 0, axis_index_groups=groups, tiled=True)  7.91 us
    pallas_call x1, Pallas kernels, frozen_product(): pl.pallas_call(functools.partial(frozen_kernel, len(own), parts), out_sha...  7.28 us
    unnamed x57, local copies, waits for them, and re-layouts  5.57 us
    pallas_call x1, Pallas kernels, forward(): pl.pallas_call(functools.partial(forward_kernel, HEAD_WIDTH ** (-0.5)), o...  4.39 us
  transfers between devices with their start and end apart: 24, of which 10 were waited for; matrix products, arithmetic and copies ran while one was open for 3% of the time, Pallas kernels for 5%

profile of v6, /device:TPU:9, one launch (start us, length us, event | category | flops | bytes accessed | tf_op | source)
XLA Modules:
  0.0 181.6 jit_solution(18220237689453017130)
XLA Ops:
  0.7 4.4 %attention.1 = (f32[2,512,256]{2,1,0:T(8,128)}, bf16[512,256]{1,0:T(8,128)(2,1)}, f32[512,64]{1,0:T(8,128)}, bf16[512,128]{1,0:T(8,128)(2,1)}, bf16[512,128]{1,0:T(8,128)(2,1)}, /*index=5*/bf16[416,512]{1,0:T(8,128)(2,1)}) custom-call(bf16[512,256]{1,0:T(8,128)(2,1)} %bitcast.28, s32[1,512]{1,0:T(1,128)} %label_ref.1, bf16[64,256]{1,0:T(8,128)(2,1)} %bitcast.34, ...), custom_call_target="tpu_custom_call" | custom-call | tf_op jit(solution)/shard_map/attention/pallas_call | solution.py:436
  5.1 2.6 %collective-permute-start = (bf16[416,512]{1,0:T(8,128)(2,1)}, bf16[416,512]{1,0:T(8,128)(2,1)S(1)}, u32[]{:S(2)}, u32[]{:S(2)}) collective-permute-start(bf16[416,512]{1,0:T(8,128)(2,1)} %get-tuple-element.29), channel_id=1, source_target_pairs={{0,1},{1,0},{2,3},{3,2},{4,5},{5,4},{6,7},{7,6},{8,9},{9,8},{10,11... | collective-permute-start | bytes 1277960 | tf_op jit(solution)/shard_map/ppermute | solution.py:75
  7.7 0.1 pad_add_fusion.place_ref
  7.8 1.5 collective-permute-done.came_ref
  9.3 0.9 copy-done.16
  10.2 1.5 blend.1
  11.7 1.4 copy-done.3
  13.1 4.0 %all-to-all-start = ((bf16[4,544,512]{2,1,0:T(8,128)(2,1)}), bf16[4,544,512]{2,1,0:T(8,128)(2,1)S(1)}, u32[]{:S(2)}, u32[]{:S(2)}) async-start(bf16[4,544,512]{2,1,0:T(8,128)(2,1)} %bitcast.27), calls=%async_computation | async-start | bytes 4456448 | tf_op jit(solution)/shard_map/all_to_all | solution.py:39
  17.1 3.5 %collective-permute-start.1 = (bf16[512,512]{1,0:T(8,128)(2,1)}, bf16[512,512]{1,0:T(8,128)(2,1)S(1)}, u32[]{:S(2)}, u32[]{:S(2)}) collective-permute-start(bf16[512,512]{1,0:T(8,128)(2,1)} %get-tuple-element.32), channel_id=1, source_target_pairs={{0,2},{1,33},{2,4},{3,35},{4,6},{5,37},{6,0},{7,39},{8,10},{9,41},... | collective-permute-start | bytes 1572872 | tf_op jit(solution)/shard_map/ppermute | solution.py:35
  20.7 4.9 %collective-permute-start.2 = (bf16[512,512]{1,0:T(8,128)(2,1)}, bf16[512,512]{1,0:T(8,128)(2,1)S(1)}, u32[]{:S(2)}, u32[]{:S(2)}) collective-permute-start(bf16[512,512]{1,0:T(8,128)(2,1)} %get-tuple-element.32), channel_id=1, source_target_pairs={{0,6},{1,65},{2,0},{3,67},{4,2},{5,69},{6,4},{7,71},{8,14},{9,73},... | collective-permute-start | bytes 1572872 | tf_op jit(solution)/shard_map/ppermute | solution.py:35
  25.6 7.9 %all-to-all-done = bf16[4,544,512]{2,1,0:T(8,128)(2,1)S(1)} async-done(((bf16[4,544,512]{2,1,0:T(8,128)(2,1)}), bf16[4,544,512]{2,1,0:T(8,128)(2,1)S(1)}, u32[]{:S(2)}, u32[]{:S(2)}) %all-to-all-start) | async-done | bytes 2228256 | tf_op jit(solution)/shard_map/all_to_all | solution.py:39
  33.5 0.2 ride_sum.1
  33.7 0.7 collective-permute-start.3
  34.4 0.7 collective-permute-start.4
  35.0 0.7 collective-permute-start.5
  35.8 0.0 copy-start.13
  35.8 21.8 %collective-permute-done.2.refs_2_ = bf16[512,512]{1,0:T(8,128)(2,1)S(1)} collective-permute-done((bf16[512,512]{1,0:T(8,128)(2,1)}, bf16[512,512]{1,0:T(8,128)(2,1)S(1)}, u32[]{:S(2)}, u32[]{:S(2)}) %collective-permute-start.2) | collective-permute-done | bytes 524320 | tf_op jit(solution)/shard_map/ppermute | solution.py:35
  57.7 1.2 maximum_maximum_fusion
  58.8 3.5 %collective-permute-start.6 = (bf16[1056,512]{1,0:T(8,128)(2,1)}, bf16[1056,512]{1,0:T(8,128)(2,1)}, u32[]{:S(2)}, u32[]{:S(2)}) collective-permute-start(bf16[1056,512]{1,0:T(8,128)(2,1)} %maximum_maximum_fusion), channel_id=1, source_target_pairs={{0,8},{1,129},{2,10},{3,131},{4,12},{5,133},{6,14},{7,135},{8,16},... | collective-permute-start | bytes 3244040 | tf_op jit(solution)/shard_map/ppermute | solution.py:35
  62.3 4.3 %collective-permute-start.7 = (bf16[1056,512]{1,0:T(8,128)(2,1)}, bf16[1056,512]{1,0:T(8,128)(2,1)}, u32[]{:S(2)}, u32[]{:S(2)}) collective-permute-start(bf16[1056,512]{1,0:T(8,128)(2,1)} %maximum_maximum_fusion), channel_id=1, source_target_pairs={{0,16},{1,257},{2,18},{3,259},{4,20},{5,261},{6,22},{7,263},{8,24}... | collective-permute-start | bytes 3244040 | tf_op jit(solution)/shard_map/ppermute | solution.py:35
  66.6 3.1 %collective-permute-start.8 = (bf16[1056,512]{1,0:T(8,128)(2,1)}, bf16[1056,512]{1,0:T(8,128)(2,1)}, u32[]{:S(2)}, u32[]{:S(2)}) collective-permute-start(bf16[1056,512]{1,0:T(8,128)(2,1)} %maximum_maximum_fusion), channel_id=1, source_target_pairs={{0,24},{1,385},{2,26},{3,387},{4,28},{5,389},{6,30},{7,391},{8,0},... | collective-permute-start | bytes 3244040 | tf_op jit(solution)/shard_map/ppermute | solution.py:35
  69.7 1.1 slice_select_fusion
  70.8 2.9 %collective-permute-start.9 = (bf16[256,512]{1,0:T(8,128)(2,1)S(1)}, bf16[256,512]{1,0:T(8,128)(2,1)S(1)}, u32[]{:S(2)}, u32[]{:S(2)}) collective-permute-start(bf16[256,512]{1,0:T(8,128)(2,1)S(1)} %get-tuple-element.56), channel_id=1, source_target_pairs={{0,2},{1,97},{2,4},{3,99},{4,6},{5,101},{6,0},{7,103},{8,10},{9,10... | collective-permute-start | bytes 786440 | tf_op jit(solution)/shard_map/ppermute | solution.py:35
  73.8 4.1 %collective-permute-start.10 = (bf16[256,512]{1,0:T(8,128)(2,1)S(1)}, bf16[256,512]{1,0:T(8,128)(2,1)S(1)}, u32[]{:S(2)}, u32[]{:S(2)}) collective-permute-start(bf16[256,512]{1,0:T(8,128)(2,1)S(1)} %get-tuple-element.55), channel_id=1, source_target_pairs={{0,6},{1,97},{2,0},{3,99},{4,2},{5,101},{6,4},{7,103},{8,14},{9,10... | collective-permute-start | bytes 786440 | tf_op jit(solution)/shard_map/ppermute | solution.py:35
  77.9 1.9 %collective-permute-done.9 = bf16[256,512]{1,0:T(8,128)(2,1)S(1)} collective-permute-done((bf16[256,512]{1,0:T(8,128)(2,1)S(1)}, bf16[256,512]{1,0:T(8,128)(2,1)S(1)}, u32[]{:S(2)}, u32[]{:S(2)}) %collective-permute-start.9) | collective-permute-done | bytes 262176 | tf_op jit(solution)/shard_map/ppermute | solution.py:35
  79.8 0.7 constant_dynamic-update-slice_fusion.1
  80.6 2.2 %collective-permute-done.10 = bf16[256,512]{1,0:T(8,128)(2,1)S(1)} collective-permute-done((bf16[256,512]{1,0:T(8,128)(2,1)S(1)}, bf16[256,512]{1,0:T(8,128)(2,1)S(1)}, u32[]{:S(2)}, u32[]{:S(2)}) %collective-permute-start.10) | collective-permute-done | bytes 262176 | tf_op jit(solution)/shard_map/ppermute | solution.py:35
  82.7 0.7 constant_dynamic-update-slice_fusion.refs_0_.refs_6_
  83.5 5.9 %collective-permute-done.7.refs_4_ = bf16[1056,512]{1,0:T(8,128)(2,1)} collective-permute-done((bf16[1056,512]{1,0:T(8,128)(2,1)}, bf16[1056,512]{1,0:T(8,128)(2,1)}, u32[]{:S(2)}, u32[]{:S(2)}) %collective-permute-start.7) | collective-permute-done | bytes 1081376 | tf_op jit(solution)/shard_map/ppermute | solution.py:35
  89.3 1.5 collective-permute-done.8.refs_5_
  90.8 0.0 copy-start.14
  90.8 0.7 copy-done.14
  91.6 3.9 %give_near.1 = (bf16[6400,256]{1,0:T(8,128)(2,1)}, bf16[512,128]{1,0:T(8,128)(2,1)S(1)}) custom-call(s32[3]{0:T(128)S(1)} %pad_add_fusion.place_ref, bf16[128,128]{1,0:T(8,128)(2,1)S(1)} %copy-done.14, bf16[2176,512]{1,0:T(8,128)(2,1)S(1)} %bitcast.25, bf16[512,512]{1,0:T(8,128)(2,1)S(1)} %collective-permute-done.1.refs_1_, ...), custom_call_target="tpu_custom_call" | custom-call | tf_op jit(solution)/shard_map/give_near/pallas_call | solution.py:246
  95.5 0.6 copy-done.21
  96.1 10.9 %collective-permute-start.14 = (bf16[6400,256]{1,0:T(8,128)(2,1)}, bf16[6400,256]{1,0:T(8,128)(2,1)}, u32[]{:S(2)}, u32[]{:S(2)}) collective-permute-start(bf16[6400,256]{1,0:T(8,128)(2,1)} %get-tuple-element.34), channel_id=1, source_target_pairs={{0,1},{1,0},{2,3},{3,2},{4,5},{5,4},{6,7},{7,6},{8,9},{9,8},{10,11... | collective-permute-start | bytes 9830408 | tf_op jit(solution)/shard_map/ppermute | solution.py:75
  107.0 3.1 %collective-permute-start.11 = (bf16[512,512]{1,0:T(8,128)(2,1)}, bf16[512,512]{1,0:T(8,128)(2,1)S(1)}, u32[]{:S(2)}, u32[]{:S(2)}) collective-permute-start(bf16[512,512]{1,0:T(8,128)(2,1)} %constant_dynamic-update-slice_fusion.refs_0_.refs_6_), channel_id=1, source_target_pairs={{0,8},{1,129},{2,10},{3,131},{4,12},{5,133},{6,14},{7,135},{8,16},... | collective-permute-start | bytes 1572872 | tf_op jit(solution)/shard_map/ppermute | solution.py:35
  110.1 4.4 %collective-permute-start.12 = (bf16[512,512]{1,0:T(8,128)(2,1)}, bf16[512,512]{1,0:T(8,128)(2,1)S(1)}, u32[]{:S(2)}, u32[]{:S(2)}) collective-permute-start(bf16[512,512]{1,0:T(8,128)(2,1)} %constant_dynamic-update-slice_fusion.refs_0_.refs_6_), channel_id=1, source_target_pairs={{0,16},{1,257},{2,18},{3,259},{4,20},{5,261},{6,22},{7,263},{8,24}... | collective-permute-start | bytes 1572872 | tf_op jit(solution)/shard_map/ppermute | solution.py:35
  114.5 3.1 %collective-permute-start.13 = (bf16[512,512]{1,0:T(8,128)(2,1)}, bf16[512,512]{1,0:T(8,128)(2,1)S(1)}, u32[]{:S(2)}, u32[]{:S(2)}) collective-permute-start(bf16[512,512]{1,0:T(8,128)(2,1)} %constant_dynamic-update-slice_fusion.refs_0_.refs_6_), channel_id=1, source_target_pairs={{0,24},{1,385},{2,26},{3,387},{4,28},{5,389},{6,30},{7,391},{8,0},... | collective-permute-start | bytes 1572872 | tf_op jit(solution)/shard_map/ppermute | solution.py:35
  117.6 0.9 fusion.15
  118.5 0.3 fusion.6
  118.8 0.0 copy-start.23
  118.8 0.0 copy-start.24
  118.8 0.0 copy-start.25
  118.9 0.0 copy-start.26
  118.9 0.0 copy-start.27
  118.9 1.2 fusion
  120.2 12.1 %collective-permute-start.15 = (f32[128,256]{1,0:T(8,128)S(1)}, f32[128,256]{1,0:T(8,128)S(1)}, u32[]{:S(2)}, u32[]{:S(2)}) collective-permute-start(f32[128,256]{1,0:T(8,128)S(1)} %pad_maximum_fusion), channel_id=1, source_target_pairs={{0,32},{32,0},{64,96},{96,64},{128,160},{160,128},{192,224},{224,1... | collective-permute-start | bytes 393224 | tf_op jit(solution)/shard_map/ppermute | solution.py:75
  132.3 3.2 %collective-permute-done.15 = f32[128,256]{1,0:T(8,128)S(1)} collective-permute-done((f32[128,256]{1,0:T(8,128)S(1)}, f32[128,256]{1,0:T(8,128)S(1)}, u32[]{:S(2)}, u32[]{:S(2)}) %collective-permute-start.15) | collective-permute-done | bytes 131104 | tf_op jit(solution)/shard_map/ppermute | solution.py:75
  135.6 1.2 give.1
  136.8 2.1 %collective-permute-start.16 = (bf16[2048,256]{1,0:T(8,128)(2,1)S(1)}, bf16[2048,256]{1,0:T(8,128)(2,1)}, u32[]{:S(2)}, u32[]{:S(2)}) collective-permute-start(bf16[2048,256]{1,0:T(8,128)(2,1)S(1)} %give.1), channel_id=1, source_target_pairs={{0,1},{1,0},{2,3},{3,2},{4,5},{5,4},{6,7},{7,6},{8,9},{9,8},{10,11... | collective-permute-start | bytes 3145736 | tf_op jit(solution)/shard_map/ppermute | solution.py:75
  139.0 0.5 compare_select_fusion.10.place_ref
  139.6 2.1 %collective-permute-start.17 = (f32[128,256]{1,0:T(8,128)S(1)}, f32[128,256]{1,0:T(8,128)S(1)}, u32[]{:S(2)}, u32[]{:S(2)}) collective-permute-start(f32[128,256]{1,0:T(8,128)S(1)} %fusion.14), channel_id=1, source_target_pairs={{0,64},{32,96},{64,0},{96,32},{128,192},{160,224},{192,128},{224,1... | collective-permute-start | bytes 393224 | tf_op jit(solution)/shard_map/ppermute | solution.py:75
  141.7 7.3 %frozen.1 = (f32[512,256]{1,0:T(8,128)}, f32[512,256]{1,0:T(8,128)}) custom-call(s32[1]{0:T(128)} %bitcast.core_ref, s32[16]{0:T(128)} %compare_select_fusion.10.place_ref, bf16[2176,512]{1,0:T(8,128)(2,1)} %bitcast.26, bf16[512,512]{1,0:T(8,128)(2,1)} %copy-done.1, bf16[512,512]{1,0:T(8,128)(2,1)} %copy-done.2, ...), custom_call_target="tpu_custom_call" | custom-call | flops 4294967296 | bytes 25165824 | tf_op jit(solution)/shard_map/frozen/pallas_call | solution.py:316
  149.0 4.1 %collective-permute-start.18 = (f32[512,256]{1,0:T(8,128)}, f32[512,256]{1,0:T(8,128)S(1)}, u32[]{:S(2)}, u32[]{:S(2)}) collective-permute-start(f32[512,256]{1,0:T(8,128)} %get-tuple-element.41), channel_id=1, source_target_pairs={{0,1},{1,0},{2,3},{3,2},{4,5},{5,4},{6,7},{7,6},{8,9},{9,8},{10,11... | collective-permute-start | bytes 1572872 | tf_op jit(solution)/shard_map/ppermute | solution.py:75
  153.2 3.2 %collective-permute-start.19 = (f32[128,256]{1,0:T(8,128)S(1)}, f32[128,256]{1,0:T(8,128)S(1)}, u32[]{:S(2)}, u32[]{:S(2)}) collective-permute-start(f32[128,256]{1,0:T(8,128)S(1)} %add.80), channel_id=1, source_target_pairs={{0,128},{32,160},{64,192},{96,224},{128,0},{160,32},{192,64},{224,... | collective-permute-start | bytes 393224 | tf_op jit(solution)/shard_map/ppermute | solution.py:75
  156.4 1.0 copy-done.9
  157.5 1.4 attention_gradient.1
  158.8 1.4 collective-permute-done.19
  160.2 2.7 %collective-permute-start.20 = (f32[128,512]{1,0:T(8,128)S(1)}, f32[128,512]{1,0:T(8,128)S(1)}, u32[]{:S(2)}, u32[]{:S(2)}) collective-permute-start(f32[128,512]{1,0:T(8,128)S(1)} %get-tuple-element.49), channel_id=1, source_target_pairs={{0,1},{1,0},{2,3},{3,2},{4,5},{5,4},{6,7},{7,6},{8,9},{9,8},{10,11... | collective-permute-start | bytes 786440 | tf_op jit(solution)/shard_map/ppermute | solution.py:75
  162.9 3.9 %collective-permute-start.22 = (f32[128,256]{1,0:T(8,128)S(1)}, f32[128,256]{1,0:T(8,128)S(1)}, u32[]{:S(2)}, u32[]{:S(2)}) collective-permute-start(f32[128,256]{1,0:T(8,128)S(1)} %add.81), channel_id=1, source_target_pairs={{0,256},{32,288},{64,320},{96,352},{128,384},{160,416},{192,448},{... | collective-permute-start | bytes 393224 | tf_op jit(solution)/shard_map/ppermute | solution.py:75
  166.9 6.5 %collective-permute-start.21 = (bf16[64,512]{1,0:T(8,128)(2,1)S(1)}, bf16[64,512]{1,0:T(8,128)(2,1)S(1)}, u32[]{:S(2)}, u32[]{:S(2)}) collective-permute-start(bf16[64,512]{1,0:T(8,128)(2,1)S(1)} %get-tuple-element.51), channel_id=1, source_target_pairs={{0,2},{2,0},{4,6},{6,4},{8,10},{10,8},{12,14},{14,12},{16,18},{18,... | collective-permute-start | bytes 196616 | tf_op jit(solution)/shard_map/ppermute | solution.py:75
  173.5 0.7 fusion.16
  174.1 6.8 %collective-permute-done.21 = bf16[64,512]{1,0:T(8,128)(2,1)S(1)} collective-permute-done((bf16[64,512]{1,0:T(8,128)(2,1)S(1)}, bf16[64,512]{1,0:T(8,128)(2,1)S(1)}, u32[]{:S(2)}, u32[]{:S(2)}) %collective-permute-start.21) | collective-permute-done | bytes 65568 | tf_op jit(solution)/shard_map/ppermute | solution.py:75
  181.0 0.6 slice_bitcast_fusion.1
  (68 shorter events, 0.3 us)
Async XLA Ops:
  0.6 8.6 %copy-start.7 = (bf16[1,256,512]{2,1,0:T(8,128)(2,1)S(1)}, bf16[1,256,512]{2,1,0:T(8,128)(2,1)}, u32[]{:S(2)}) copy-start(bf16[1,256,512]{2,1,0:T(8,128)(2,1)} %param.16) | copy-start | bytes 786436
  0.6 8.6 %copy-start.15 = (bf16[1,64,512]{2,1,0:T(8,128)(2,1)S(1)}, bf16[1,64,512]{2,1,0:T(8,128)(2,1)}, u32[]{:S(2)}) copy-start(bf16[1,64,512]{2,1,0:T(8,128)(2,1)} %param.17) | copy-start | bytes 196612
  0.7 8.6 %copy-start.8 = (bf16[256,512]{1,0:T(8,128)(2,1)S(1)}, bf16[256,512]{1,0:T(8,128)(2,1)}, u32[]{:S(2)}) copy-start(bf16[256,512]{1,0:T(8,128)(2,1)} %slab_ref.3) | copy-start | bytes 786436
  0.7 8.6 %copy-start.18 = (bf16[64,256]{1,0:T(8,128)(2,1)S(1)}, bf16[64,256]{1,0:T(8,128)(2,1)}, u32[]{:S(2)}) copy-start(bf16[64,256]{1,0:T(8,128)(2,1)} %upper_ref.3) | copy-start | bytes 98308
  0.7 8.6 %copy-start.22 = (s32[1,128]{1,0:T(1,128)S(1)}, s32[1,128]{1,0:T(1,128)}, u32[]{:S(2)}) copy-start(s32[1,128]{1,0:T(1,128)} %tapped_ref.1) | copy-start | bytes 1540
  5.1 4.2 %collective-permute-start = (bf16[416,512]{1,0:T(8,128)(2,1)}, bf16[416,512]{1,0:T(8,128)(2,1)S(1)}, u32[]{:S(2)}, u32[]{:S(2)}) collective-permute-start(bf16[416,512]{1,0:T(8,128)(2,1)} %get-tuple-element.29), channel_id=1, source_target_pairs={{0,1},{1,0},{2,3},{3,2},{4,5},{5,4},{6,7},{7,6},{8,9},{9,8},{10,11... | collective-permute-start | bytes 1277960 | tf_op jit(solution)/shard_map/ppermute | solution.py:75
  9.3 1.0 copy-start.16
  11.7 1.4 copy-start.3
  13.1 20.4 %all-to-all-start = ((bf16[4,544,512]{2,1,0:T(8,128)(2,1)}), bf16[4,544,512]{2,1,0:T(8,128)(2,1)S(1)}, u32[]{:S(2)}, u32[]{:S(2)}) async-start(bf16[4,544,512]{2,1,0:T(8,128)(2,1)} %bitcast.27), calls=%async_computation | async-start | bytes 4456448 | tf_op jit(solution)/shard_map/all_to_all | solution.py:39
  17.1 18.7 %collective-permute-start.1 = (bf16[512,512]{1,0:T(8,128)(2,1)}, bf16[512,512]{1,0:T(8,128)(2,1)S(1)}, u32[]{:S(2)}, u32[]{:S(2)}) collective-permute-start(bf16[512,512]{1,0:T(8,128)(2,1)} %get-tuple-element.32), channel_id=1, source_target_pairs={{0,2},{1,33},{2,4},{3,35},{4,6},{5,37},{6,0},{7,39},{8,10},{9,41},... | collective-permute-start | bytes 1572872 | tf_op jit(solution)/shard_map/ppermute | solution.py:35
  20.7 37.0 %collective-permute-start.2 = (bf16[512,512]{1,0:T(8,128)(2,1)}, bf16[512,512]{1,0:T(8,128)(2,1)S(1)}, u32[]{:S(2)}, u32[]{:S(2)}) collective-permute-start(bf16[512,512]{1,0:T(8,128)(2,1)} %get-tuple-element.32), channel_id=1, source_target_pairs={{0,6},{1,65},{2,0},{3,67},{4,2},{5,69},{6,4},{7,71},{8,14},{9,73},... | collective-permute-start | bytes 1572872 | tf_op jit(solution)/shard_map/ppermute | solution.py:35
  33.5 57.3 %copy-start = (bf16[4,544,512]{2,1,0:T(8,128)(2,1)}, bf16[4,544,512]{2,1,0:T(8,128)(2,1)S(1)}, u32[]{:S(2)}) copy-start(bf16[4,544,512]{2,1,0:T(8,128)(2,1)S(1)} %all-to-all-done) | copy-start | bytes 6684676
  33.7 2.0 %collective-permute-start.3 = (bf16[128,128]{1,0:T(8,128)(2,1)S(1)}, bf16[128,128]{1,0:T(8,128)(2,1)S(1)}, u32[]{:S(2)}, u32[]{:S(2)}) collective-permute-start(bf16[128,128]{1,0:T(8,128)(2,1)S(1)} %ride_sum.1), channel_id=1, source_target_pairs={{0,4},{2,6},{4,0},{6,2},{8,12},{10,14},{12,8},{14,10},{16,20},{18,... | collective-permute-start | bytes 98312 | tf_op jit(solution)/shard_map/ppermute | solution.py:71
  34.4 1.4 collective-permute-start.4
  35.0 0.7 collective-permute-start.5
  35.8 21.9 %copy-start.13 = (bf16[128,128]{1,0:T(8,128)(2,1)}, bf16[128,128]{1,0:T(8,128)(2,1)S(1)}, u32[]{:S(2)}) copy-start(bf16[128,128]{1,0:T(8,128)(2,1)S(1)} %add_convert_fusion.1.quarter_ref) | copy-start | bytes 98308
  35.8 55.0 %copy-start.1 = (bf16[512,512]{1,0:T(8,128)(2,1)}, bf16[512,512]{1,0:T(8,128)(2,1)S(1)}, u32[]{:S(2)}) copy-start(bf16[512,512]{1,0:T(8,128)(2,1)S(1)} %collective-permute-done.1.refs_1_) | copy-start | bytes 1572868
  57.7 33.1 %copy-start.2 = (bf16[512,512]{1,0:T(8,128)(2,1)}, bf16[512,512]{1,0:T(8,128)(2,1)S(1)}, u32[]{:S(2)}) copy-start(bf16[512,512]{1,0:T(8,128)(2,1)S(1)} %collective-permute-done.2.refs_2_) | copy-start | bytes 1572868
  58.8 24.6 %collective-permute-start.6 = (bf16[1056,512]{1,0:T(8,128)(2,1)}, bf16[1056,512]{1,0:T(8,128)(2,1)}, u32[]{:S(2)}, u32[]{:S(2)}) collective-permute-start(bf16[1056,512]{1,0:T(8,128)(2,1)} %maximum_maximum_fusion), channel_id=1, source_target_pairs={{0,8},{1,129},{2,10},{3,131},{4,12},{5,133},{6,14},{7,135},{8,16},... | collective-permute-start | bytes 3244040 | tf_op jit(solution)/shard_map/ppermute | solution.py:35
  62.3 27.0 %collective-permute-start.7 = (bf16[1056,512]{1,0:T(8,128)(2,1)}, bf16[1056,512]{1,0:T(8,128)(2,1)}, u32[]{:S(2)}, u32[]{:S(2)}) collective-permute-start(bf16[1056,512]{1,0:T(8,128)(2,1)} %maximum_maximum_fusion), channel_id=1, source_target_pairs={{0,16},{1,257},{2,18},{3,259},{4,20},{5,261},{6,22},{7,263},{8,24}... | collective-permute-start | bytes 3244040 | tf_op jit(solution)/shard_map/ppermute | solution.py:35
  66.6 24.2 %collective-permute-start.8 = (bf16[1056,512]{1,0:T(8,128)(2,1)}, bf16[1056,512]{1,0:T(8,128)(2,1)}, u32[]{:S(2)}, u32[]{:S(2)}) collective-permute-start(bf16[1056,512]{1,0:T(8,128)(2,1)} %maximum_maximum_fusion), channel_id=1, source_target_pairs={{0,24},{1,385},{2,26},{3,387},{4,28},{5,389},{6,30},{7,391},{8,0},... | collective-permute-start | bytes 3244040 | tf_op jit(solution)/shard_map/ppermute | solution.py:35
  70.8 9.0 %collective-permute-start.9 = (bf16[256,512]{1,0:T(8,128)(2,1)S(1)}, bf16[256,512]{1,0:T(8,128)(2,1)S(1)}, u32[]{:S(2)}, u32[]{:S(2)}) collective-permute-start(bf16[256,512]{1,0:T(8,128)(2,1)S(1)} %get-tuple-element.56), channel_id=1, source_target_pairs={{0,2},{1,97},{2,4},{3,99},{4,6},{5,101},{6,0},{7,103},{8,10},{9,10... | collective-permute-start | bytes 786440 | tf_op jit(solution)/shard_map/ppermute | solution.py:35
  73.8 9.0 %collective-permute-start.10 = (bf16[256,512]{1,0:T(8,128)(2,1)S(1)}, bf16[256,512]{1,0:T(8,128)(2,1)S(1)}, u32[]{:S(2)}, u32[]{:S(2)}) collective-permute-start(bf16[256,512]{1,0:T(8,128)(2,1)S(1)} %get-tuple-element.55), channel_id=1, source_target_pairs={{0,6},{1,97},{2,0},{3,99},{4,2},{5,101},{6,4},{7,103},{8,14},{9,10... | collective-permute-start | bytes 786440 | tf_op jit(solution)/shard_map/ppermute | solution.py:35
  83.5 35.1 %copy-start.6 = (bf16[512,256]{1,0:T(8,128)(2,1)S(1)}, bf16[512,256]{1,0:T(8,128)(2,1)}, u32[]{:S(2)}) copy-start(bf16[512,256]{1,0:T(8,128)(2,1)} %get-tuple-element.36.out_ref) | copy-start | bytes 786436
  90.8 0.8 copy-start.14
  95.5 0.7 copy-start.21
  96.1 21.4 %collective-permute-start.14 = (bf16[6400,256]{1,0:T(8,128)(2,1)}, bf16[6400,256]{1,0:T(8,128)(2,1)}, u32[]{:S(2)}, u32[]{:S(2)}) collective-permute-start(bf16[6400,256]{1,0:T(8,128)(2,1)} %get-tuple-element.34), channel_id=1, source_target_pairs={{0,1},{1,0},{2,3},{3,2},{4,5},{5,4},{6,7},{7,6},{8,9},{9,8},{10,11... | collective-permute-start | bytes 9830408 | tf_op jit(solution)/shard_map/ppermute | solution.py:75
  107.0 28.5 %collective-permute-start.11 = (bf16[512,512]{1,0:T(8,128)(2,1)}, bf16[512,512]{1,0:T(8,128)(2,1)S(1)}, u32[]{:S(2)}, u32[]{:S(2)}) collective-permute-start(bf16[512,512]{1,0:T(8,128)(2,1)} %constant_dynamic-update-slice_fusion.refs_0_.refs_6_), channel_id=1, source_target_pairs={{0,8},{1,129},{2,10},{3,131},{4,12},{5,133},{6,14},{7,135},{8,16},... | collective-permute-start | bytes 1572872 | tf_op jit(solution)/shard_map/ppermute | solution.py:35
  110.1 25.4 %collective-permute-start.12 = (bf16[512,512]{1,0:T(8,128)(2,1)}, bf16[512,512]{1,0:T(8,128)(2,1)S(1)}, u32[]{:S(2)}, u32[]{:S(2)}) collective-permute-start(bf16[512,512]{1,0:T(8,128)(2,1)} %constant_dynamic-update-slice_fusion.refs_0_.refs_6_), channel_id=1, source_target_pairs={{0,16},{1,257},{2,18},{3,259},{4,20},{5,261},{6,22},{7,263},{8,24}... | collective-permute-start | bytes 1572872 | tf_op jit(solution)/shard_map/ppermute | solution.py:35
  114.5 21.1 %collective-permute-start.13 = (bf16[512,512]{1,0:T(8,128)(2,1)}, bf16[512,512]{1,0:T(8,128)(2,1)S(1)}, u32[]{:S(2)}, u32[]{:S(2)}) collective-permute-start(bf16[512,512]{1,0:T(8,128)(2,1)} %constant_dynamic-update-slice_fusion.refs_0_.refs_6_), channel_id=1, source_target_pairs={{0,24},{1,385},{2,26},{3,387},{4,28},{5,389},{6,30},{7,391},{8,0},... | collective-permute-start | bytes 1572872 | tf_op jit(solution)/shard_map/ppermute | solution.py:35
  118.8 20.2 %copy-start.23 = (s32[16]{0:T(128)S(1)}, s32[16]{0:T(128)}, u32[]{:S(2)}) copy-start(s32[16]{0:T(128)} %constant.106.clone) | copy-start | bytes 196
  118.8 20.2 %copy-start.24 = (s32[16]{0:T(128)S(1)}, s32[16]{0:T(128)}, u32[]{:S(2)}) copy-start(s32[16]{0:T(128)} %constant.107.clone) | copy-start | bytes 196
  118.8 20.2 %copy-start.25 = (pred[16]{0:T(512)(128)(4,1)S(1)}, pred[16]{0:T(512)(128)(4,1)}, u32[]{:S(2)}) copy-start(pred[16]{0:T(512)(128)(4,1)} %constant.119) | copy-start | bytes 52
  118.9 20.2 %copy-start.26 = (s32[16]{0:T(128)S(1)}, s32[16]{0:T(128)}, u32[]{:S(2)}) copy-start(s32[16]{0:T(128)} %constant.120) | copy-start | bytes 196
  118.9 20.2 %copy-start.27 = (s32[16]{0:T(128)S(1)}, s32[16]{0:T(128)}, u32[]{:S(2)}) copy-start(s32[16]{0:T(128)} %constant.121) | copy-start | bytes 196
  120.2 15.4 %collective-permute-start.15 = (f32[128,256]{1,0:T(8,128)S(1)}, f32[128,256]{1,0:T(8,128)S(1)}, u32[]{:S(2)}, u32[]{:S(2)}) collective-permute-start(f32[128,256]{1,0:T(8,128)S(1)} %pad_maximum_fusion), channel_id=1, source_target_pairs={{0,32},{32,0},{64,96},{96,64},{128,160},{160,128},{192,224},{224,1... | collective-permute-start | bytes 393224 | tf_op jit(solution)/shard_map/ppermute | solution.py:75
  135.5 6.1 %copy-start.10 = (bf16[512,512]{1,0:T(8,128)(2,1)}, bf16[512,512]{1,0:T(8,128)(2,1)S(1)}, u32[]{:S(2)}) copy-start(bf16[512,512]{1,0:T(8,128)(2,1)S(1)} %collective-permute-done.11.refs_1_.refs_7_) | copy-start | bytes 1572868
  135.6 6.1 %copy-start.11 = (bf16[512,512]{1,0:T(8,128)(2,1)}, bf16[512,512]{1,0:T(8,128)(2,1)S(1)}, u32[]{:S(2)}) copy-start(bf16[512,512]{1,0:T(8,128)(2,1)S(1)} %collective-permute-done.12.refs_2_.refs_8_) | copy-start | bytes 1572868
  135.6 6.1 %copy-start.12 = (bf16[512,512]{1,0:T(8,128)(2,1)}, bf16[512,512]{1,0:T(8,128)(2,1)S(1)}, u32[]{:S(2)}) copy-start(bf16[512,512]{1,0:T(8,128)(2,1)S(1)} %collective-permute-done.13.refs_3_.refs_9_) | copy-start | bytes 1572868
  136.8 4.9 %collective-permute-start.16 = (bf16[2048,256]{1,0:T(8,128)(2,1)S(1)}, bf16[2048,256]{1,0:T(8,128)(2,1)}, u32[]{:S(2)}, u32[]{:S(2)}) collective-permute-start(bf16[2048,256]{1,0:T(8,128)(2,1)S(1)} %give.1), channel_id=1, source_target_pairs={{0,1},{1,0},{2,3},{3,2},{4,5},{5,4},{6,7},{7,6},{8,9},{9,8},{10,11... | collective-permute-start | bytes 3145736 | tf_op jit(solution)/shard_map/ppermute | solution.py:75
  139.6 16.8 %copy-start.4 = (f32[2,512,256]{2,1,0:T(8,128)S(1)}, f32[2,512,256]{2,1,0:T(8,128)}, u32[]{:S(2)}) copy-start(f32[2,512,256]{2,1,0:T(8,128)} %get-tuple-element.42.band_ref) | copy-start | bytes 3145732
  139.6 16.8 %copy-start.5 = (bf16[1,512,256]{2,1,0:T(8,128)(2,1)S(1)}, bf16[1,512,256]{2,1,0:T(8,128)(2,1)}, u32[]{:S(2)}) copy-start(bf16[1,512,256]{2,1,0:T(8,128)(2,1)} %param.12) | copy-start | bytes 786436
  139.6 16.8 %copy-start.17 = (bf16[256,64]{0,1:T(8,128)(2,1)S(1)}, bf16[256,64]{0,1:T(8,128)(2,1)}, u32[]{:S(2)}) copy-start(bf16[256,64]{0,1:T(8,128)(2,1)} %param.20) | copy-start | bytes 98308
  139.6 16.8 %copy-start.19 = (bf16[512,128]{1,0:T(8,128)(2,1)S(1)}, bf16[512,128]{1,0:T(8,128)(2,1)}, u32[]{:S(2)}) copy-start(bf16[512,128]{1,0:T(8,128)(2,1)} %get-tuple-element.43.k_ref) | copy-start | bytes 393220
  139.6 16.8 %copy-start.20 = (bf16[512,128]{1,0:T(8,128)(2,1)S(1)}, bf16[512,128]{1,0:T(8,128)(2,1)}, u32[]{:S(2)}) copy-start(bf16[512,128]{1,0:T(8,128)(2,1)} %get-tuple-element.44.v_ref) | copy-start | bytes 393220
  139.6 9.4 %collective-permute-start.17 = (f32[128,256]{1,0:T(8,128)S(1)}, f32[128,256]{1,0:T(8,128)S(1)}, u32[]{:S(2)}, u32[]{:S(2)}) collective-permute-start(f32[128,256]{1,0:T(8,128)S(1)} %fusion.14), channel_id=1, source_target_pairs={{0,64},{32,96},{64,0},{96,32},{128,192},{160,224},{192,128},{224,1... | collective-permute-start | bytes 393224 | tf_op jit(solution)/shard_map/ppermute | solution.py:75
  149.0 7.3 %collective-permute-start.18 = (f32[512,256]{1,0:T(8,128)}, f32[512,256]{1,0:T(8,128)S(1)}, u32[]{:S(2)}, u32[]{:S(2)}) collective-permute-start(f32[512,256]{1,0:T(8,128)} %get-tuple-element.41), channel_id=1, source_target_pairs={{0,1},{1,0},{2,3},{3,2},{4,5},{5,4},{6,7},{7,6},{8,9},{9,8},{10,11... | collective-permute-start | bytes 1572872 | tf_op jit(solution)/shard_map/ppermute | solution.py:75
  153.2 7.0 %collective-permute-start.19 = (f32[128,256]{1,0:T(8,128)S(1)}, f32[128,256]{1,0:T(8,128)S(1)}, u32[]{:S(2)}, u32[]{:S(2)}) collective-permute-start(f32[128,256]{1,0:T(8,128)S(1)} %add.80), channel_id=1, source_target_pairs={{0,128},{32,160},{64,192},{96,224},{128,0},{160,32},{192,64},{224,... | collective-permute-start | bytes 393224 | tf_op jit(solution)/shard_map/ppermute | solution.py:75
  156.4 1.0 copy-start.9
  160.2 6.6 %collective-permute-start.20 = (f32[128,512]{1,0:T(8,128)S(1)}, f32[128,512]{1,0:T(8,128)S(1)}, u32[]{:S(2)}, u32[]{:S(2)}) collective-permute-start(f32[128,512]{1,0:T(8,128)S(1)} %get-tuple-element.49), channel_id=1, source_target_pairs={{0,1},{1,0},{2,3},{3,2},{4,5},{5,4},{6,7},{7,6},{8,9},{9,8},{10,11... | collective-permute-start | bytes 786440 | tf_op jit(solution)/shard_map/ppermute | solution.py:75
  162.9 10.5 %collective-permute-start.22 = (f32[128,256]{1,0:T(8,128)S(1)}, f32[128,256]{1,0:T(8,128)S(1)}, u32[]{:S(2)}, u32[]{:S(2)}) collective-permute-start(f32[128,256]{1,0:T(8,128)S(1)} %add.81), channel_id=1, source_target_pairs={{0,256},{32,288},{64,320},{96,352},{128,384},{160,416},{192,448},{... | collective-permute-start | bytes 393224 | tf_op jit(solution)/shard_map/ppermute | solution.py:75
  166.9 14.0 %collective-permute-start.21 = (bf16[64,512]{1,0:T(8,128)(2,1)S(1)}, bf16[64,512]{1,0:T(8,128)(2,1)S(1)}, u32[]{:S(2)}, u32[]{:S(2)}) collective-permute-start(bf16[64,512]{1,0:T(8,128)(2,1)S(1)} %get-tuple-element.51), channel_id=1, source_target_pairs={{0,2},{2,0},{4,6},{6,4},{8,10},{10,8},{12,14},{14,12},{16,18},{18,... | collective-permute-start | bytes 196616 | tf_op jit(solution)/shard_map/ppermute | solution.py:75
